TPU v7x, 1024 devices: a whole 4x8x16 slice. The times are simulated.
1024 devices in a mesh: dp: 16 (over y, x_lo), expert: 64 (over x_hi, z, core).
Axes of the slice: x: 4 (x_hi: 2, x_lo: 2; x = x_hi * 2 + x_lo), y: 8, z: 16, core: 2. Of those that a mesh axis runs over, the one named last changes fastest.
Arguments:
- tokens: bfloat16 [1024, 256, 1280], P(('dp', 'expert')), may hold values from -16 to 16
- cotangent: bfloat16 [1024, 256, 1280], P(('dp', 'expert')), may hold values from -6 to 6
- slot_params: bfloat16 [1280, 8], replicated, may hold values from -1 to 1
- in_weight: bfloat16 [1280, 40960], P(None, 'expert'), may hold values from -0.15625 to 0.15625
- out_weight: bfloat16 [1280, 40960], P(None, 'expert'), may hold values from -0.078125 to 0.078125
Outputs:
- mixed: bfloat16 [1024, 256, 1280], P(('dp', 'expert'))
- grad_tokens: bfloat16 [1024, 256, 1280], P(('dp', 'expert'))
- grad_in_weight: float32 [1280, 40960], P('dp', 'expert')
- grad_out_weight: float32 [1280, 40960], P('dp', 'expert')
All inputs are finite; a program needn't handle non-finite values.
Results may differ from a plain program's by a relative error of at most 0.022.
Values may be sent and summed in bfloat16 or wider, within the bound.
No kernel may reach another device: no remote copies, remote signals or barrier semaphores. Data moves between devices by JAX's collectives and lax.ppermute only.
A program may use at most 32 MiB of HBM per device.

v0:
```python
import jax
import jax.numpy as jnp
from jax import lax
from jax.sharding import PartitionSpec as P

root_half = 0.7071067811865476
density = 0.3989422804014327


def gelu_parts(preact):
    cumulative = 0.5 * (1.0 + lax.erf(preact * root_half))
    return (preact * cumulative, cumulative + preact * jnp.exp(-0.5 * preact * preact) * density)


def per_device(tokens, cotangent, slot_params, in_weight, out_weight):
    experts = slot_params.shape[1]
    peers = lax.axis_size("expert")
    shards = peers // experts
    width = tokens.shape[2]
    hidden_cols = in_weight.shape[1]
    logits = jnp.einsum("ipd,ds->ips", tokens, slot_params, preferred_element_type=jnp.float32)
    dispatch_soft = jax.nn.softmax(logits, axis=1)
    combine_soft = jax.nn.softmax(logits, axis=2)
    dispatch = dispatch_soft.astype(jnp.bfloat16)
    combine = combine_soft.astype(jnp.bfloat16)
    slot_in = jnp.einsum(
        "ips,ipd->sid", dispatch, tokens, preferred_element_type=jnp.float32
    ).astype(jnp.bfloat16)
    slot_grad = jnp.einsum(
        "ips,ipd->sid", combine, cotangent, preferred_element_type=jnp.float32
    ).astype(jnp.bfloat16)

    def spread(values):
        widened = jnp.broadcast_to(values[:, None], (experts, shards) + values.shape[1:])
        return widened.reshape((peers,) + values.shape[1:])

    received = lax.all_to_all(spread(slot_in), "expert", split_axis=0, concat_axis=0, tiled=True)
    preact = jnp.einsum("nkd,df->nkf", received, in_weight, preferred_element_type=jnp.float32)
    activation, slope = gelu_parts(preact)
    activated = activation.astype(jnp.bfloat16)
    out_part = jnp.einsum("nkf,df->nkd", activated, out_weight, preferred_element_type=jnp.float32)
    out_part, activated, slope = (out_part.astype(jnp.bfloat16), activated, slope)
    out_part, activated, slope, received = (out_part, activated, slope, received)
    returned = lax.all_to_all(out_part, "expert", split_axis=0, concat_axis=0, tiled=True)
    grads_in = lax.all_to_all(spread(slot_grad), "expert", split_axis=0, concat_axis=0, tiled=True)
    grad_hidden = jnp.einsum(
        "nkd,df->nkf", grads_in, out_weight, preferred_element_type=jnp.float32
    )
    grad_preact = (grad_hidden * slope).astype(jnp.bfloat16)
    grad_part = jnp.einsum(
        "nkf,df->nkd", grad_preact, in_weight, preferred_element_type=jnp.float32
    )
    grad_part, grad_preact = (grad_part.astype(jnp.bfloat16), grad_preact)
    returned_grad = lax.all_to_all(grad_part, "expert", split_axis=0, concat_axis=0, tiled=True)
    rows_in = received.reshape(-1, width)
    rows_grad = grads_in.reshape(-1, width)
    rows_act = activated.reshape(-1, hidden_cols)
    rows_pre = grad_preact.reshape(-1, hidden_cols)
    term_in = jnp.einsum("rd,rf->df", rows_in, rows_pre, preferred_element_type=jnp.float32)
    term_out = jnp.einsum("rd,rf->df", rows_grad, rows_act, preferred_element_type=jnp.float32)
    summed = lax.psum_scatter(
        jnp.concatenate([term_in, term_out], axis=1).astype(jnp.bfloat16),
        "dp",
        scatter_dimension=0,
        tiled=True,
    ).astype(jnp.float32)
    grad_in_weight = summed[:, :hidden_cols]
    grad_out_weight = summed[:, hidden_cols:]

    def add_shards(parts):
        grouped = parts.reshape((experts, shards) + parts.shape[1:]).astype(jnp.float32)
        return jnp.sum(grouped, axis=1).astype(jnp.bfloat16)

    slot_out = add_shards(returned)
    grad_slot_in = add_shards(returned_grad)
    mixed = jnp.einsum(
        "ips,sid->ipd", combine, slot_out, preferred_element_type=jnp.float32
    ).astype(jnp.bfloat16)
    combine_grad = jnp.einsum(
        "ipd,sid->ips", cotangent, slot_out, preferred_element_type=jnp.float32
    )
    dispatch_grad = jnp.einsum(
        "ipd,sid->ips", tokens, grad_slot_in, preferred_element_type=jnp.float32
    )
    logit_grad = combine_soft * (
        combine_grad - jnp.sum(combine_soft * combine_grad, axis=2, keepdims=True)
    )
    logit_grad = logit_grad + dispatch_soft * (
        dispatch_grad - jnp.sum(dispatch_soft * dispatch_grad, axis=1, keepdims=True)
    )
    logit_grad = logit_grad.astype(jnp.bfloat16)
    grad_tokens = jnp.einsum(
        "ips,sid->ipd", dispatch, grad_slot_in, preferred_element_type=jnp.float32
    )
    grad_tokens = grad_tokens + jnp.einsum(
        "ips,ds->ipd", logit_grad, slot_params, preferred_element_type=jnp.float32
    )
    return (mixed, grad_tokens.astype(jnp.bfloat16), grad_in_weight, grad_out_weight)


def solution(mesh):
    in_specs = (
        P(("dp", "expert"), None, None),
        P(("dp", "expert"), None, None),
        P(),
        P(None, "expert"),
        P(None, "expert"),
    )
    out_specs = (
        P(("dp", "expert"), None, None),
        P(("dp", "expert"), None, None),
        P("dp", "expert"),
        P("dp", "expert"),
    )
    return jax.shard_map(
        per_device, mesh=mesh, in_specs=in_specs, out_specs=out_specs, check_vma=False
    )
```

profile of v0, /device:TPU:1, one launch (start us, length us, event | category | flops | bytes accessed | tf_op | source)
XLA Modules:
  0.0 182.1 jit_solution(12147407216837963052)
XLA Ops:
  7.2 0.0 copy-start
  7.2 1.7 fusion.42
  8.9 0.2 fusion.26
  9.1 1.3 convolution_convert_fusion.6
  10.4 0.5 broadcast.30
  11.0 0.7 reduce.16
  11.7 0.7 reshape.162
  12.4 23.3 %all-to-all-start = ((bf16[64,2,640]{2,1,0:T(2,128)(2,1)}), bf16[64,2,640]{2,1,0:T(2,128)(2,1)S(1)}, u32[]{:S(2)}, u32[]{:S(2)}) async-start(bf16[64,2,640]{2,1,0:T(2,128)(2,1)} %reshape.162), calls=%async_computation | async-start | bytes 327680 | tf_op jit(solution)/shard_map/all_to_all | solution.py:37
  35.7 0.2 convolution_convert_fusion.5
  35.9 0.7 reduce.18
  36.6 0.7 reshape.160
  37.3 18.2 %all-to-all-done = bf16[64,2,640]{2,1,0:T(2,128)(2,1)S(1)} async-done(((bf16[64,2,640]{2,1,0:T(2,128)(2,1)}), bf16[64,2,640]{2,1,0:T(2,128)(2,1)S(1)}, u32[]{:S(2)}, u32[]{:S(2)}) %all-to-all-start) | async-done | bytes 163872 | tf_op jit(solution)/shard_map/all_to_all | solution.py:37
  55.5 5.1 %all-to-all-start.2 = ((bf16[64,2,640]{2,1,0:T(2,128)(2,1)}), bf16[64,2,640]{2,1,0:T(2,128)(2,1)}, u32[]{:S(2)}, u32[]{:S(2)}) async-start(bf16[64,2,640]{2,1,0:T(2,128)(2,1)} %reshape.160), calls=%async_computation.2 | async-start | bytes 327680 | tf_op jit(solution)/shard_map/all_to_all | solution.py:45
  60.6 0.0 reduce-scatter.4.cloned.1.call-start
  60.7 0.1 reshape.163
  60.8 0.7 copy-done.3
  61.5 0.4 fusion.19
  61.9 18.6 %all-to-all-done.2 = bf16[64,2,640]{2,1,0:T(2,128)(2,1)} async-done(((bf16[64,2,640]{2,1,0:T(2,128)(2,1)}), bf16[64,2,640]{2,1,0:T(2,128)(2,1)}, u32[]{:S(2)}, u32[]{:S(2)}) %all-to-all-start.2) | async-done | bytes 163872 | tf_op jit(solution)/shard_map/all_to_all | solution.py:45
  80.5 2.1 %reshape.161 = bf16[64,1,1280]{2,1,0:T(2,128)(2,1)} reshape(bf16[64,2,640]{2,1,0:T(2,128)(2,1)} %all-to-all-done.2) | data formatting | bytes 327680
  82.6 1.7 convolution_convert_fusion
  84.3 0.4 fusion.5
  84.7 0.6 convolution_convert_fusion.1
  85.4 1.9 %pad_maximum_fusion = bf16[1280,1280]{0,1:T(8,128)(2,1)} fusion(bf16[1280,640]{0,1:T(8,128)(2,1)S(1)} %convolution_convert_fusion, bf16[1280,640]{0,1:T(8,128)(2,1)S(1)} %convolution_convert_fusion.1), kind=kLoop, calls=%fused_computation | loop fusion | flops 6553600 | bytes 6553600 | tf_op jit(solution)/shard_map/concatenate | solution.py:62
  87.3 5.7 %copy.21 = bf16[1280,1280]{1,0:T(8,128)(2,1)} copy(bf16[1280,1280]{0,1:T(8,128)(2,1)} %pad_maximum_fusion) | data formatting | bytes 6553600
  92.9 0.0 reduce-scatter.4.cloned.1.call-update
  93.0 1.3 fusion.4
  94.3 2.3 %reduce.19 = bf16[64,1280]{1,0:T(8,128)(2,1)} reduce(bf16[64,1,1280]{2,0,1:T(8,128)(2,1)} %fusion.4, bf16[]{:T(256)} %broadcast.30), dimensions={1}, to_apply=%copy.18.reduce_sub_computation | reduce | bytes 327682 | tf_op jit(solution)/shard_map/convert_element_type | solution.py:53
  96.5 1.6 reshape.166
  98.2 5.1 %all-to-all-start.3 = ((bf16[64,2,640]{2,1,0:T(2,128)(2,1)}), bf16[64,2,640]{2,1,0:T(2,128)(2,1)}, u32[]{:S(2)}, u32[]{:S(2)}) async-start(bf16[64,2,640]{2,1,0:T(2,128)(2,1)} %reshape.166), calls=%async_computation.3 | async-start | bytes 327680 | tf_op jit(solution)/shard_map/all_to_all | solution.py:54
  103.3 1.3 fusion.3
  104.6 1.7 reduce.17
  106.2 0.7 reshape.164
  107.0 16.3 %all-to-all-done.3 = bf16[64,2,640]{2,1,0:T(2,128)(2,1)} async-done(((bf16[64,2,640]{2,1,0:T(2,128)(2,1)}), bf16[64,2,640]{2,1,0:T(2,128)(2,1)}, u32[]{:S(2)}, u32[]{:S(2)}) %all-to-all-start.3) | async-done | bytes 163872 | tf_op jit(solution)/shard_map/all_to_all | solution.py:54
  123.3 4.3 %all-to-all-start.1 = ((bf16[64,2,640]{2,1,0:T(2,128)(2,1)}), bf16[64,2,640]{2,1,0:T(2,128)(2,1)S(1)}, u32[]{:S(2)}, u32[]{:S(2)}) async-start(bf16[64,2,640]{2,1,0:T(2,128)(2,1)} %reshape.164), calls=%async_computation.1 | async-start | bytes 327680 | tf_op jit(solution)/shard_map/all_to_all | solution.py:44
  127.6 1.5 reshape.167
  129.0 18.5 %all-to-all-done.1 = bf16[64,2,640]{2,1,0:T(2,128)(2,1)S(1)} async-done(((bf16[64,2,640]{2,1,0:T(2,128)(2,1)}), bf16[64,2,640]{2,1,0:T(2,128)(2,1)S(1)}, u32[]{:S(2)}, u32[]{:S(2)}) %all-to-all-start.1) | async-done | bytes 163872 | tf_op jit(solution)/shard_map/all_to_all | solution.py:44
  147.5 0.1 reshape.165
  147.7 0.1 bitcast_reduce_fusion.1
  147.8 1.2 fusion.1
  149.0 0.1 bitcast_reduce_fusion
  149.2 0.2 convolution_bitcast_fusion
  149.4 0.4 multiply_reduce_fusion.1
  149.8 0.4 fusion.31
  150.3 1.3 fusion.2
  151.6 20.8 %reduce-scatter.4.cloned.1.call-done = bf16[80,1280]{1,0:T(8,128)(2,1)} async-done(((bf16[1280,1280]{1,0:T(8,128)(2,1)}), bf16[80,1280]{1,0:T(8,128)(2,1)}) %reduce-scatter.4.cloned.1.call-update) | async-done | bytes 204816
  172.4 1.1 copy.22
  173.6 0.8 copy.19
  174.4 0.8 copy.20
  (19 shorter events, 0.2 us)
Async XLA Ops:
  7.2 54.4 %copy-start = (bf16[1280,640]{1,0:T(8,128)(2,1)S(1)}, bf16[1280,640]{1,0:T(8,128)(2,1)}, u32[]{:S(2)}) copy-start(bf16[1280,640]{1,0:T(8,128)(2,1)} %param.8) | copy-start | bytes 4915204
  7.2 28.5 %copy-start.6 = (bf16[1,256,1280]{2,1,0:T(8,128)(2,1)S(1)}, bf16[1,256,1280]{2,1,0:T(8,128)(2,1)}, u32[]{:S(2)}) copy-start(bf16[1,256,1280]{2,1,0:T(8,128)(2,1)} %param.6) | copy-start | bytes 1966084
  12.4 43.1 %all-to-all-start = ((bf16[64,2,640]{2,1,0:T(2,128)(2,1)}), bf16[64,2,640]{2,1,0:T(2,128)(2,1)S(1)}, u32[]{:S(2)}, u32[]{:S(2)}) async-start(bf16[64,2,640]{2,1,0:T(2,128)(2,1)} %reshape.162), calls=%async_computation | async-start | bytes 327680 | tf_op jit(solution)/shard_map/all_to_all | solution.py:37
  55.5 25.0 %all-to-all-start.2 = ((bf16[64,2,640]{2,1,0:T(2,128)(2,1)}), bf16[64,2,640]{2,1,0:T(2,128)(2,1)}, u32[]{:S(2)}, u32[]{:S(2)}) async-start(bf16[64,2,640]{2,1,0:T(2,128)(2,1)} %reshape.160), calls=%async_computation.2 | async-start | bytes 327680 | tf_op jit(solution)/shard_map/all_to_all | solution.py:45
  60.6 111.8 %reduce-scatter.4.cloned.1.call-start = ((), (), s32[]{:S(2)}) async-start(), calls=%async_computation.5 | async-start | bytes 3481600
  60.8 0.7 copy-start.3
  61.9 22.4 %copy-start.1 = (bf16[1280,640]{1,0:T(8,128)(2,1)S(1)}, bf16[1280,640]{1,0:T(8,128)(2,1)}, u32[]{:S(2)}) copy-start(bf16[1280,640]{1,0:T(8,128)(2,1)} %param.9) | copy-start | bytes 4915204
  82.6 1.7 copy-start.5
  82.6 2.1 %copy-start.4 = (bf16[64,1,1280]{2,1,0:T(2,128)(2,1)S(1)}, bf16[64,1,1280]{2,1,0:T(2,128)(2,1)}, u32[]{:S(2)}) copy-start(bf16[64,1,1280]{2,1,0:T(2,128)(2,1)} %copy-done.3) | copy-start | bytes 491524
  98.2 25.1 %all-to-all-start.3 = ((bf16[64,2,640]{2,1,0:T(2,128)(2,1)}), bf16[64,2,640]{2,1,0:T(2,128)(2,1)}, u32[]{:S(2)}, u32[]{:S(2)}) async-start(bf16[64,2,640]{2,1,0:T(2,128)(2,1)} %reshape.166), calls=%async_computation.3 | async-start | bytes 327680 | tf_op jit(solution)/shard_map/all_to_all | solution.py:54
  104.6 44.6 %copy-start.2 = (bf16[1,256,1280]{2,1,0:T(8,128)(2,1)S(1)}, bf16[1,256,1280]{2,1,0:T(8,128)(2,1)}, u32[]{:S(2)}) copy-start(bf16[1,256,1280]{2,1,0:T(8,128)(2,1)} %param.5) | copy-start | bytes 1966084
  123.3 24.3 %all-to-all-start.1 = ((bf16[64,2,640]{2,1,0:T(2,128)(2,1)}), bf16[64,2,640]{2,1,0:T(2,128)(2,1)S(1)}, u32[]{:S(2)}, u32[]{:S(2)}) async-start(bf16[64,2,640]{2,1,0:T(2,128)(2,1)} %reshape.164), calls=%async_computation.1 | async-start | bytes 327680 | tf_op jit(solution)/shard_map/all_to_all | solution.py:44
  147.7 1.7 copy-start.7
  149.0 1.2 copy-start.8
Sparse Core Ops, SparseCore 0:
  93.1 79.2 reduce-scatter.3
where the time goes:
time: 186 us; the launch traced here: 182 us
  waiting for transfers between devices  92.5 us (50%)
  starting transfers between devices  37.9 us (20%)
  local copies, waits for them, and re-layouts  17.4 us (9%)
  between operations  14.2 us (8%)
  matrix products  12.4 us (7%)
  other arithmetic  7.68 us (4%)
    all_to_all x1, starting transfers between devices, per_device(): lax.all_to_all(spread(slot_in), 'expert', split_axis=0, concat_axis=0, ti...  23.3 us
    unnamed x2, waiting for transfers between devices  20.9 us
    all_to_all x1, waiting for transfers between devices, per_device(): lax.all_to_all(spread(slot_grad), 'expert', split_axis=0, concat_axis=0,...  18.6 us
    all_to_all x1, waiting for transfers between devices, per_device(): lax.all_to_all(out_part, 'expert', split_axis=0, concat_axis=0, tiled=True)  18.5 us
    all_to_all x1, waiting for transfers between devices, per_device(): lax.all_to_all(spread(slot_in), 'expert', split_axis=0, concat_axis=0, ti...  18.2 us
    unnamed x30, local copies, waits for them, and re-layouts  16.8 us
    all_to_all x1, waiting for transfers between devices, per_device(): lax.all_to_all(grad_part, 'expert', split_axis=0, concat_axis=0, tiled=True)  16.3 us
    all_to_all x1, starting transfers between devices, per_device(): lax.all_to_all(grad_part, 'expert', split_axis=0, concat_axis=0, tiled=True)  5.13 us
  transfers between devices with their start and end apart: 5, of which 5 were waited for; matrix products, arithmetic and copies ran while one was open for 9% of the time, Pallas kernels for 0%

commit v1 on v0

v1 whole, which is shorter than its diff:
```python
import functools

import jax
import jax.numpy as jnp
import numpy as np
from jax import lax
from jax.experimental import pallas as pl
from jax.experimental.pallas import tpu as pltpu
from jax.sharding import Mesh
from jax.sharding import PartitionSpec as P

root_half = 0.7071067811865476
density = 0.3989422804014327
f32 = jnp.float32
bf16 = jnp.bfloat16

AXES = ("yh", "yl", "xl", "xh", "zh", "zl", "c")
SIZES = (4, 2, 2, 2, 4, 4, 2)
DP = ("yh", "yl", "xl")
PEERS = ("xh", "zh", "zl", "c")
CHIPS = ("xh", "zh", "zl")
QUAD = ("yl", "xl")
EXPERTS, SPREAD, CHIP_COUNT = 8, 4, 32
QUADS = 4
VMEM = 48 * 1024 * 1024


def nn(a, b):
    return lax.dot_general(a, b, (((1,), (0,)), ((), ())), preferred_element_type=f32)


def nt(a, b):
    return lax.dot_general(a, b, (((1,), (1,)), ((), ())), preferred_element_type=f32)


def tn(a, b):
    return lax.dot_general(a, b, (((0,), (0,)), ((), ())), preferred_element_type=f32)


def pick(rows, cols, source):
    r = lax.broadcasted_iota(jnp.int32, (rows, cols), 0)
    c = lax.broadcasted_iota(jnp.int32, (rows, cols), 1)
    return jnp.where(c == source(r), 1.0, 0.0).astype(bf16)


def call(kernel, outs, flops, nbytes, scratch=(), smem=0, ins=1):
    vm = pl.BlockSpec(memory_space=pltpu.VMEM)
    specs = [pl.BlockSpec(memory_space=pltpu.SMEM)] * smem + [vm] * (ins - smem)
    return pl.pallas_call(
        kernel,
        out_shape=[jax.ShapeDtypeStruct(s, d) for s, d in outs],
        in_specs=specs,
        out_specs=[vm] * len(outs),
        scratch_shapes=list(scratch),
        compiler_params=pltpu.CompilerParams(vmem_limit_bytes=VMEM),
        cost_estimate=pl.CostEstimate(flops=flops, bytes_accessed=nbytes, transcendentals=0),
    )


def route_kernel(tok, cot, sp, send, disp, comb):
    logits = nt(sp[...], tok[...])
    ed = jnp.exp(logits - jnp.max(logits, axis=1, keepdims=True))
    d = ed / jnp.sum(ed, axis=1, keepdims=True)
    ec = jnp.exp(logits - jnp.max(logits, axis=0, keepdims=True))
    c = ec / jnp.sum(ec, axis=0, keepdims=True)
    disp[...] = d
    comb[...] = c
    slot_in = nn(d.astype(bf16), tok[...]).astype(bf16)
    slot_grad = nn(c.astype(bf16), cot[...]).astype(bf16)
    both = jnp.concatenate([slot_in.astype(f32), slot_grad.astype(f32)], axis=0).astype(bf16)
    rows = 2 * CHIP_COUNT
    sel = pick(rows, 16, lambda r: (r % 2) * EXPERTS + r // (2 * SPREAD))
    send[...] = nn(sel, both).astype(bf16)


def expert_kernel(place, own, other, w_in, w_out, part_own, part_other, c0, c1, c2, c3, turned):
    n = own.shape[0] // 2
    even = pick(n, 2 * n, lambda r: 2 * r)
    odd = pick(n, 2 * n, lambda r: 2 * r + 1)
    rows_in = jnp.concatenate([nn(even, own[...]), nn(even, other[...])], axis=0).astype(bf16)
    rows_grad = jnp.concatenate([nn(odd, own[...]), nn(odd, other[...])], axis=0).astype(bf16)
    preact = nn(rows_in, w_in[...])
    hidden_grad = nn(rows_grad, w_out[...])
    cumulative = 0.5 * (1.0 + lax.erf(preact * root_half))
    slope = cumulative + preact * jnp.exp(-0.5 * preact * preact) * density
    act = (preact * cumulative).astype(bf16)
    gp = (hidden_grad * slope).astype(bf16)
    out_part = nt(act, w_out[...]).astype(bf16)
    grad_part = nt(gp, w_in[...]).astype(bf16)
    part_own[...] = (tn(even, out_part[:n]) + tn(odd, grad_part[:n])).astype(bf16)
    part_other[...] = (tn(even, out_part[n:]) + tn(odd, grad_part[n:])).astype(bf16)
    both = jnp.concatenate([rows_in, rows_grad], axis=0)
    turned[...] = jnp.transpose(both.astype(f32)).astype(bf16)
    yh, j0 = place[0], place[1]
    depth = turned.shape[0] // 16
    for m, chunk in enumerate((c0, c1, c2, c3)):
        chunk[0 : 2 * n, :] = gp
        chunk[2 * n : 4 * n, :] = act
        j = jnp.bitwise_xor(j0, m)
        pieces = []
        for k in range(4):
            at = (lax.rem(yh + k, 4) * QUADS + j) * depth
            pieces.append(turned[pl.ds(pl.multiple_of(at, 16), depth), :])
        piece = jnp.concatenate(pieces, axis=0)
        for b in range(5):
            chunk[4 * n : 6 * n, 128 * b : 128 * (b + 1)] = piece[64 * b : 64 * (b + 1)]


def term_kernel(c0, c1, c2, c3, keep, s1, s2, s3):
    left, right = [], []
    zero = jnp.zeros((64, 640), bf16)
    for chunk in (c0, c1, c2, c3):
        left.append(jnp.concatenate([chunk[128:192, 128 * b : 128 * (b + 1)] for b in range(5)], axis=0))
        right.append(jnp.concatenate([chunk[0:64, :], zero], axis=1))
        right.append(jnp.concatenate([zero, chunk[64:128, :]], axis=1))
    total = nn(jnp.concatenate(left, axis=1), jnp.concatenate(right, axis=0))
    depth = keep.shape[0]
    keep[...] = total[:depth]
    for k, s in enumerate((s1, s2, s3)):
        s[...] = total[(k + 1) * depth : (k + 2) * depth].astype(bf16)


def finish_kernel(tok, cot, sp, parts, disp, comb, mixed, grad_tokens):
    r = lax.broadcasted_iota(jnp.int32, (16, 2 * CHIP_COUNT), 0)
    c = lax.broadcasted_iota(jnp.int32, (16, 2 * CHIP_COUNT), 1)
    sel = jnp.where(((c % 2) * EXPERTS + c // (2 * SPREAD)) == r, 1.0, 0.0).astype(bf16)
    slots = nn(sel, parts[...])
    slot_out = slots[:8].astype(bf16)
    grad_slot_in = slots[8:].astype(bf16)
    d, cm = disp[...], comb[...]
    mixed[...] = tn(cm.astype(bf16), slot_out).astype(bf16)
    combine_grad = nt(slot_out, cot[...])
    dispatch_grad = nt(grad_slot_in, tok[...])
    lg = cm * (combine_grad - jnp.sum(cm * combine_grad, axis=0, keepdims=True))
    lg = lg + d * (dispatch_grad - jnp.sum(d * dispatch_grad, axis=1, keepdims=True))
    rows = jnp.concatenate([d.astype(bf16).astype(f32), lg.astype(bf16).astype(f32)], axis=0)
    cols = jnp.concatenate([grad_slot_in.astype(f32), sp[...].astype(f32)], axis=0)
    grad_tokens[...] = tn(rows.astype(bf16), cols.astype(bf16)).astype(bf16)


def per_device(tokens, cotangent, slot_params, in_weight, out_weight):
    tok, cot = tokens[0], cotangent[0]
    patch, width = tok.shape
    hidden = in_weight.shape[1]
    sp = slot_params.T
    n2 = 2 * CHIP_COUNT
    send, disp, comb = call(
        route_kernel,
        [((n2, width), bf16), ((EXPERTS, patch), f32), ((EXPERTS, patch), f32)],
        10**7, 1500000, ins=3,
    )(tok, cot, sp)

    def exchange(rows):
        got = lax.all_to_all(rows.reshape(CHIP_COUNT, 2, width), CHIPS, 0, 0, tiled=True)
        return got.reshape(n2, width)

    swap = [(0, 1), (1, 0)]
    own = exchange(send)
    other = lax.ppermute(own, "c", swap)
    place = jnp.stack([lax.axis_index("yh"), lax.axis_index(QUAD)]).astype(jnp.int32)
    chunk_shape = ((192, hidden), bf16)
    part_own, part_other, c0, c1, c2, c3 = call(
        expert_kernel,
        [((n2, width), bf16), ((n2, width), bf16)] + [chunk_shape] * 4,
        5 * 10**8, 4500000, scratch=[pltpu.VMEM((width, 128), bf16)], smem=1, ins=5,
    )(place, own, other, in_weight, out_weight)

    back = lax.ppermute(part_other, "c", swap)
    got = [c0]
    for m, chunk in ((1, c1), (2, c2), (3, c3)):
        got.append(lax.ppermute(chunk, QUAD, [(i, i ^ m) for i in range(QUADS)]))
    parts = exchange((part_own.astype(f32) + back.astype(f32)).astype(bf16))

    depth = width // 16
    piece = ((depth, 2 * hidden), bf16)
    keep, s1, s2, s3 = call(
        term_kernel,
        [((depth, 2 * hidden), f32), piece, piece, piece],
        4 * 10**8, 2500000, ins=4,
    )(*got)
    total = keep
    for k, s in ((1, s1), (2, s2), (3, s3)):
        total = total + lax.ppermute(s, "yh", [(i, (i + k) % 4) for i in range(4)]).astype(f32)

    mixed, grad_tokens = call(
        finish_kernel,
        [((patch, width), bf16), ((patch, width), bf16)],
        3 * 10**7, 3000000, ins=6,
    )(tok, cot, sp, parts, disp, comb)
    return mixed[None], grad_tokens[None], total[:, :hidden], total[:, hidden:]


def solution(mesh):
    fine = Mesh(np.asarray(mesh.devices).reshape(SIZES), AXES)
    return jax.shard_map(
        per_device,
        mesh=fine,
        in_specs=(P(AXES), P(AXES), P(), P(None, PEERS), P(None, PEERS)),
        out_specs=(P(AXES), P(AXES), P(DP, PEERS), P(DP, PEERS)),
        check_vma=False,
    )
```

time: 186 us -> 113 us (0.61)
  the two profiles are of different devices: /device:TPU:1 before, /device:TPU:8 now
where the time goes in v1:
time: 113 us; the launch traced here: 112 us
  blocking collectives  41.3 us (37%)
  starting transfers between devices  31.7 us (28%)
  waiting for transfers between devices  25.7 us (23%)
  Pallas kernels  6.37 us (6%)
  local copies, waits for them, and re-layouts  6.05 us (5%)
    all_to_all x1, blocking collectives, exchange(): lax.all_to_all(rows.reshape(CHIP_COUNT, 2, width), CHIPS, 0, 0, tiled=True)  41.3 us
    ppermute x3, starting transfers between devices, per_device(): lax.ppermute(s, 'yh', [(i, (i + k) % 4) for i in range(4)]).astype(f32)  14.8 us
    all_to_all x1, waiting for transfers between devices, exchange(): lax.all_to_all(rows.reshape(CHIP_COUNT, 2, width), CHIPS, 0, 0, tiled=True)  14 us
    ppermute x3, starting transfers between devices, per_device(): got.append(lax.ppermute(chunk, QUAD, [(i, i ^ m) for i in range(QUADS)]))  9.21 us
    ppermute x3, waiting for transfers between devices, per_device(): got.append(lax.ppermute(chunk, QUAD, [(i, i ^ m) for i in range(QUADS)]))  7.09 us
    unnamed x16, local copies, waits for them, and re-layouts  4.35 us
    all_to_all x1, starting transfers between devices, exchange(): lax.all_to_all(rows.reshape(CHIP_COUNT, 2, width), CHIPS, 0, 0, tiled=True)  3.86 us
    ppermute x3, waiting for transfers between devices, per_device(): lax.ppermute(s, 'yh', [(i, (i + k) % 4) for i in range(4)]).astype(f32)  3.38 us
  transfers between devices with their start and end apart: 9, of which 6 were waited for; matrix products, arithmetic and copies ran while one was open for 2% of the time, Pallas kernels for 1%

profile of v1, /device:TPU:8, one launch (start us, length us, event | category | flops | bytes accessed | tf_op | source)
XLA Modules:
  0.0 112.2 jit_solution(8791029745767214343)
XLA Ops:
  0.6 0.0 copy-start
  0.6 1.1 copy-done
  1.7 0.0 copy-start.2
  1.7 1.1 copy-done.2
  2.8 0.0 copy-start.6
  2.8 0.7 copy-done.6
  3.5 0.0 copy-start.4
  3.5 1.2 %shard_map.84 = (bf16[64,1280]{1,0:T(8,128)(2,1)S(1)}, f32[8,256]{1,0:T(8,128)S(1)}, f32[8,256]{1,0:T(8,128)S(1)}) custom-call(bf16[256,1280]{1,0:T(8,128)(2,1)S(1)} %bitcast.7, bf16[256,1280]{1,0:T(8,128)(2,1)S(1)} %bitcast.9, bf16[8,1280]{1,0:T(8,128)(2,1)S(1)} %bitcast.11), custom_call_target="tpu_custom_call" | custom-call | flops 10000000 | bytes 1500000 | tf_op jit(solution)/shard_map/pallas_call | solution.py:147
  4.7 0.1 reshape.20
  4.8 41.3 %all_to_all.10 = bf16[32,2,1280]{2,1,0:T(2,128)(2,1)S(1)} all-to-all(bf16[32,2,1280]{2,1,0:T(2,128)(2,1)S(1)} %reshape.20), channel_id=1, replica_groups=mesh['yh'=4,'yl'=2,'xl'=2,'xh'=2,'zh'=4,'zl'=4,'c'=2] {'xh','zh','zl'}, dimensions={0} | all-to-all | bytes 327680 | tf_op jit(solution)/shard_map/all_to_all | solution.py:154
  46.1 0.1 reshape.21.own
  46.1 1.9 %collective-permute-start = (bf16[64,1280]{1,0:T(8,128)(2,1)S(1)}, bf16[64,1280]{1,0:T(8,128)(2,1)S(1)}, u32[]{:S(2)}, u32[]{:S(2)}) collective-permute-start(bf16[64,1280]{1,0:T(8,128)(2,1)S(1)} %reshape.21.own), channel_id=1, source_target_pairs={{0,1},{1,0},{2,3},{3,2},{4,5},{5,4},{6,7},{7,6},{8,9},{9,8},{10,11... | collective-permute-start | bytes 491528 | tf_op jit(solution)/shard_map/ppermute | solution.py:159
  48.1 0.1 pad_add_fusion.place
  48.1 1.3 %collective-permute-done.other = bf16[64,1280]{1,0:T(8,128)(2,1)S(1)} collective-permute-done((bf16[64,1280]{1,0:T(8,128)(2,1)S(1)}, bf16[64,1280]{1,0:T(8,128)(2,1)S(1)}, u32[]{:S(2)}, u32[]{:S(2)}) %collective-permute-start) | collective-permute-done | bytes 163872 | tf_op jit(solution)/shard_map/ppermute | solution.py:159
  49.4 0.0 copy-done.4
  49.4 0.0 copy-start.5
  49.4 1.4 %copy-done.5 = bf16[1280,640]{1,0:T(8,128)(2,1)S(1)} copy-done((bf16[1280,640]{1,0:T(8,128)(2,1)S(1)}, bf16[1280,640]{1,0:T(8,128)(2,1)}, u32[]{:S(2)}) %copy-start.5) | copy-done | bytes 1638424
  50.8 2.6 %shard_map.85 = (bf16[64,1280]{1,0:T(8,128)(2,1)S(1)}, bf16[64,1280]{1,0:T(8,128)(2,1)S(1)}, bf16[192,640]{1,0:T(8,128)(2,1)S(1)}, bf16[192,640]{1,0:T(8,128)(2,...) custom-call(s32[2]{0:T(128)S(1)} %pad_add_fusion.place, bf16[64,1280]{1,0:T(8,128)(2,1)S(1)} %reshape.21.own, ...), custom_call_target="tpu_custom_call" | custom-call | flops 500000000 | bytes 4500000 | tf_op jit(solution)/shard_map/pallas_call | solution.py:162
  53.4 2.5 %collective-permute-start.2 = (bf16[192,640]{1,0:T(8,128)(2,1)S(1)}, bf16[192,640]{1,0:T(8,128)(2,1)S(1)}, u32[]{:S(2)}, u32[]{:S(2)}) collective-permute-start(bf16[192,640]{1,0:T(8,128)(2,1)S(1)} %get-tuple-element.27), channel_id=1, source_target_pairs={{0,64},{64,0},{128,192},{192,128},{1,65},{65,1},{129,193},{193,129... | collective-permute-start | bytes 737288 | tf_op jit(solution)/shard_map/ppermute | solution.py:171
  55.9 2.4 %collective-permute-start.3 = (bf16[192,640]{1,0:T(8,128)(2,1)S(1)}, bf16[192,640]{1,0:T(8,128)(2,1)S(1)}, u32[]{:S(2)}, u32[]{:S(2)}) collective-permute-start(bf16[192,640]{1,0:T(8,128)(2,1)S(1)} %get-tuple-element.28), channel_id=1, source_target_pairs={{0,128},{64,192},{128,0},{192,64},{1,129},{65,193},{129,1},{193,65... | collective-permute-start | bytes 737288 | tf_op jit(solution)/shard_map/ppermute | solution.py:171
  58.3 4.4 %collective-permute-start.4 = (bf16[192,640]{1,0:T(8,128)(2,1)S(1)}, bf16[192,640]{1,0:T(8,128)(2,1)S(1)}, u32[]{:S(2)}, u32[]{:S(2)}) collective-permute-start(bf16[192,640]{1,0:T(8,128)(2,1)S(1)} %get-tuple-element.29), channel_id=1, source_target_pairs={{0,192},{64,128},{128,64},{192,0},{1,193},{65,129},{129,65},{193,1... | collective-permute-start | bytes 737288 | tf_op jit(solution)/shard_map/ppermute | solution.py:171
  62.7 1.9 %collective-permute-start.1 = (bf16[64,1280]{1,0:T(8,128)(2,1)S(1)}, bf16[64,1280]{1,0:T(8,128)(2,1)S(1)}, u32[]{:S(2)}, u32[]{:S(2)}) collective-permute-start(bf16[64,1280]{1,0:T(8,128)(2,1)S(1)} %get-tuple-element.21), channel_id=1, source_target_pairs={{0,1},{1,0},{2,3},{3,2},{4,5},{5,4},{6,7},{7,6},{8,9},{9,8},{10,11... | collective-permute-start | bytes 491528 | tf_op jit(solution)/shard_map/ppermute | solution.py:168
  64.6 0.0 collective-permute-done.2.c1
  64.6 2.1 %collective-permute-done.3.c2 = bf16[192,640]{1,0:T(8,128)(2,1)S(1)} collective-permute-done((bf16[192,640]{1,0:T(8,128)(2,1)S(1)}, bf16[192,640]{1,0:T(8,128)(2,1)S(1)}, u32[]{:S(2)}, u32[]{:S(2)}) %collective-permute-start.3) | collective-permute-done | bytes 245792 | tf_op jit(solution)/shard_map/ppermute | solution.py:171
  66.7 5.0 %collective-permute-done.4.c3 = bf16[192,640]{1,0:T(8,128)(2,1)S(1)} collective-permute-done((bf16[192,640]{1,0:T(8,128)(2,1)S(1)}, bf16[192,640]{1,0:T(8,128)(2,1)S(1)}, u32[]{:S(2)}, u32[]{:S(2)}) %collective-permute-start.4) | collective-permute-done | bytes 245792 | tf_op jit(solution)/shard_map/ppermute | solution.py:171
  71.7 0.6 shard_map.87
  72.3 4.5 %collective-permute-start.5 = (bf16[80,1280]{1,0:T(8,128)(2,1)S(1)}, bf16[80,1280]{1,0:T(8,128)(2,1)S(1)}, u32[]{:S(2)}, u32[]{:S(2)}) collective-permute-start(bf16[80,1280]{1,0:T(8,128)(2,1)S(1)} %get-tuple-element.31), channel_id=1, source_target_pairs={{0,256},{256,512},{512,768},{768,0},{1,257},{257,513},{513,769},{7... | collective-permute-start | bytes 614408 | tf_op jit(solution)/shard_map/ppermute | solution.py:183
  76.8 5.0 %collective-permute-start.6 = (bf16[80,1280]{1,0:T(8,128)(2,1)S(1)}, bf16[80,1280]{1,0:T(8,128)(2,1)S(1)}, u32[]{:S(2)}, u32[]{:S(2)}) collective-permute-start(bf16[80,1280]{1,0:T(8,128)(2,1)S(1)} %get-tuple-element.32), channel_id=1, source_target_pairs={{0,512},{256,768},{512,0},{768,256},{1,513},{257,769},{513,1},{769... | collective-permute-start | bytes 614408 | tf_op jit(solution)/shard_map/ppermute | solution.py:183
  81.8 5.2 %collective-permute-start.7 = (bf16[80,1280]{1,0:T(8,128)(2,1)S(1)}, bf16[80,1280]{1,0:T(8,128)(2,1)S(1)}, u32[]{:S(2)}, u32[]{:S(2)}) collective-permute-start(bf16[80,1280]{1,0:T(8,128)(2,1)S(1)} %get-tuple-element.33), channel_id=1, source_target_pairs={{0,768},{256,0},{512,256},{768,512},{1,769},{257,1},{513,257},{769... | collective-permute-start | bytes 614408 | tf_op jit(solution)/shard_map/ppermute | solution.py:183
  87.1 0.0 collective-permute-done.1
  87.2 0.0 copy-start.1
  87.2 0.0 copy-start.3
  87.2 0.0 copy-start.7
  87.2 0.7 reshape.22
  87.9 3.9 %all-to-all-start.1 = ((bf16[32,2,1280]{2,1,0:T(2,128)(2,1)}), bf16[32,2,1280]{2,1,0:T(2,128)(2,1)S(1)}, u32[]{:S(2)}, u32[]{:S(2)}) async-start(bf16[32,2,1280]{2,1,0:T(2,128)(2,1)} %reshape.22), calls=%async_computation.1 | async-start | bytes 327680 | tf_op jit(solution)/shard_map/all_to_all | solution.py:154
  91.8 0.0 collective-permute-done.5
  91.8 1.3 %collective-permute-done.6 = bf16[80,1280]{1,0:T(8,128)(2,1)S(1)} collective-permute-done((bf16[80,1280]{1,0:T(8,128)(2,1)S(1)}, bf16[80,1280]{1,0:T(8,128)(2,1)S(1)}, u32[]{:S(2)}, u32[]{:S(2)}) %collective-permute-start.6) | collective-permute-done | bytes 204832 | tf_op jit(solution)/shard_map/ppermute | solution.py:183
  93.1 2.1 %collective-permute-done.7 = bf16[80,1280]{1,0:T(8,128)(2,1)S(1)} collective-permute-done((bf16[80,1280]{1,0:T(8,128)(2,1)S(1)}, bf16[80,1280]{1,0:T(8,128)(2,1)S(1)}, u32[]{:S(2)}, u32[]{:S(2)}) %collective-permute-start.7) | collective-permute-done | bytes 204832 | tf_op jit(solution)/shard_map/ppermute | solution.py:183
  95.2 0.1 convert_add_fusion
  95.3 0.8 fusion
  96.1 14.0 %all-to-all-done.1 = bf16[32,2,1280]{2,1,0:T(2,128)(2,1)S(1)} async-done(((bf16[32,2,1280]{2,1,0:T(2,128)(2,1)}), bf16[32,2,1280]{2,1,0:T(2,128)(2,1)S(1)}, u32[]{:S(2)}, u32[]{:S(2)}) %all-to-all-start.1) | async-done | bytes 163872 | tf_op jit(solution)/shard_map/all_to_all | solution.py:154
  110.1 0.1 reshape.23.parts
  110.1 0.0 copy-done.1
  110.1 0.0 copy-done.3
  110.1 0.0 copy-done.7
  110.2 2.0 %shard_map.86 = (bf16[256,1280]{1,0:T(8,128)(2,1)}, bf16[256,1280]{1,0:T(8,128)(2,1)}) custom-call(bf16[256,1280]{1,0:T(8,128)(2,1)S(1)} %bitcast.8, bf16[256,1280]{1,0:T(8,128)(2,1)S(1)} %bitcast.10, bf16[8,1280]{1,0:T(8,128)(2,1)S(1)} %bitcast.12, bf16[64,1280]{1,0:T(8,128)(2,1)S(1)} %reshape.23.parts, f32[8,256]{1,0:T(8,128)S(1)} %get-tuple-element.22.disp, ...), custom_call_target="tpu_custom_call" | custom-call | flops 30000000 | bytes 3000000 | tf_op jit(solution)/shard_map/pallas_call | solution.py:185
  (1 shorter events, 0.0 us)
Async XLA Ops:
  0.6 1.1 copy-start
  1.7 1.1 copy-start.2
  2.8 0.7 copy-start.6
  3.5 45.9 %copy-start.4 = (bf16[1280,640]{1,0:T(8,128)(2,1)S(1)}, bf16[1280,640]{1,0:T(8,128)(2,1)}, u32[]{:S(2)}) copy-start(bf16[1280,640]{1,0:T(8,128)(2,1)} %w_in.1) | copy-start | bytes 4915204
  46.1 3.3 %collective-permute-start = (bf16[64,1280]{1,0:T(8,128)(2,1)S(1)}, bf16[64,1280]{1,0:T(8,128)(2,1)S(1)}, u32[]{:S(2)}, u32[]{:S(2)}) collective-permute-start(bf16[64,1280]{1,0:T(8,128)(2,1)S(1)} %reshape.21.own), channel_id=1, source_target_pairs={{0,1},{1,0},{2,3},{3,2},{4,5},{5,4},{6,7},{7,6},{8,9},{9,8},{10,11... | collective-permute-start | bytes 491528 | tf_op jit(solution)/shard_map/ppermute | solution.py:159
  49.4 1.4 %copy-start.5 = (bf16[1280,640]{1,0:T(8,128)(2,1)S(1)}, bf16[1280,640]{1,0:T(8,128)(2,1)}, u32[]{:S(2)}) copy-start(bf16[1280,640]{1,0:T(8,128)(2,1)} %w_out.1) | copy-start | bytes 4915204
  53.4 11.2 %collective-permute-start.2 = (bf16[192,640]{1,0:T(8,128)(2,1)S(1)}, bf16[192,640]{1,0:T(8,128)(2,1)S(1)}, u32[]{:S(2)}, u32[]{:S(2)}) collective-permute-start(bf16[192,640]{1,0:T(8,128)(2,1)S(1)} %get-tuple-element.27), channel_id=1, source_target_pairs={{0,64},{64,0},{128,192},{192,128},{1,65},{65,1},{129,193},{193,129... | collective-permute-start | bytes 737288 | tf_op jit(solution)/shard_map/ppermute | solution.py:171
  55.9 10.7 %collective-permute-start.3 = (bf16[192,640]{1,0:T(8,128)(2,1)S(1)}, bf16[192,640]{1,0:T(8,128)(2,1)S(1)}, u32[]{:S(2)}, u32[]{:S(2)}) collective-permute-start(bf16[192,640]{1,0:T(8,128)(2,1)S(1)} %get-tuple-element.28), channel_id=1, source_target_pairs={{0,128},{64,192},{128,0},{192,64},{1,129},{65,193},{129,1},{193,65... | collective-permute-start | bytes 737288 | tf_op jit(solution)/shard_map/ppermute | solution.py:171
  58.3 13.4 %collective-permute-start.4 = (bf16[192,640]{1,0:T(8,128)(2,1)S(1)}, bf16[192,640]{1,0:T(8,128)(2,1)S(1)}, u32[]{:S(2)}, u32[]{:S(2)}) collective-permute-start(bf16[192,640]{1,0:T(8,128)(2,1)S(1)} %get-tuple-element.29), channel_id=1, source_target_pairs={{0,192},{64,128},{128,64},{192,0},{1,193},{65,129},{129,65},{193,1... | collective-permute-start | bytes 737288 | tf_op jit(solution)/shard_map/ppermute | solution.py:171
  62.7 24.4 %collective-permute-start.1 = (bf16[64,1280]{1,0:T(8,128)(2,1)S(1)}, bf16[64,1280]{1,0:T(8,128)(2,1)S(1)}, u32[]{:S(2)}, u32[]{:S(2)}) collective-permute-start(bf16[64,1280]{1,0:T(8,128)(2,1)S(1)} %get-tuple-element.21), channel_id=1, source_target_pairs={{0,1},{1,0},{2,3},{3,2},{4,5},{5,4},{6,7},{7,6},{8,9},{9,8},{10,11... | collective-permute-start | bytes 491528 | tf_op jit(solution)/shard_map/ppermute | solution.py:168
  72.3 19.5 %collective-permute-start.5 = (bf16[80,1280]{1,0:T(8,128)(2,1)S(1)}, bf16[80,1280]{1,0:T(8,128)(2,1)S(1)}, u32[]{:S(2)}, u32[]{:S(2)}) collective-permute-start(bf16[80,1280]{1,0:T(8,128)(2,1)S(1)} %get-tuple-element.31), channel_id=1, source_target_pairs={{0,256},{256,512},{512,768},{768,0},{1,257},{257,513},{513,769},{7... | collective-permute-start | bytes 614408 | tf_op jit(solution)/shard_map/ppermute | solution.py:183
  76.8 16.3 %collective-permute-start.6 = (bf16[80,1280]{1,0:T(8,128)(2,1)S(1)}, bf16[80,1280]{1,0:T(8,128)(2,1)S(1)}, u32[]{:S(2)}, u32[]{:S(2)}) collective-permute-start(bf16[80,1280]{1,0:T(8,128)(2,1)S(1)} %get-tuple-element.32), channel_id=1, source_target_pairs={{0,512},{256,768},{512,0},{768,256},{1,513},{257,769},{513,1},{769... | collective-permute-start | bytes 614408 | tf_op jit(solution)/shard_map/ppermute | solution.py:183
  81.8 13.3 %collective-permute-start.7 = (bf16[80,1280]{1,0:T(8,128)(2,1)S(1)}, bf16[80,1280]{1,0:T(8,128)(2,1)S(1)}, u32[]{:S(2)}, u32[]{:S(2)}) collective-permute-start(bf16[80,1280]{1,0:T(8,128)(2,1)S(1)} %get-tuple-element.33), channel_id=1, source_target_pairs={{0,768},{256,0},{512,256},{768,512},{1,769},{257,1},{513,257},{769... | collective-permute-start | bytes 614408 | tf_op jit(solution)/shard_map/ppermute | solution.py:183
  87.2 23.0 %copy-start.1 = (bf16[1,256,1280]{2,1,0:T(8,128)(2,1)S(1)}, bf16[1,256,1280]{2,1,0:T(8,128)(2,1)}, u32[]{:S(2)}) copy-start(bf16[1,256,1280]{2,1,0:T(8,128)(2,1)} %param.5) | copy-start | bytes 1966084
  87.2 23.0 %copy-start.3 = (bf16[1,256,1280]{2,1,0:T(8,128)(2,1)S(1)}, bf16[1,256,1280]{2,1,0:T(8,128)(2,1)}, u32[]{:S(2)}) copy-start(bf16[1,256,1280]{2,1,0:T(8,128)(2,1)} %param.6) | copy-start | bytes 1966084
  87.2 23.0 %copy-start.7 = (bf16[1280,8]{0,1:T(8,128)(2,1)S(1)}, bf16[1280,8]{0,1:T(8,128)(2,1)}, u32[]{:S(2)}) copy-start(bf16[1280,8]{0,1:T(8,128)(2,1)} %param.7) | copy-start | bytes 61444
  87.9 22.1 %all-to-all-start.1 = ((bf16[32,2,1280]{2,1,0:T(2,128)(2,1)}), bf16[32,2,1280]{2,1,0:T(2,128)(2,1)S(1)}, u32[]{:S(2)}, u32[]{:S(2)}) async-start(bf16[32,2,1280]{2,1,0:T(2,128)(2,1)} %reshape.22), calls=%async_computation.1 | async-start | bytes 327680 | tf_op jit(solution)/shard_map/all_to_all | solution.py:154

commit v2 on v1

--- a/solution.py
+++ b/solution.py
@@ -22,7 +22,7 @@
 QUAD = ("yl", "xl")
 EXPERTS, SPREAD, CHIP_COUNT = 8, 4, 32
 QUADS = 4
-VMEM = 48 * 1024 * 1024
+ROOM = 20_000_000
 
 
 def nn(a, b):
@@ -43,21 +43,28 @@
     return jnp.where(c == source(r), 1.0, 0.0).astype(bf16)
 
 
-def call(kernel, outs, flops, nbytes, scratch=(), smem=0, ins=1):
+def call(kernel, outs, flops, nbytes, ins, scratch=(), room=ROOM):
     vm = pl.BlockSpec(memory_space=pltpu.VMEM)
-    specs = [pl.BlockSpec(memory_space=pltpu.SMEM)] * smem + [vm] * (ins - smem)
+    spaces = {"v": vm, "s": pl.BlockSpec(memory_space=pltpu.SMEM), "a": pl.BlockSpec(memory_space=pl.ANY)}
+    spaces["h"] = pl.BlockSpec(memory_space=pltpu.HBM)
+    specs = [spaces[letter] for letter in ins]
     return pl.pallas_call(
         kernel,
         out_shape=[jax.ShapeDtypeStruct(s, d) for s, d in outs],
         in_specs=specs,
         out_specs=[vm] * len(outs),
         scratch_shapes=list(scratch),
-        compiler_params=pltpu.CompilerParams(vmem_limit_bytes=VMEM),
+        compiler_params=pltpu.CompilerParams(vmem_limit_bytes=room),
         cost_estimate=pl.CostEstimate(flops=flops, bytes_accessed=nbytes, transcendentals=0),
     )
 
 
-def route_kernel(tok, cot, sp, send, disp, comb):
+def route_kernel(tok_hbm, cot_hbm, sp, send, disp, comb, tok, cot, sems):
+    copy_tok = pltpu.make_async_copy(tok_hbm, tok, sems.at[0])
+    copy_cot = pltpu.make_async_copy(cot_hbm, cot, sems.at[1])
+    copy_tok.start()
+    copy_cot.start()
+    copy_tok.wait()
     logits = nt(sp[...], tok[...])
     ed = jnp.exp(logits - jnp.max(logits, axis=1, keepdims=True))
     d = ed / jnp.sum(ed, axis=1, keepdims=True)
@@ -66,6 +73,7 @@
     disp[...] = d
     comb[...] = c
     slot_in = nn(d.astype(bf16), tok[...]).astype(bf16)
+    copy_cot.wait()
     slot_grad = nn(c.astype(bf16), cot[...]).astype(bf16)
     both = jnp.concatenate([slot_in.astype(f32), slot_grad.astype(f32)], axis=0).astype(bf16)
     rows = 2 * CHIP_COUNT
@@ -106,7 +114,7 @@
             chunk[4 * n : 6 * n, 128 * b : 128 * (b + 1)] = piece[64 * b : 64 * (b + 1)]
 
 
-def term_kernel(c0, c1, c2, c3, keep, s1, s2, s3):
+def term_kernel(c0, c1, c2, c3, _, keep, s1, s2, s3):
     left, right = [], []
     zero = jnp.zeros((64, 640), bf16)
     for chunk in (c0, c1, c2, c3):
@@ -120,7 +128,8 @@
         s[...] = total[(k + 1) * depth : (k + 2) * depth].astype(bf16)
 
 
-def finish_kernel(tok, cot, sp, parts, disp, comb, mixed, grad_tokens):
+def finish_kernel(tok, cot, sp, parts, disp, comb, mixed, grad_tokens, done):
+    done[...] = jnp.zeros_like(done)
     r = lax.broadcasted_iota(jnp.int32, (16, 2 * CHIP_COUNT), 0)
     c = lax.broadcasted_iota(jnp.int32, (16, 2 * CHIP_COUNT), 1)
     sel = jnp.where(((c % 2) * EXPERTS + c // (2 * SPREAD)) == r, 1.0, 0.0).astype(bf16)
@@ -138,6 +147,13 @@
     grad_tokens[...] = tn(rows.astype(bf16), cols.astype(bf16)).astype(bf16)
 
 
+def total_kernel(keep, a, b, c, _, grad_in, grad_out):
+    total = keep[...] + a[...].astype(f32) + b[...].astype(f32) + c[...].astype(f32)
+    hidden = grad_in.shape[1]
+    grad_in[...] = total[:, :hidden]
+    grad_out[...] = total[:, hidden:]
+
+
 def per_device(tokens, cotangent, slot_params, in_weight, out_weight):
     tok, cot = tokens[0], cotangent[0]
     patch, width = tok.shape
@@ -147,7 +163,8 @@
     send, disp, comb = call(
         route_kernel,
         [((n2, width), bf16), ((EXPERTS, patch), f32), ((EXPERTS, patch), f32)],
-        10**7, 1500000, ins=3,
+        10**7, 1500000, "hhv",
+        [pltpu.VMEM((patch, width), bf16)] * 2 + [pltpu.SemaphoreType.DMA((2,))], 62_000_000,
     )(tok, cot, sp)
 
     def exchange(rows):
@@ -162,32 +179,36 @@
     part_own, part_other, c0, c1, c2, c3 = call(
         expert_kernel,
         [((n2, width), bf16), ((n2, width), bf16)] + [chunk_shape] * 4,
-        5 * 10**8, 4500000, scratch=[pltpu.VMEM((width, 128), bf16)], smem=1, ins=5,
+        5 * 10**8, 4500000, "svvvv", [pltpu.VMEM((width, 128), bf16)],
     )(place, own, other, in_weight, out_weight)
 
     back = lax.ppermute(part_other, "c", swap)
     got = [c0]
     for m, chunk in ((1, c1), (2, c2), (3, c3)):
         got.append(lax.ppermute(chunk, QUAD, [(i, i ^ m) for i in range(QUADS)]))
-    parts = exchange((part_own.astype(f32) + back.astype(f32)).astype(bf16))
+    returned = (part_own.astype(f32) + back.astype(f32)).astype(bf16)
+    parts = exchange(returned)
 
     depth = width // 16
     piece = ((depth, 2 * hidden), bf16)
     keep, s1, s2, s3 = call(
         term_kernel,
         [((depth, 2 * hidden), f32), piece, piece, piece],
-        4 * 10**8, 2500000, ins=4,
-    )(*got)
-    total = keep
-    for k, s in ((1, s1), (2, s2), (3, s3)):
-        total = total + lax.ppermute(s, "yh", [(i, (i + k) % 4) for i in range(4)]).astype(f32)
-
-    mixed, grad_tokens = call(
+        4 * 10**8, 2500000, "vvvva",
+    )(*got, returned)
+    shares = [
+        lax.ppermute(s, "yh", [(i, (i + k) % 4) for i in range(4)]) for k, s in ((2, s2), (1, s1), (3, s3))
+    ]
+
+    mixed, grad_tokens, done = call(
         finish_kernel,
-        [((patch, width), bf16), ((patch, width), bf16)],
-        3 * 10**7, 3000000, ins=6,
+        [((patch, width), bf16), ((patch, width), bf16), ((8, 128), f32)],
+        3 * 10**7, 3000000, "vvvvvv",
     )(tok, cot, sp, parts, disp, comb)
-    return mixed[None], grad_tokens[None], total[:, :hidden], total[:, hidden:]
+    grad_in, grad_out = call(
+        total_kernel, [((depth, hidden), f32)] * 2, 10**6, 1500000, "vvvva",
+    )(keep, *shares, done)
+    return mixed[None], grad_tokens[None], grad_in, grad_out
 
 
 def solution(mesh):

time: 113 us -> 109 us (0.965)
  the two profiles are of different devices: /device:TPU:8 before, /device:TPU:1 now
where the time goes in v2:
time: 109 us
  blocking collectives  39.5 us (36%)
  starting transfers between devices  34.7 us (32%)
  waiting for transfers between devices  20.4 us (19%)
  Pallas kernels  9.9 us (9%)
  local copies, waits for them, and re-layouts  3.31 us (3%)
    all_to_all x1, blocking collectives, exchange(): lax.all_to_all(rows.reshape(CHIP_COUNT, 2, width), CHIPS, 0, 0, tiled=True)  39.5 us
    ppermute x3, starting transfers between devices, per_device(): lax.ppermute(s, 'yh', [(i, (i + k) % 4) for i in range(4)])  14.9 us
    ppermute x3, waiting for transfers between devices, per_device(): lax.ppermute(s, 'yh', [(i, (i + k) % 4) for i in range(4)])  9.79 us
    ppermute x3, waiting for transfers between devices, per_device(): got.append(lax.ppermute(chunk, QUAD, [(i, i ^ m) for i in range(QUADS)]))  8.72 us
    ppermute x3, starting transfers between devices, per_device(): got.append(lax.ppermute(chunk, QUAD, [(i, i ^ m) for i in range(QUADS)]))  8.37 us
    ppermute x1, starting transfers between devices, per_device(): other = lax.ppermute(own, 'c', swap)  5.15 us
    pallas_call x1, Pallas kernels, per_device(): call(route_kernel, [((n2, width), bf16), ((EXPERTS, patch), f32), ((EXPER...  3.91 us
    all_to_all x1, starting transfers between devices, exchange(): lax.all_to_all(rows.reshape(CHIP_COUNT, 2, width), CHIPS, 0, 0, tiled=True)  3.86 us
  transfers between devices with their start and end apart: 9, of which 7 were waited for; matrix products, arithmetic and copies ran while one was open for 0% of the time, Pallas kernels for 2%

profile of v2, /device:TPU:1, one launch (start us, length us, event | category | flops | bytes accessed | tf_op | source)
XLA Modules:
  0.0 108.8 jit_solution(1333814889609924814)
XLA Ops:
  0.6 0.0 copy-start.2
  0.6 3.9 %shard_map.84 = (bf16[64,1280]{1,0:T(8,128)(2,1)}, f32[8,256]{1,0:T(8,128)}, f32[8,256]{1,0:T(8,128)}) custom-call(bf16[256,1280]{1,0:T(8,128)(2,1)} %bitcast.7, bf16[256,1280]{1,0:T(8,128)(2,1)} %bitcast.9, bf16[8,1280]{1,0:T(8,128)(2,1)} %bitcast.11), custom_call_target="tpu_custom_call" | custom-call | flops 10000000 | bytes 1500000 | tf_op jit(solution)/shard_map/pallas_call | solution.py:163
  4.6 1.0 reshape.20
  5.5 39.5 %all_to_all.10 = bf16[32,2,1280]{2,1,0:T(2,128)(2,1)S(1)} all-to-all(bf16[32,2,1280]{2,1,0:T(2,128)(2,1)S(1)} %reshape.20), channel_id=1, replica_groups=mesh['yh'=4,'yl'=2,'xl'=2,'xh'=2,'zh'=4,'zl'=4,'c'=2] {'xh','zh','zl'}, dimensions={0} | all-to-all | bytes 327680 | tf_op jit(solution)/shard_map/all_to_all | solution.py:171
  45.1 0.1 reshape.21.own
  45.1 5.2 %collective-permute-start = (bf16[64,1280]{1,0:T(8,128)(2,1)S(1)}, bf16[64,1280]{1,0:T(8,128)(2,1)S(1)}, u32[]{:S(2)}, u32[]{:S(2)}) collective-permute-start(bf16[64,1280]{1,0:T(8,128)(2,1)S(1)} %reshape.21.own), channel_id=1, source_target_pairs={{0,1},{1,0},{2,3},{3,2},{4,5},{5,4},{6,7},{7,6},{8,9},{9,8},{10,11... | collective-permute-start | bytes 491528 | tf_op jit(solution)/shard_map/ppermute | solution.py:176
  50.3 0.1 pad_add_fusion.place
  50.4 0.9 collective-permute-done.other
  51.3 0.0 copy-done.2
  51.3 0.0 copy-start.3
  51.3 1.4 %copy-done.3 = bf16[1280,640]{1,0:T(8,128)(2,1)S(1)} copy-done((bf16[1280,640]{1,0:T(8,128)(2,1)S(1)}, bf16[1280,640]{1,0:T(8,128)(2,1)}, u32[]{:S(2)}) %copy-start.3) | copy-done | bytes 1638424
  52.7 2.6 %shard_map.85 = (bf16[64,1280]{1,0:T(8,128)(2,1)S(1)}, bf16[64,1280]{1,0:T(8,128)(2,1)S(1)}, bf16[192,640]{1,0:T(8,128)(2,1)S(1)}, bf16[192,640]{1,0:T(8,128)(2,...) custom-call(s32[2]{0:T(128)S(1)} %pad_add_fusion.place, bf16[64,1280]{1,0:T(8,128)(2,1)S(1)} %reshape.21.own, ...), custom_call_target="tpu_custom_call" | custom-call | flops 500000000 | bytes 4500000 | tf_op jit(solution)/shard_map/pallas_call | solution.py:179
  55.3 0.0 copy-start
  55.3 0.0 copy-start.1
  55.3 0.0 copy-start.4
  55.3 0.0 copy-start.5
  55.4 0.0 copy-start.6
  55.4 2.4 %collective-permute-start.1 = (bf16[64,1280]{1,0:T(8,128)(2,1)S(1)}, bf16[64,1280]{1,0:T(8,128)(2,1)S(1)}, u32[]{:S(2)}, u32[]{:S(2)}) collective-permute-start(bf16[64,1280]{1,0:T(8,128)(2,1)S(1)} %get-tuple-element.24), channel_id=1, source_target_pairs={{0,1},{1,0},{2,3},{3,2},{4,5},{5,4},{6,7},{7,6},{8,9},{9,8},{10,11... | collective-permute-start | bytes 491528 | tf_op jit(solution)/shard_map/ppermute | solution.py:185
  57.8 1.0 collective-permute-done.1
  58.8 0.7 reshape.22
  59.6 3.9 %all-to-all-start.1 = ((bf16[32,2,1280]{2,1,0:T(2,128)(2,1)}), bf16[32,2,1280]{2,1,0:T(2,128)(2,1)S(1)}, u32[]{:S(2)}, u32[]{:S(2)}) async-start(bf16[32,2,1280]{2,1,0:T(2,128)(2,1)} %reshape.22), calls=%async_computation.1 | async-start | bytes 327680 | tf_op jit(solution)/shard_map/all_to_all | solution.py:171
  63.4 2.2 %collective-permute-start.2 = (bf16[192,640]{1,0:T(8,128)(2,1)S(1)}, bf16[192,640]{1,0:T(8,128)(2,1)S(1)}, u32[]{:S(2)}, u32[]{:S(2)}) collective-permute-start(bf16[192,640]{1,0:T(8,128)(2,1)S(1)} %get-tuple-element.30), channel_id=1, source_target_pairs={{0,64},{64,0},{128,192},{192,128},{1,65},{65,1},{129,193},{193,129... | collective-permute-start | bytes 737288 | tf_op jit(solution)/shard_map/ppermute | solution.py:188
  65.7 3.2 %collective-permute-start.3 = (bf16[192,640]{1,0:T(8,128)(2,1)S(1)}, bf16[192,640]{1,0:T(8,128)(2,1)S(1)}, u32[]{:S(2)}, u32[]{:S(2)}) collective-permute-start(bf16[192,640]{1,0:T(8,128)(2,1)S(1)} %get-tuple-element.31), channel_id=1, source_target_pairs={{0,128},{64,192},{128,0},{192,64},{1,129},{65,193},{129,1},{193,65... | collective-permute-start | bytes 737288 | tf_op jit(solution)/shard_map/ppermute | solution.py:188
  68.9 2.9 %collective-permute-start.4 = (bf16[192,640]{1,0:T(8,128)(2,1)S(1)}, bf16[192,640]{1,0:T(8,128)(2,1)S(1)}, u32[]{:S(2)}, u32[]{:S(2)}) collective-permute-start(bf16[192,640]{1,0:T(8,128)(2,1)S(1)} %get-tuple-element.32), channel_id=1, source_target_pairs={{0,192},{64,128},{128,64},{192,0},{1,193},{65,129},{129,65},{193,1... | collective-permute-start | bytes 737288 | tf_op jit(solution)/shard_map/ppermute | solution.py:188
  71.8 1.8 %collective-permute-done.2.c1 = bf16[192,640]{1,0:T(8,128)(2,1)S(1)} collective-permute-done((bf16[192,640]{1,0:T(8,128)(2,1)S(1)}, bf16[192,640]{1,0:T(8,128)(2,1)S(1)}, u32[]{:S(2)}, u32[]{:S(2)}) %collective-permute-start.2) | collective-permute-done | bytes 245792 | tf_op jit(solution)/shard_map/ppermute | solution.py:188
  73.7 0.8 collective-permute-done.3.c2
  74.4 6.1 %collective-permute-done.4.c3 = bf16[192,640]{1,0:T(8,128)(2,1)S(1)} collective-permute-done((bf16[192,640]{1,0:T(8,128)(2,1)S(1)}, bf16[192,640]{1,0:T(8,128)(2,1)S(1)}, u32[]{:S(2)}, u32[]{:S(2)}) %collective-permute-start.4) | collective-permute-done | bytes 245792 | tf_op jit(solution)/shard_map/ppermute | solution.py:188
  80.6 0.6 shard_map.87
  81.1 7.5 %collective-permute-start.5 = (bf16[80,1280]{1,0:T(8,128)(2,1)S(1)}, bf16[80,1280]{1,0:T(8,128)(2,1)S(1)}, u32[]{:S(2)}, u32[]{:S(2)}) collective-permute-start(bf16[80,1280]{1,0:T(8,128)(2,1)S(1)} %get-tuple-element.34), channel_id=1, source_target_pairs={{0,512},{256,768},{512,0},{768,256},{1,513},{257,769},{513,1},{769... | collective-permute-start | bytes 614408 | tf_op jit(solution)/shard_map/ppermute | solution.py:200
  88.6 2.4 %collective-permute-start.6 = (bf16[80,1280]{1,0:T(8,128)(2,1)S(1)}, bf16[80,1280]{1,0:T(8,128)(2,1)S(1)}, u32[]{:S(2)}, u32[]{:S(2)}) collective-permute-start(bf16[80,1280]{1,0:T(8,128)(2,1)S(1)} %get-tuple-element.35), channel_id=1, source_target_pairs={{0,256},{256,512},{512,768},{768,0},{1,257},{257,513},{513,769},{7... | collective-permute-start | bytes 614408 | tf_op jit(solution)/shard_map/ppermute | solution.py:200
  91.0 5.0 %collective-permute-start.7 = (bf16[80,1280]{1,0:T(8,128)(2,1)S(1)}, bf16[80,1280]{1,0:T(8,128)(2,1)S(1)}, u32[]{:S(2)}, u32[]{:S(2)}) collective-permute-start(bf16[80,1280]{1,0:T(8,128)(2,1)S(1)} %get-tuple-element.36), channel_id=1, source_target_pairs={{0,768},{256,0},{512,256},{768,512},{1,769},{257,1},{513,257},{769... | collective-permute-start | bytes 614408 | tf_op jit(solution)/shard_map/ppermute | solution.py:200
  96.0 0.0 all-to-all-done.1
  96.0 0.1 reshape.23.parts
  96.1 0.0 copy-done
  96.1 0.0 copy-done.1
  96.1 0.0 copy-done.4
  96.1 0.0 copy-done.5
  96.2 0.0 copy-done.6
  96.2 2.0 %shard_map.86 = (bf16[256,1280]{1,0:T(8,128)(2,1)}, bf16[256,1280]{1,0:T(8,128)(2,1)}, f32[8,128]{1,0:T(8,128)S(1)}) custom-call(bf16[256,1280]{1,0:T(8,128)(2,1)S(1)} %bitcast.8, bf16[256,1280]{1,0:T(8,128)(2,1)S(1)} %bitcast.10, bf16[8,1280]{1,0:T(8,128)(2,1)S(1)} %bitcast.12, bf16[64,1280]{1,0:T(8,128)(2,1)S(1)} %reshape.23.parts, ...), custom_call_target="tpu_custom_call" | custom-call | flops 30000000 | bytes 3000000 | tf_op jit(solution)/shard_map/pallas_call | solution.py:203
  98.2 0.0 collective-permute-done.5.a
  98.2 4.8 %collective-permute-done.6.b = bf16[80,1280]{1,0:T(8,128)(2,1)S(1)} collective-permute-done((bf16[80,1280]{1,0:T(8,128)(2,1)S(1)}, bf16[80,1280]{1,0:T(8,128)(2,1)S(1)}, u32[]{:S(2)}, u32[]{:S(2)}) %collective-permute-start.6) | collective-permute-done | bytes 204832 | tf_op jit(solution)/shard_map/ppermute | solution.py:200
  103.0 5.0 %collective-permute-done.7.c = bf16[80,1280]{1,0:T(8,128)(2,1)S(1)} collective-permute-done((bf16[80,1280]{1,0:T(8,128)(2,1)S(1)}, bf16[80,1280]{1,0:T(8,128)(2,1)S(1)}, u32[]{:S(2)}, u32[]{:S(2)}) %collective-permute-start.7) | collective-permute-done | bytes 204832 | tf_op jit(solution)/shard_map/ppermute | solution.py:200
  108.0 0.8 shard_map.88
  (1 shorter events, 0.0 us)
Async XLA Ops:
  0.6 50.7 %copy-start.2 = (bf16[1280,640]{1,0:T(8,128)(2,1)S(1)}, bf16[1280,640]{1,0:T(8,128)(2,1)}, u32[]{:S(2)}) copy-start(bf16[1280,640]{1,0:T(8,128)(2,1)} %w_in.1) | copy-start | bytes 4915204
  45.1 6.2 %collective-permute-start = (bf16[64,1280]{1,0:T(8,128)(2,1)S(1)}, bf16[64,1280]{1,0:T(8,128)(2,1)S(1)}, u32[]{:S(2)}, u32[]{:S(2)}) collective-permute-start(bf16[64,1280]{1,0:T(8,128)(2,1)S(1)} %reshape.21.own), channel_id=1, source_target_pairs={{0,1},{1,0},{2,3},{3,2},{4,5},{5,4},{6,7},{7,6},{8,9},{9,8},{10,11... | collective-permute-start | bytes 491528 | tf_op jit(solution)/shard_map/ppermute | solution.py:176
  51.3 1.4 %copy-start.3 = (bf16[1280,640]{1,0:T(8,128)(2,1)S(1)}, bf16[1280,640]{1,0:T(8,128)(2,1)}, u32[]{:S(2)}) copy-start(bf16[1280,640]{1,0:T(8,128)(2,1)} %w_out.1) | copy-start | bytes 4915204
  55.3 40.8 %copy-start = (bf16[1,256,1280]{2,1,0:T(8,128)(2,1)S(1)}, bf16[1,256,1280]{2,1,0:T(8,128)(2,1)}, u32[]{:S(2)}) copy-start(bf16[1,256,1280]{2,1,0:T(8,128)(2,1)} %param.5) | copy-start | bytes 1966084
  55.3 40.8 %copy-start.1 = (bf16[1,256,1280]{2,1,0:T(8,128)(2,1)S(1)}, bf16[1,256,1280]{2,1,0:T(8,128)(2,1)}, u32[]{:S(2)}) copy-start(bf16[1,256,1280]{2,1,0:T(8,128)(2,1)} %param.6) | copy-start | bytes 1966084
  55.3 40.8 %copy-start.4 = (bf16[1280,8]{0,1:T(8,128)(2,1)S(1)}, bf16[1280,8]{0,1:T(8,128)(2,1)}, u32[]{:S(2)}) copy-start(bf16[1280,8]{0,1:T(8,128)(2,1)} %param.7) | copy-start | bytes 61444
  55.3 40.8 %copy-start.5 = (f32[8,256]{1,0:T(8,128)S(1)}, f32[8,256]{1,0:T(8,128)}, u32[]{:S(2)}) copy-start(f32[8,256]{1,0:T(8,128)} %get-tuple-element.25.disp) | copy-start | bytes 24580
  55.4 40.8 %copy-start.6 = (f32[8,256]{1,0:T(8,128)S(1)}, f32[8,256]{1,0:T(8,128)}, u32[]{:S(2)}) copy-start(f32[8,256]{1,0:T(8,128)} %get-tuple-element.26.comb) | copy-start | bytes 24580
  55.4 3.4 %collective-permute-start.1 = (bf16[64,1280]{1,0:T(8,128)(2,1)S(1)}, bf16[64,1280]{1,0:T(8,128)(2,1)S(1)}, u32[]{:S(2)}, u32[]{:S(2)}) collective-permute-start(bf16[64,1280]{1,0:T(8,128)(2,1)S(1)} %get-tuple-element.24), channel_id=1, source_target_pairs={{0,1},{1,0},{2,3},{3,2},{4,5},{5,4},{6,7},{7,6},{8,9},{9,8},{10,11... | collective-permute-start | bytes 491528 | tf_op jit(solution)/shard_map/ppermute | solution.py:185
  59.6 36.5 %all-to-all-start.1 = ((bf16[32,2,1280]{2,1,0:T(2,128)(2,1)}), bf16[32,2,1280]{2,1,0:T(2,128)(2,1)S(1)}, u32[]{:S(2)}, u32[]{:S(2)}) async-start(bf16[32,2,1280]{2,1,0:T(2,128)(2,1)} %reshape.22), calls=%async_computation.1 | async-start | bytes 327680 | tf_op jit(solution)/shard_map/all_to_all | solution.py:171
  63.4 10.2 %collective-permute-start.2 = (bf16[192,640]{1,0:T(8,128)(2,1)S(1)}, bf16[192,640]{1,0:T(8,128)(2,1)S(1)}, u32[]{:S(2)}, u32[]{:S(2)}) collective-permute-start(bf16[192,640]{1,0:T(8,128)(2,1)S(1)} %get-tuple-element.30), channel_id=1, source_target_pairs={{0,64},{64,0},{128,192},{192,128},{1,65},{65,1},{129,193},{193,129... | collective-permute-start | bytes 737288 | tf_op jit(solution)/shard_map/ppermute | solution.py:188
  65.7 8.8 %collective-permute-start.3 = (bf16[192,640]{1,0:T(8,128)(2,1)S(1)}, bf16[192,640]{1,0:T(8,128)(2,1)S(1)}, u32[]{:S(2)}, u32[]{:S(2)}) collective-permute-start(bf16[192,640]{1,0:T(8,128)(2,1)S(1)} %get-tuple-element.31), channel_id=1, source_target_pairs={{0,128},{64,192},{128,0},{192,64},{1,129},{65,193},{129,1},{193,65... | collective-permute-start | bytes 737288 | tf_op jit(solution)/shard_map/ppermute | solution.py:188
  68.9 11.7 %collective-permute-start.4 = (bf16[192,640]{1,0:T(8,128)(2,1)S(1)}, bf16[192,640]{1,0:T(8,128)(2,1)S(1)}, u32[]{:S(2)}, u32[]{:S(2)}) collective-permute-start(bf16[192,640]{1,0:T(8,128)(2,1)S(1)} %get-tuple-element.32), channel_id=1, source_target_pairs={{0,192},{64,128},{128,64},{192,0},{1,193},{65,129},{129,65},{193,1... | collective-permute-start | bytes 737288 | tf_op jit(solution)/shard_map/ppermute | solution.py:188
  81.1 17.1 %collective-permute-start.5 = (bf16[80,1280]{1,0:T(8,128)(2,1)S(1)}, bf16[80,1280]{1,0:T(8,128)(2,1)S(1)}, u32[]{:S(2)}, u32[]{:S(2)}) collective-permute-start(bf16[80,1280]{1,0:T(8,128)(2,1)S(1)} %get-tuple-element.34), channel_id=1, source_target_pairs={{0,512},{256,768},{512,0},{768,256},{1,513},{257,769},{513,1},{769... | collective-permute-start | bytes 614408 | tf_op jit(solution)/shard_map/ppermute | solution.py:200
  88.6 14.4 %collective-permute-start.6 = (bf16[80,1280]{1,0:T(8,128)(2,1)S(1)}, bf16[80,1280]{1,0:T(8,128)(2,1)S(1)}, u32[]{:S(2)}, u32[]{:S(2)}) collective-permute-start(bf16[80,1280]{1,0:T(8,128)(2,1)S(1)} %get-tuple-element.35), channel_id=1, source_target_pairs={{0,256},{256,512},{512,768},{768,0},{1,257},{257,513},{513,769},{7... | collective-permute-start | bytes 614408 | tf_op jit(solution)/shard_map/ppermute | solution.py:200
  91.0 17.0 %collective-permute-start.7 = (bf16[80,1280]{1,0:T(8,128)(2,1)S(1)}, bf16[80,1280]{1,0:T(8,128)(2,1)S(1)}, u32[]{:S(2)}, u32[]{:S(2)}) collective-permute-start(bf16[80,1280]{1,0:T(8,128)(2,1)S(1)} %get-tuple-element.36), channel_id=1, source_target_pairs={{0,768},{256,0},{512,256},{768,512},{1,769},{257,1},{513,257},{769... | collective-permute-start | bytes 614408 | tf_op jit(solution)/shard_map/ppermute | solution.py:200

commit v3 on v2

--- a/solution.py
+++ b/solution.py
@@ -22,6 +22,7 @@
 QUAD = ("yl", "xl")
 EXPERTS, SPREAD, CHIP_COUNT = 8, 4, 32
 QUADS = 4
+PIECES = 4
 ROOM = 20_000_000
 
 
@@ -60,11 +61,15 @@
 
 
 def route_kernel(tok_hbm, cot_hbm, sp, send, disp, comb, tok, cot, sems):
-    copy_tok = pltpu.make_async_copy(tok_hbm, tok, sems.at[0])
-    copy_cot = pltpu.make_async_copy(cot_hbm, cot, sems.at[1])
-    copy_tok.start()
-    copy_cot.start()
-    copy_tok.wait()
+    step = tok.shape[0] // PIECES
+    copies = []
+    for i, (src, dst) in enumerate(((tok_hbm, tok), (cot_hbm, cot))):
+        for p in range(PIECES):
+            rows = pl.ds(p * step, step)
+            copies.append(pltpu.make_async_copy(src.at[rows], dst.at[rows], sems.at[i, p]))
+            copies[-1].start()
+    for copy in copies[:PIECES]:
+        copy.wait()
     logits = nt(sp[...], tok[...])
     ed = jnp.exp(logits - jnp.max(logits, axis=1, keepdims=True))
     d = ed / jnp.sum(ed, axis=1, keepdims=True)
@@ -73,7 +78,8 @@
     disp[...] = d
     comb[...] = c
     slot_in = nn(d.astype(bf16), tok[...]).astype(bf16)
-    copy_cot.wait()
+    for copy in copies[PIECES:]:
+        copy.wait()
     slot_grad = nn(c.astype(bf16), cot[...]).astype(bf16)
     both = jnp.concatenate([slot_in.astype(f32), slot_grad.astype(f32)], axis=0).astype(bf16)
     rows = 2 * CHIP_COUNT
@@ -99,7 +105,7 @@
     part_other[...] = (tn(even, out_part[n:]) + tn(odd, grad_part[n:])).astype(bf16)
     both = jnp.concatenate([rows_in, rows_grad], axis=0)
     turned[...] = jnp.transpose(both.astype(f32)).astype(bf16)
-    yh, j0 = place[0], place[1]
+    j0 = place[0]
     depth = turned.shape[0] // 16
     for m, chunk in enumerate((c0, c1, c2, c3)):
         chunk[0 : 2 * n, :] = gp
@@ -107,14 +113,14 @@
         j = jnp.bitwise_xor(j0, m)
         pieces = []
         for k in range(4):
-            at = (lax.rem(yh + k, 4) * QUADS + j) * depth
+            at = (k * QUADS + j) * depth
             pieces.append(turned[pl.ds(pl.multiple_of(at, 16), depth), :])
         piece = jnp.concatenate(pieces, axis=0)
         for b in range(5):
             chunk[4 * n : 6 * n, 128 * b : 128 * (b + 1)] = piece[64 * b : 64 * (b + 1)]
 
 
-def term_kernel(c0, c1, c2, c3, _, keep, s1, s2, s3):
+def term_kernel(c0, c1, c2, c3, _, terms):
     left, right = [], []
     zero = jnp.zeros((64, 640), bf16)
     for chunk in (c0, c1, c2, c3):
@@ -122,10 +128,8 @@
         right.append(jnp.concatenate([chunk[0:64, :], zero], axis=1))
         right.append(jnp.concatenate([zero, chunk[64:128, :]], axis=1))
     total = nn(jnp.concatenate(left, axis=1), jnp.concatenate(right, axis=0))
-    depth = keep.shape[0]
-    keep[...] = total[:depth]
-    for k, s in enumerate((s1, s2, s3)):
-        s[...] = total[(k + 1) * depth : (k + 2) * depth].astype(bf16)
+    for k in range(terms.shape[0]):
+        terms[k] = total[k * terms.shape[1] : (k + 1) * terms.shape[1]].astype(bf16)
 
 
 def finish_kernel(tok, cot, sp, parts, disp, comb, mixed, grad_tokens, done):
@@ -147,8 +151,10 @@
     grad_tokens[...] = tn(rows.astype(bf16), cols.astype(bf16)).astype(bf16)
 
 
-def total_kernel(keep, a, b, c, _, grad_in, grad_out):
-    total = keep[...] + a[...].astype(f32) + b[...].astype(f32) + c[...].astype(f32)
+def total_kernel(terms, _, grad_in, grad_out):
+    total = terms[0].astype(f32)
+    for k in range(1, terms.shape[0]):
+        total = total + terms[k].astype(f32)
     hidden = grad_in.shape[1]
     grad_in[...] = total[:, :hidden]
     grad_out[...] = total[:, hidden:]
@@ -164,7 +170,7 @@
         route_kernel,
         [((n2, width), bf16), ((EXPERTS, patch), f32), ((EXPERTS, patch), f32)],
         10**7, 1500000, "hhv",
-        [pltpu.VMEM((patch, width), bf16)] * 2 + [pltpu.SemaphoreType.DMA((2,))], 62_000_000,
+        [pltpu.VMEM((patch, width), bf16)] * 2 + [pltpu.SemaphoreType.DMA((2, PIECES))], 56_000_000,
     )(tok, cot, sp)
 
     def exchange(rows):
@@ -174,7 +180,7 @@
     swap = [(0, 1), (1, 0)]
     own = exchange(send)
     other = lax.ppermute(own, "c", swap)
-    place = jnp.stack([lax.axis_index("yh"), lax.axis_index(QUAD)]).astype(jnp.int32)
+    place = lax.axis_index(QUAD).astype(jnp.int32).reshape(1)
     chunk_shape = ((192, hidden), bf16)
     part_own, part_other, c0, c1, c2, c3 = call(
         expert_kernel,
@@ -190,15 +196,10 @@
     parts = exchange(returned)
 
     depth = width // 16
-    piece = ((depth, 2 * hidden), bf16)
-    keep, s1, s2, s3 = call(
-        term_kernel,
-        [((depth, 2 * hidden), f32), piece, piece, piece],
-        4 * 10**8, 2500000, "vvvva",
+    (terms,) = call(
+        term_kernel, [((4, depth, 2 * hidden), bf16)], 4 * 10**8, 2500000, "vvvva",
     )(*got, returned)
-    shares = [
-        lax.ppermute(s, "yh", [(i, (i + k) % 4) for i in range(4)]) for k, s in ((2, s2), (1, s1), (3, s3))
-    ]
+    shares = lax.all_to_all(terms, "yh", 0, 0, tiled=True)
 
     mixed, grad_tokens, done = call(
         finish_kernel,
@@ -206,8 +207,8 @@
         3 * 10**7, 3000000, "vvvvvv",
     )(tok, cot, sp, parts, disp, comb)
     grad_in, grad_out = call(
-        total_kernel, [((depth, hidden), f32)] * 2, 10**6, 1500000, "vvvva",
-    )(keep, *shares, done)
+        total_kernel, [((depth, hidden), f32)] * 2, 10**6, 1500000, "va",
+    )(shares, done)
     return mixed[None], grad_tokens[None], grad_in, grad_out
 
 

time: 109 us -> 109 us (level)
  waiting for transfers between devices: 20.4 us -> 29.6 us
  starting transfers between devices: 34.7 us -> 26.5 us
    all_to_all x0 -> x1, waiting for transfers between devices: none -> 18.8 us  [per_device(): shares = lax.all_to_all(terms, 'yh', 0, 0, tiled=True)]
    ppermute x3 -> x0, starting transfers between devices: 14.9 us -> none  [per_device(): lax.ppermute(s, 'yh', [(i, (i + k) % 4) for i in range(4)])]
    ppermute x3 -> x0, waiting for transfers between devices: 9.79 us -> none  [per_device(): lax.ppermute(s, 'yh', [(i, (i + k) % 4) for i in range(4)])]
    all_to_all x0 -> x1, starting transfers between devices: none -> 6.82 us  [per_device(): shares = lax.all_to_all(terms, 'yh', 0, 0, tiled=True)]
    pallas_call x1, Pallas kernels: 3.91 us -> 2.51 us  [per_device(): call(route_kernel, [((n2, width), bf16), ((EXPERTS, patch), f32), ((EXPER...]
    unnamed x14 -> x12, local copies, waits for them, and re-layouts: 1.47 us -> 2.29 us
  transfers between devices with their start and end apart: 9 -> 7, of which waited for: 7 -> 6; matrix products, arithmetic and copies ran while one was open for 0% -> 0% of each run, Pallas kernels for 2% -> 3%
where the time goes in v3:
time: 109 us; the launch traced here: 108 us
  blocking collectives  39.5 us (36%)
  waiting for transfers between devices  29.6 us (27%)
  starting transfers between devices  26.5 us (24%)
  Pallas kernels  8.86 us (8%)
  local copies, waits for them, and re-layouts  3.21 us (3%)
    all_to_all x1, blocking collectives, exchange(): lax.all_to_all(rows.reshape(CHIP_COUNT, 2, width), CHIPS, 0, 0, tiled=True)  39.5 us
    all_to_all x1, waiting for transfers between devices, per_device(): shares = lax.all_to_all(terms, 'yh', 0, 0, tiled=True)  18.8 us
    ppermute x3, waiting for transfers between devices, per_device(): got.append(lax.ppermute(chunk, QUAD, [(i, i ^ m) for i in range(QUADS)]))  8.72 us
    ppermute x3, starting transfers between devices, per_device(): got.append(lax.ppermute(chunk, QUAD, [(i, i ^ m) for i in range(QUADS)]))  8.37 us
    all_to_all x1, starting transfers between devices, per_device(): shares = lax.all_to_all(terms, 'yh', 0, 0, tiled=True)  6.82 us
    ppermute x1, starting transfers between devices, per_device(): other = lax.ppermute(own, 'c', swap)  5.15 us
    all_to_all x1, starting transfers between devices, exchange(): lax.all_to_all(rows.reshape(CHIP_COUNT, 2, width), CHIPS, 0, 0, tiled=True)  3.87 us
    pallas_call x1, Pallas kernels, per_device(): call(route_kernel, [((n2, width), bf16), ((EXPERTS, patch), f32), ((EXPER...  2.51 us
  transfers between devices with their start and end apart: 7, of which 6 were waited for; matrix products, arithmetic and copies ran while one was open for 0% of the time, Pallas kernels for 3%

profile of v3, /device:TPU:1, one launch (start us, length us, event | category | flops | bytes accessed | tf_op | source)
XLA Modules:
  0.0 108.5 jit_solution(17126793983393680503)
XLA Ops:
  0.6 0.0 copy-start.2
  0.6 0.0 copy-start.4
  0.7 0.8 copy-done.4
  1.5 2.5 %shard_map.84 = (bf16[64,1280]{1,0:T(8,128)(2,1)S(1)}, f32[8,256]{1,0:T(8,128)S(1)}, f32[8,256]{1,0:T(8,128)S(1)}) custom-call(bf16[256,1280]{1,0:T(8,128)(2,1)} %bitcast.6, bf16[256,1280]{1,0:T(8,128)(2,1)} %bitcast.8, bf16[8,1280]{1,0:T(8,128)(2,1)S(1)} %bitcast.10), custom_call_target="tpu_custom_call" | custom-call | flops 10000000 | bytes 1500000 | tf_op jit(solution)/shard_map/pallas_call | solution.py:169
  4.0 0.1 reshape.24
  4.1 39.5 %all_to_all.15 = bf16[32,2,1280]{2,1,0:T(2,128)(2,1)S(1)} all-to-all(bf16[32,2,1280]{2,1,0:T(2,128)(2,1)S(1)} %reshape.24), channel_id=1, replica_groups=mesh['yh'=4,'yl'=2,'xl'=2,'xh'=2,'zh'=4,'zl'=4,'c'=2] {'xh','zh','zl'}, dimensions={0} | all-to-all | bytes 327680 | tf_op jit(solution)/shard_map/all_to_all | solution.py:177
  43.6 0.1 reshape.25.own
  43.7 5.2 %collective-permute-start = (bf16[64,1280]{1,0:T(8,128)(2,1)S(1)}, bf16[64,1280]{1,0:T(8,128)(2,1)S(1)}, u32[]{:S(2)}, u32[]{:S(2)}) collective-permute-start(bf16[64,1280]{1,0:T(8,128)(2,1)S(1)} %reshape.25.own), channel_id=1, source_target_pairs={{0,1},{1,0},{2,3},{3,2},{4,5},{5,4},{6,7},{7,6},{8,9},{9,8},{10,11... | collective-permute-start | bytes 491528 | tf_op jit(solution)/shard_map/ppermute | solution.py:182
  48.9 1.0 collective-permute-done.other
  49.9 0.0 copy-done.2
  49.9 0.0 copy-start.3
  49.9 1.4 %copy-done.3 = bf16[1280,640]{1,0:T(8,128)(2,1)S(1)} copy-done((bf16[1280,640]{1,0:T(8,128)(2,1)S(1)}, bf16[1280,640]{1,0:T(8,128)(2,1)}, u32[]{:S(2)}) %copy-start.3) | copy-done | bytes 1638424
  51.3 2.0 %shard_map.85 = (bf16[64,1280]{1,0:T(8,128)(2,1)S(1)}, bf16[64,1280]{1,0:T(8,128)(2,1)S(1)}, bf16[192,640]{1,0:T(8,128)(2,1)S(1)}, bf16[192,640]{1,0:T(8,128)(2,...) custom-call(s32[1]{0:T(128)} %bitcast.3.place, bf16[64,1280]{1,0:T(8,128)(2,1)S(1)} %reshape.25.own, ...), custom_call_target="tpu_custom_call" | custom-call | flops 500000000 | bytes 4500000 | tf_op jit(solution)/shard_map/pallas_call | solution.py:185
  53.3 2.3 %collective-permute-start.1 = (bf16[64,1280]{1,0:T(8,128)(2,1)S(1)}, bf16[64,1280]{1,0:T(8,128)(2,1)S(1)}, u32[]{:S(2)}, u32[]{:S(2)}) collective-permute-start(bf16[64,1280]{1,0:T(8,128)(2,1)S(1)} %get-tuple-element.20), channel_id=1, source_target_pairs={{0,1},{1,0},{2,3},{3,2},{4,5},{5,4},{6,7},{7,6},{8,9},{9,8},{10,11... | collective-permute-start | bytes 491528 | tf_op jit(solution)/shard_map/ppermute | solution.py:191
  55.6 1.0 collective-permute-done.1
  56.6 0.7 reshape.26
  57.4 3.9 %all-to-all-start.1 = ((bf16[32,2,1280]{2,1,0:T(2,128)(2,1)}), bf16[32,2,1280]{2,1,0:T(2,128)(2,1)S(1)}, u32[]{:S(2)}, u32[]{:S(2)}) async-start(bf16[32,2,1280]{2,1,0:T(2,128)(2,1)} %reshape.26), calls=%async_computation.1 | async-start | bytes 327680 | tf_op jit(solution)/shard_map/all_to_all | solution.py:177
  61.3 2.2 %collective-permute-start.2 = (bf16[192,640]{1,0:T(8,128)(2,1)S(1)}, bf16[192,640]{1,0:T(8,128)(2,1)S(1)}, u32[]{:S(2)}, u32[]{:S(2)}) collective-permute-start(bf16[192,640]{1,0:T(8,128)(2,1)S(1)} %get-tuple-element.26), channel_id=1, source_target_pairs={{0,64},{64,0},{128,192},{192,128},{1,65},{65,1},{129,193},{193,129... | collective-permute-start | bytes 737288 | tf_op jit(solution)/shard_map/ppermute | solution.py:194
  63.5 3.2 %collective-permute-start.3 = (bf16[192,640]{1,0:T(8,128)(2,1)S(1)}, bf16[192,640]{1,0:T(8,128)(2,1)S(1)}, u32[]{:S(2)}, u32[]{:S(2)}) collective-permute-start(bf16[192,640]{1,0:T(8,128)(2,1)S(1)} %get-tuple-element.27), channel_id=1, source_target_pairs={{0,128},{64,192},{128,0},{192,64},{1,129},{65,193},{129,1},{193,65... | collective-permute-start | bytes 737288 | tf_op jit(solution)/shard_map/ppermute | solution.py:194
  66.7 2.9 %collective-permute-start.4 = (bf16[192,640]{1,0:T(8,128)(2,1)S(1)}, bf16[192,640]{1,0:T(8,128)(2,1)S(1)}, u32[]{:S(2)}, u32[]{:S(2)}) collective-permute-start(bf16[192,640]{1,0:T(8,128)(2,1)S(1)} %get-tuple-element.28), channel_id=1, source_target_pairs={{0,192},{64,128},{128,64},{192,0},{1,193},{65,129},{129,65},{193,1... | collective-permute-start | bytes 737288 | tf_op jit(solution)/shard_map/ppermute | solution.py:194
  69.7 1.8 %collective-permute-done.2.c1 = bf16[192,640]{1,0:T(8,128)(2,1)S(1)} collective-permute-done((bf16[192,640]{1,0:T(8,128)(2,1)S(1)}, bf16[192,640]{1,0:T(8,128)(2,1)S(1)}, u32[]{:S(2)}, u32[]{:S(2)}) %collective-permute-start.2) | collective-permute-done | bytes 245792 | tf_op jit(solution)/shard_map/ppermute | solution.py:194
  71.5 0.8 collective-permute-done.3.c2
  72.2 6.1 %collective-permute-done.4.c3 = bf16[192,640]{1,0:T(8,128)(2,1)S(1)} collective-permute-done((bf16[192,640]{1,0:T(8,128)(2,1)S(1)}, bf16[192,640]{1,0:T(8,128)(2,1)S(1)}, u32[]{:S(2)}, u32[]{:S(2)}) %collective-permute-start.4) | collective-permute-done | bytes 245792 | tf_op jit(solution)/shard_map/ppermute | solution.py:194
  78.4 0.0 copy-start
  78.4 0.0 copy-start.1
  78.4 0.0 copy-start.5
  78.4 1.5 %shard_map.87 = bf16[4,80,1280]{2,1,0:T(8,128)(2,1)} custom-call(bf16[192,640]{1,0:T(8,128)(2,1)S(1)} %get-tuple-element.25.c0, bf16[192,640]{1,0:T(8,128)(2,1)S(1)} %collective-permute-done.2.c1, bf16[192,640]{1,0:T(8,128)(2,1)S(1)} %collective-permute-done.3.c2, bf16[192,640]{1,0:T(8,128)(2,1)S(1)} %collective-permute-done.4.c3, ...), custom_call_target="tpu_custom_call" | custom-call | flops 400000000 | bytes 2500000 | tf_op jit(solution)/shard_map/pallas_call | solution.py:199
  79.9 0.0 all-to-all-done.1
  79.9 6.8 %all-to-all-start.2 = ((bf16[4,80,1280]{2,1,0:T(8,128)(2,1)}), bf16[4,80,1280]{2,1,0:T(8,128)(2,1)S(1)}, u32[]{:S(2)}, u32[]{:S(2)}) async-start(bf16[4,80,1280]{2,1,0:T(8,128)(2,1)} %shard_map.87), calls=%async_computation.2 | async-start | bytes 1638400 | tf_op jit(solution)/shard_map/all_to_all | solution.py:202
  86.7 0.1 reshape.27.parts
  86.7 0.0 copy-done
  86.8 0.0 copy-done.1
  86.8 0.0 copy-done.5
  86.8 2.0 %shard_map.86 = (bf16[256,1280]{1,0:T(8,128)(2,1)}, bf16[256,1280]{1,0:T(8,128)(2,1)}, f32[8,128]{1,0:T(8,128)S(1)}) custom-call(bf16[256,1280]{1,0:T(8,128)(2,1)S(1)} %bitcast.7, bf16[256,1280]{1,0:T(8,128)(2,1)S(1)} %bitcast.9, bf16[8,1280]{1,0:T(8,128)(2,1)S(1)} %bitcast.11, bf16[64,1280]{1,0:T(8,128)(2,1)S(1)} %reshape.27.parts, ...), custom_call_target="tpu_custom_call" | custom-call | flops 30000000 | bytes 3000000 | tf_op jit(solution)/shard_map/pallas_call | solution.py:204
  88.8 18.8 %all-to-all-done.2.terms = bf16[4,80,1280]{2,1,0:T(8,128)(2,1)S(1)} async-done(((bf16[4,80,1280]{2,1,0:T(8,128)(2,1)}), bf16[4,80,1280]{2,1,0:T(8,128)(2,1)S(1)}, u32[]{:S(2)}, u32[]{:S(2)}) %all-to-all-start.2) | async-done | bytes 819232 | tf_op jit(solution)/shard_map/all_to_all | solution.py:202
  107.7 0.8 shard_map.88
  (1 shorter events, 0.0 us)
Async XLA Ops:
  0.6 49.2 %copy-start.2 = (bf16[1280,640]{1,0:T(8,128)(2,1)S(1)}, bf16[1280,640]{1,0:T(8,128)(2,1)}, u32[]{:S(2)}) copy-start(bf16[1280,640]{1,0:T(8,128)(2,1)} %w_in.1) | copy-start | bytes 4915204
  0.6 0.9 copy-start.4
  43.7 6.2 %collective-permute-start = (bf16[64,1280]{1,0:T(8,128)(2,1)S(1)}, bf16[64,1280]{1,0:T(8,128)(2,1)S(1)}, u32[]{:S(2)}, u32[]{:S(2)}) collective-permute-start(bf16[64,1280]{1,0:T(8,128)(2,1)S(1)} %reshape.25.own), channel_id=1, source_target_pairs={{0,1},{1,0},{2,3},{3,2},{4,5},{5,4},{6,7},{7,6},{8,9},{9,8},{10,11... | collective-permute-start | bytes 491528 | tf_op jit(solution)/shard_map/ppermute | solution.py:182
  49.9 1.4 %copy-start.3 = (bf16[1280,640]{1,0:T(8,128)(2,1)S(1)}, bf16[1280,640]{1,0:T(8,128)(2,1)}, u32[]{:S(2)}) copy-start(bf16[1280,640]{1,0:T(8,128)(2,1)} %w_out.1) | copy-start | bytes 4915204
  53.3 3.3 %collective-permute-start.1 = (bf16[64,1280]{1,0:T(8,128)(2,1)S(1)}, bf16[64,1280]{1,0:T(8,128)(2,1)S(1)}, u32[]{:S(2)}, u32[]{:S(2)}) collective-permute-start(bf16[64,1280]{1,0:T(8,128)(2,1)S(1)} %get-tuple-element.20), channel_id=1, source_target_pairs={{0,1},{1,0},{2,3},{3,2},{4,5},{5,4},{6,7},{7,6},{8,9},{9,8},{10,11... | collective-permute-start | bytes 491528 | tf_op jit(solution)/shard_map/ppermute | solution.py:191
  57.4 22.5 %all-to-all-start.1 = ((bf16[32,2,1280]{2,1,0:T(2,128)(2,1)}), bf16[32,2,1280]{2,1,0:T(2,128)(2,1)S(1)}, u32[]{:S(2)}, u32[]{:S(2)}) async-start(bf16[32,2,1280]{2,1,0:T(2,128)(2,1)} %reshape.26), calls=%async_computation.1 | async-start | bytes 327680 | tf_op jit(solution)/shard_map/all_to_all | solution.py:177
  61.3 10.2 %collective-permute-start.2 = (bf16[192,640]{1,0:T(8,128)(2,1)S(1)}, bf16[192,640]{1,0:T(8,128)(2,1)S(1)}, u32[]{:S(2)}, u32[]{:S(2)}) collective-permute-start(bf16[192,640]{1,0:T(8,128)(2,1)S(1)} %get-tuple-element.26), channel_id=1, source_target_pairs={{0,64},{64,0},{128,192},{192,128},{1,65},{65,1},{129,193},{193,129... | collective-permute-start | bytes 737288 | tf_op jit(solution)/shard_map/ppermute | solution.py:194
  63.5 8.8 %collective-permute-start.3 = (bf16[192,640]{1,0:T(8,128)(2,1)S(1)}, bf16[192,640]{1,0:T(8,128)(2,1)S(1)}, u32[]{:S(2)}, u32[]{:S(2)}) collective-permute-start(bf16[192,640]{1,0:T(8,128)(2,1)S(1)} %get-tuple-element.27), channel_id=1, source_target_pairs={{0,128},{64,192},{128,0},{192,64},{1,129},{65,193},{129,1},{193,65... | collective-permute-start | bytes 737288 | tf_op jit(solution)/shard_map/ppermute | solution.py:194
  66.7 11.7 %collective-permute-start.4 = (bf16[192,640]{1,0:T(8,128)(2,1)S(1)}, bf16[192,640]{1,0:T(8,128)(2,1)S(1)}, u32[]{:S(2)}, u32[]{:S(2)}) collective-permute-start(bf16[192,640]{1,0:T(8,128)(2,1)S(1)} %get-tuple-element.28), channel_id=1, source_target_pairs={{0,192},{64,128},{128,64},{192,0},{1,193},{65,129},{129,65},{193,1... | collective-permute-start | bytes 737288 | tf_op jit(solution)/shard_map/ppermute | solution.py:194
  78.4 8.4 %copy-start = (bf16[1,256,1280]{2,1,0:T(8,128)(2,1)S(1)}, bf16[1,256,1280]{2,1,0:T(8,128)(2,1)}, u32[]{:S(2)}) copy-start(bf16[1,256,1280]{2,1,0:T(8,128)(2,1)} %param.5) | copy-start | bytes 1966084
  78.4 8.4 %copy-start.1 = (bf16[1,256,1280]{2,1,0:T(8,128)(2,1)S(1)}, bf16[1,256,1280]{2,1,0:T(8,128)(2,1)}, u32[]{:S(2)}) copy-start(bf16[1,256,1280]{2,1,0:T(8,128)(2,1)} %param.6) | copy-start | bytes 1966084
  78.4 8.4 %copy-start.5 = (bf16[1280,8]{0,1:T(8,128)(2,1)S(1)}, bf16[1280,8]{0,1:T(8,128)(2,1)}, u32[]{:S(2)}) copy-start(bf16[1280,8]{0,1:T(8,128)(2,1)} %param.7) | copy-start | bytes 61444
  79.9 27.8 %all-to-all-start.2 = ((bf16[4,80,1280]{2,1,0:T(8,128)(2,1)}), bf16[4,80,1280]{2,1,0:T(8,128)(2,1)S(1)}, u32[]{:S(2)}, u32[]{:S(2)}) async-start(bf16[4,80,1280]{2,1,0:T(8,128)(2,1)} %shard_map.87), calls=%async_computation.2 | async-start | bytes 1638400 | tf_op jit(solution)/shard_map/all_to_all | solution.py:202

commit v4 on v2

--- a/solution.py
+++ b/solution.py
@@ -22,6 +22,7 @@
 QUAD = ("yl", "xl")
 EXPERTS, SPREAD, CHIP_COUNT = 8, 4, 32
 QUADS = 4
+PIECES = 4
 ROOM = 20_000_000
 
 
@@ -60,11 +61,15 @@
 
 
 def route_kernel(tok_hbm, cot_hbm, sp, send, disp, comb, tok, cot, sems):
-    copy_tok = pltpu.make_async_copy(tok_hbm, tok, sems.at[0])
-    copy_cot = pltpu.make_async_copy(cot_hbm, cot, sems.at[1])
-    copy_tok.start()
-    copy_cot.start()
-    copy_tok.wait()
+    step = tok.shape[0] // PIECES
+    copies = []
+    for i, (src, dst) in enumerate(((tok_hbm, tok), (cot_hbm, cot))):
+        for p in range(PIECES):
+            rows = pl.ds(p * step, step)
+            copies.append(pltpu.make_async_copy(src.at[rows], dst.at[rows], sems.at[i, p]))
+            copies[-1].start()
+    for copy in copies[:PIECES]:
+        copy.wait()
     logits = nt(sp[...], tok[...])
     ed = jnp.exp(logits - jnp.max(logits, axis=1, keepdims=True))
     d = ed / jnp.sum(ed, axis=1, keepdims=True)
@@ -73,7 +78,8 @@
     disp[...] = d
     comb[...] = c
     slot_in = nn(d.astype(bf16), tok[...]).astype(bf16)
-    copy_cot.wait()
+    for copy in copies[PIECES:]:
+        copy.wait()
     slot_grad = nn(c.astype(bf16), cot[...]).astype(bf16)
     both = jnp.concatenate([slot_in.astype(f32), slot_grad.astype(f32)], axis=0).astype(bf16)
     rows = 2 * CHIP_COUNT
@@ -81,13 +87,21 @@
     send[...] = nn(sel, both).astype(bf16)
 
 
-def expert_kernel(place, own, other, w_in, w_out, part_own, part_other, c0, c1, c2, c3, turned):
+def expert_kernel(place, own, other, w_in, w_out_hbm, part_own, part_other, c0, c1, c2, c3, turned, w_out, sems):
+    step = w_out.shape[0] // PIECES
+    copies = []
+    for p in range(PIECES):
+        rows = pl.ds(p * step, step)
+        copies.append(pltpu.make_async_copy(w_out_hbm.at[rows], w_out.at[rows], sems.at[p]))
+        copies[-1].start()
     n = own.shape[0] // 2
     even = pick(n, 2 * n, lambda r: 2 * r)
     odd = pick(n, 2 * n, lambda r: 2 * r + 1)
     rows_in = jnp.concatenate([nn(even, own[...]), nn(even, other[...])], axis=0).astype(bf16)
     rows_grad = jnp.concatenate([nn(odd, own[...]), nn(odd, other[...])], axis=0).astype(bf16)
     preact = nn(rows_in, w_in[...])
+    for copy in copies:
+        copy.wait()
     hidden_grad = nn(rows_grad, w_out[...])
     cumulative = 0.5 * (1.0 + lax.erf(preact * root_half))
     slope = cumulative + preact * jnp.exp(-0.5 * preact * preact) * density
@@ -164,7 +178,7 @@
         route_kernel,
         [((n2, width), bf16), ((EXPERTS, patch), f32), ((EXPERTS, patch), f32)],
         10**7, 1500000, "hhv",
-        [pltpu.VMEM((patch, width), bf16)] * 2 + [pltpu.SemaphoreType.DMA((2,))], 62_000_000,
+        [pltpu.VMEM((patch, width), bf16)] * 2 + [pltpu.SemaphoreType.DMA((2, PIECES))], 56_000_000,
     )(tok, cot, sp)
 
     def exchange(rows):
@@ -179,7 +193,9 @@
     part_own, part_other, c0, c1, c2, c3 = call(
         expert_kernel,
         [((n2, width), bf16), ((n2, width), bf16)] + [chunk_shape] * 4,
-        5 * 10**8, 4500000, "svvvv", [pltpu.VMEM((width, 128), bf16)],
+        5 * 10**8, 4500000, "svvvh",
+        [pltpu.VMEM((width, 128), bf16), pltpu.VMEM((width, hidden), bf16), pltpu.SemaphoreType.DMA((PIECES,))],
+        53_000_000,
     )(place, own, other, in_weight, out_weight)
 
     back = lax.ppermute(part_other, "c", swap)
@@ -194,7 +210,7 @@
     keep, s1, s2, s3 = call(
         term_kernel,
         [((depth, 2 * hidden), f32), piece, piece, piece],
-        4 * 10**8, 2500000, "vvvva",
+        12 * 10**9, 2500000, "vvvva",
     )(*got, returned)
     shares = [
         lax.ppermute(s, "yh", [(i, (i + k) % 4) for i in range(4)]) for k, s in ((2, s2), (1, s1), (3, s3))

time: 109 us -> 104 us (0.954)
  waiting for transfers between devices: 20.4 us -> 13.6 us
    ppermute x3, waiting for transfers between devices: 8.72 us -> 3.58 us  [per_device(): got.append(lax.ppermute(chunk, QUAD, [(i, i ^ m) for i in range(QUADS)]))]
    pallas_call x1, Pallas kernels: 3.91 us -> 2.51 us  [per_device(): call(route_kernel, [((n2, width), bf16), ((EXPERTS, patch), f32), ((EXPER...]
  transfers between devices with their start and end apart: 9 -> 9, of which waited for: 7 -> 4; matrix products, arithmetic and copies ran while one was open for 0% -> 2% of each run, Pallas kernels for 2% -> 3%
where the time goes in v4:
time: 104 us
  blocking collectives  39.5 us (38%)
  starting transfers between devices  35.2 us (34%)
  waiting for transfers between devices  13.6 us (13%)
  Pallas kernels  10.2 us (10%)
  local copies, waits for them, and re-layouts  4.33 us (4%)
    all_to_all x1, blocking collectives, exchange(): lax.all_to_all(rows.reshape(CHIP_COUNT, 2, width), CHIPS, 0, 0, tiled=True)  39.5 us
    ppermute x3, starting transfers between devices, per_device(): lax.ppermute(s, 'yh', [(i, (i + k) % 4) for i in range(4)])  14.8 us
    ppermute x3, waiting for transfers between devices, per_device(): lax.ppermute(s, 'yh', [(i, (i + k) % 4) for i in range(4)])  9.14 us
    ppermute x3, starting transfers between devices, per_device(): got.append(lax.ppermute(chunk, QUAD, [(i, i ^ m) for i in range(QUADS)]))  8.37 us
    ppermute x1, starting transfers between devices, per_device(): other = lax.ppermute(own, 'c', swap)  5.15 us
    all_to_all x1, starting transfers between devices, exchange(): lax.all_to_all(rows.reshape(CHIP_COUNT, 2, width), CHIPS, 0, 0, tiled=True)  4.56 us
    ppermute x3, waiting for transfers between devices, per_device(): got.append(lax.ppermute(chunk, QUAD, [(i, i ^ m) for i in range(QUADS)]))  3.58 us
    pallas_call x1, Pallas kernels, per_device(): call(expert_kernel, [((n2, width), bf16), ((n2, width), bf16)] + [chunk_s...  3.51 us
  transfers between devices with their start and end apart: 9, of which 4 were waited for; matrix products, arithmetic and copies ran while one was open for 2% of the time, Pallas kernels for 3%

profile of v4, /device:TPU:1, one launch (start us, length us, event | category | flops | bytes accessed | tf_op | source)
XLA Modules:
  0.0 103.8 jit_solution(8728004361280467523)
XLA Ops:
  0.6 0.0 copy-start.2
  0.6 0.0 copy-start.3
  0.7 0.8 copy-done.3
  1.5 2.5 %shard_map.84 = (bf16[64,1280]{1,0:T(8,128)(2,1)S(1)}, f32[8,256]{1,0:T(8,128)S(1)}, f32[8,256]{1,0:T(8,128)S(1)}) custom-call(bf16[256,1280]{1,0:T(8,128)(2,1)} %bitcast.7, bf16[256,1280]{1,0:T(8,128)(2,1)} %bitcast.9, bf16[8,1280]{1,0:T(8,128)(2,1)S(1)} %bitcast.11), custom_call_target="tpu_custom_call" | custom-call | flops 10000000 | bytes 1500000 | tf_op jit(solution)/shard_map/pallas_call | solution.py:177
  4.0 0.1 reshape.20
  4.1 39.5 %all_to_all.10 = bf16[32,2,1280]{2,1,0:T(2,128)(2,1)S(1)} all-to-all(bf16[32,2,1280]{2,1,0:T(2,128)(2,1)S(1)} %reshape.20), channel_id=1, replica_groups=mesh['yh'=4,'yl'=2,'xl'=2,'xh'=2,'zh'=4,'zl'=4,'c'=2] {'xh','zh','zl'}, dimensions={0} | all-to-all | bytes 327680 | tf_op jit(solution)/shard_map/all_to_all | solution.py:185
  43.6 0.1 reshape.21.own
  43.7 5.2 %collective-permute-start = (bf16[64,1280]{1,0:T(8,128)(2,1)S(1)}, bf16[64,1280]{1,0:T(8,128)(2,1)S(1)}, u32[]{:S(2)}, u32[]{:S(2)}) collective-permute-start(bf16[64,1280]{1,0:T(8,128)(2,1)S(1)} %reshape.21.own), channel_id=1, source_target_pairs={{0,1},{1,0},{2,3},{3,2},{4,5},{5,4},{6,7},{7,6},{8,9},{9,8},{10,11... | collective-permute-start | bytes 491528 | tf_op jit(solution)/shard_map/ppermute | solution.py:190
  48.9 0.1 pad_add_fusion.place
  48.9 0.9 collective-permute-done.other
  49.9 0.0 copy-done.2
  49.9 3.5 %shard_map.85 = (bf16[64,1280]{1,0:T(8,128)(2,1)S(1)}, bf16[64,1280]{1,0:T(8,128)(2,1)S(1)}, bf16[192,640]{1,0:T(8,128)(2,1)S(1)}, bf16[192,640]{1,0:T(8,128)(2,...) custom-call(s32[2]{0:T(128)S(1)} %pad_add_fusion.place, bf16[64,1280]{1,0:T(8,128)(2,1)S(1)} %reshape.21.own, ...), custom_call_target="tpu_custom_call" | custom-call | flops 500000000 | bytes 4500000 | tf_op jit(solution)/shard_map/pallas_call | solution.py:193
  53.4 2.3 %collective-permute-start.1 = (bf16[64,1280]{1,0:T(8,128)(2,1)S(1)}, bf16[64,1280]{1,0:T(8,128)(2,1)S(1)}, u32[]{:S(2)}, u32[]{:S(2)}) collective-permute-start(bf16[64,1280]{1,0:T(8,128)(2,1)S(1)} %get-tuple-element.24), channel_id=1, source_target_pairs={{0,1},{1,0},{2,3},{3,2},{4,5},{5,4},{6,7},{7,6},{8,9},{9,8},{10,11... | collective-permute-start | bytes 491528 | tf_op jit(solution)/shard_map/ppermute | solution.py:201
  55.7 2.2 %collective-permute-start.2 = (bf16[192,640]{1,0:T(8,128)(2,1)S(1)}, bf16[192,640]{1,0:T(8,128)(2,1)S(1)}, u32[]{:S(2)}, u32[]{:S(2)}) collective-permute-start(bf16[192,640]{1,0:T(8,128)(2,1)S(1)} %get-tuple-element.30), channel_id=1, source_target_pairs={{0,64},{64,0},{128,192},{192,128},{1,65},{65,1},{129,193},{193,129... | collective-permute-start | bytes 737288 | tf_op jit(solution)/shard_map/ppermute | solution.py:204
  57.9 3.2 %collective-permute-start.3 = (bf16[192,640]{1,0:T(8,128)(2,1)S(1)}, bf16[192,640]{1,0:T(8,128)(2,1)S(1)}, u32[]{:S(2)}, u32[]{:S(2)}) collective-permute-start(bf16[192,640]{1,0:T(8,128)(2,1)S(1)} %get-tuple-element.31), channel_id=1, source_target_pairs={{0,128},{64,192},{128,0},{192,64},{1,129},{65,193},{129,1},{193,65... | collective-permute-start | bytes 737288 | tf_op jit(solution)/shard_map/ppermute | solution.py:204
  61.1 3.0 %collective-permute-start.4 = (bf16[192,640]{1,0:T(8,128)(2,1)S(1)}, bf16[192,640]{1,0:T(8,128)(2,1)S(1)}, u32[]{:S(2)}, u32[]{:S(2)}) collective-permute-start(bf16[192,640]{1,0:T(8,128)(2,1)S(1)} %get-tuple-element.32), channel_id=1, source_target_pairs={{0,192},{64,128},{128,64},{192,0},{1,193},{65,129},{129,65},{193,1... | collective-permute-start | bytes 737288 | tf_op jit(solution)/shard_map/ppermute | solution.py:204
  64.0 0.0 collective-permute-done.1
  64.1 0.7 reshape.22
  64.8 4.6 %all-to-all-start.1 = ((bf16[32,2,1280]{2,1,0:T(2,128)(2,1)}), bf16[32,2,1280]{2,1,0:T(2,128)(2,1)}, u32[]{:S(2)}, u32[]{:S(2)}) async-start(bf16[32,2,1280]{2,1,0:T(2,128)(2,1)} %reshape.22), calls=%async_computation.1 | async-start | bytes 327680 | tf_op jit(solution)/shard_map/all_to_all | solution.py:185
  69.4 0.0 collective-permute-done.2.c1
  69.4 0.0 collective-permute-done.3.c2
  69.4 3.6 %collective-permute-done.4.c3 = bf16[192,640]{1,0:T(8,128)(2,1)S(1)} collective-permute-done((bf16[192,640]{1,0:T(8,128)(2,1)S(1)}, bf16[192,640]{1,0:T(8,128)(2,1)S(1)}, u32[]{:S(2)}, u32[]{:S(2)}) %collective-permute-start.4) | collective-permute-done | bytes 245792 | tf_op jit(solution)/shard_map/ppermute | solution.py:204
  73.0 0.0 copy-start.5
  73.0 0.7 copy-done.5
  73.7 0.0 copy-start.6
  73.7 0.9 copy-done.6
  74.6 0.0 copy-start
  74.6 0.0 copy-start.1
  74.6 0.0 copy-start.4
  74.6 1.3 %shard_map.87 = (f32[80,1280]{1,0:T(8,128)S(1)}, bf16[80,1280]{1,0:T(8,128)(2,1)}, bf16[80,1280]{1,0:T(8,128)(2,1)}, bf16[80,1280]{1,0:T(8,128)(2,1)S(1)}) custom-call(bf16[192,640]{1,0:T(8,128)(2,1)S(1)} %get-tuple-element.29.c0, bf16[192,640]{1,0:T(8,128)(2,1)S(1)} %collective-permute-done.2.c1, bf16[192,640]{1,0:T(8,128)(2,1)S(1)} %collective-permute-done.3.c2, ...), custom_call_target="tpu_custom_call" | custom-call | flops 12000000000 | bytes 2500000 | tf_op jit(solution)/shard_map/pallas_call | solution.py:210
  75.9 7.4 %collective-permute-start.5 = (bf16[80,1280]{1,0:T(8,128)(2,1)}, bf16[80,1280]{1,0:T(8,128)(2,1)S(1)}, u32[]{:S(2)}, u32[]{:S(2)}) collective-permute-start(bf16[80,1280]{1,0:T(8,128)(2,1)} %get-tuple-element.34), channel_id=1, source_target_pairs={{0,512},{256,768},{512,0},{768,256},{1,513},{257,769},{513,1},{769... | collective-permute-start | bytes 614408 | tf_op jit(solution)/shard_map/ppermute | solution.py:216
  83.4 2.4 %collective-permute-start.6 = (bf16[80,1280]{1,0:T(8,128)(2,1)}, bf16[80,1280]{1,0:T(8,128)(2,1)S(1)}, u32[]{:S(2)}, u32[]{:S(2)}) collective-permute-start(bf16[80,1280]{1,0:T(8,128)(2,1)} %get-tuple-element.35), channel_id=1, source_target_pairs={{0,256},{256,512},{512,768},{768,0},{1,257},{257,513},{513,769},{7... | collective-permute-start | bytes 614408 | tf_op jit(solution)/shard_map/ppermute | solution.py:216
  85.8 5.0 %collective-permute-start.7 = (bf16[80,1280]{1,0:T(8,128)(2,1)S(1)}, bf16[80,1280]{1,0:T(8,128)(2,1)S(1)}, u32[]{:S(2)}, u32[]{:S(2)}) collective-permute-start(bf16[80,1280]{1,0:T(8,128)(2,1)S(1)} %get-tuple-element.36), channel_id=1, source_target_pairs={{0,768},{256,0},{512,256},{768,512},{1,769},{257,1},{513,257},{769... | collective-permute-start | bytes 614408 | tf_op jit(solution)/shard_map/ppermute | solution.py:216
  90.8 0.0 all-to-all-done.1
  90.8 1.0 reshape.23.parts
  91.8 0.0 copy-done
  91.8 0.0 copy-done.1
  91.8 0.0 copy-done.4
  91.8 2.0 %shard_map.86 = (bf16[256,1280]{1,0:T(8,128)(2,1)}, bf16[256,1280]{1,0:T(8,128)(2,1)}, f32[8,128]{1,0:T(8,128)S(1)}) custom-call(bf16[256,1280]{1,0:T(8,128)(2,1)S(1)} %bitcast.8, bf16[256,1280]{1,0:T(8,128)(2,1)S(1)} %bitcast.10, bf16[8,1280]{1,0:T(8,128)(2,1)S(1)} %bitcast.12, bf16[64,1280]{1,0:T(8,128)(2,1)S(1)} %reshape.23.parts, ...), custom_call_target="tpu_custom_call" | custom-call | flops 30000000 | bytes 3000000 | tf_op jit(solution)/shard_map/pallas_call | solution.py:219
  93.9 0.0 collective-permute-done.5.a
  93.9 4.2 %collective-permute-done.6.b = bf16[80,1280]{1,0:T(8,128)(2,1)S(1)} collective-permute-done((bf16[80,1280]{1,0:T(8,128)(2,1)}, bf16[80,1280]{1,0:T(8,128)(2,1)S(1)}, u32[]{:S(2)}, u32[]{:S(2)}) %collective-permute-start.6) | collective-permute-done | bytes 204832 | tf_op jit(solution)/shard_map/ppermute | solution.py:216
  98.0 5.0 %collective-permute-done.7.c = bf16[80,1280]{1,0:T(8,128)(2,1)S(1)} collective-permute-done((bf16[80,1280]{1,0:T(8,128)(2,1)S(1)}, bf16[80,1280]{1,0:T(8,128)(2,1)S(1)}, u32[]{:S(2)}, u32[]{:S(2)}) %collective-permute-start.7) | collective-permute-done | bytes 204832 | tf_op jit(solution)/shard_map/ppermute | solution.py:216
  103.0 0.8 shard_map.88
  (1 shorter events, 0.0 us)
Async XLA Ops:
  0.6 49.2 %copy-start.2 = (bf16[1280,640]{1,0:T(8,128)(2,1)S(1)}, bf16[1280,640]{1,0:T(8,128)(2,1)}, u32[]{:S(2)}) copy-start(bf16[1280,640]{1,0:T(8,128)(2,1)} %w_in.1) | copy-start | bytes 4915204
  0.6 0.9 copy-start.3
  43.7 6.2 %collective-permute-start = (bf16[64,1280]{1,0:T(8,128)(2,1)S(1)}, bf16[64,1280]{1,0:T(8,128)(2,1)S(1)}, u32[]{:S(2)}, u32[]{:S(2)}) collective-permute-start(bf16[64,1280]{1,0:T(8,128)(2,1)S(1)} %reshape.21.own), channel_id=1, source_target_pairs={{0,1},{1,0},{2,3},{3,2},{4,5},{5,4},{6,7},{7,6},{8,9},{9,8},{10,11... | collective-permute-start | bytes 491528 | tf_op jit(solution)/shard_map/ppermute | solution.py:190
  53.4 10.7 %collective-permute-start.1 = (bf16[64,1280]{1,0:T(8,128)(2,1)S(1)}, bf16[64,1280]{1,0:T(8,128)(2,1)S(1)}, u32[]{:S(2)}, u32[]{:S(2)}) collective-permute-start(bf16[64,1280]{1,0:T(8,128)(2,1)S(1)} %get-tuple-element.24), channel_id=1, source_target_pairs={{0,1},{1,0},{2,3},{3,2},{4,5},{5,4},{6,7},{7,6},{8,9},{9,8},{10,11... | collective-permute-start | bytes 491528 | tf_op jit(solution)/shard_map/ppermute | solution.py:201
  55.7 13.8 %collective-permute-start.2 = (bf16[192,640]{1,0:T(8,128)(2,1)S(1)}, bf16[192,640]{1,0:T(8,128)(2,1)S(1)}, u32[]{:S(2)}, u32[]{:S(2)}) collective-permute-start(bf16[192,640]{1,0:T(8,128)(2,1)S(1)} %get-tuple-element.30), channel_id=1, source_target_pairs={{0,64},{64,0},{128,192},{192,128},{1,65},{65,1},{129,193},{193,129... | collective-permute-start | bytes 737288 | tf_op jit(solution)/shard_map/ppermute | solution.py:204
  57.9 11.5 %collective-permute-start.3 = (bf16[192,640]{1,0:T(8,128)(2,1)S(1)}, bf16[192,640]{1,0:T(8,128)(2,1)S(1)}, u32[]{:S(2)}, u32[]{:S(2)}) collective-permute-start(bf16[192,640]{1,0:T(8,128)(2,1)S(1)} %get-tuple-element.31), channel_id=1, source_target_pairs={{0,128},{64,192},{128,0},{192,64},{1,129},{65,193},{129,1},{193,65... | collective-permute-start | bytes 737288 | tf_op jit(solution)/shard_map/ppermute | solution.py:204
  61.1 11.9 %collective-permute-start.4 = (bf16[192,640]{1,0:T(8,128)(2,1)S(1)}, bf16[192,640]{1,0:T(8,128)(2,1)S(1)}, u32[]{:S(2)}, u32[]{:S(2)}) collective-permute-start(bf16[192,640]{1,0:T(8,128)(2,1)S(1)} %get-tuple-element.32), channel_id=1, source_target_pairs={{0,192},{64,128},{128,64},{192,0},{1,193},{65,129},{129,65},{193,1... | collective-permute-start | bytes 737288 | tf_op jit(solution)/shard_map/ppermute | solution.py:204
  64.8 26.0 %all-to-all-start.1 = ((bf16[32,2,1280]{2,1,0:T(2,128)(2,1)}), bf16[32,2,1280]{2,1,0:T(2,128)(2,1)}, u32[]{:S(2)}, u32[]{:S(2)}) async-start(bf16[32,2,1280]{2,1,0:T(2,128)(2,1)} %reshape.22), calls=%async_computation.1 | async-start | bytes 327680 | tf_op jit(solution)/shard_map/all_to_all | solution.py:185
  73.0 0.7 copy-start.5
  73.7 0.9 copy-start.6
  74.6 17.1 %copy-start = (bf16[1,256,1280]{2,1,0:T(8,128)(2,1)S(1)}, bf16[1,256,1280]{2,1,0:T(8,128)(2,1)}, u32[]{:S(2)}) copy-start(bf16[1,256,1280]{2,1,0:T(8,128)(2,1)} %param.5) | copy-start | bytes 1966084
  74.6 17.2 %copy-start.1 = (bf16[1,256,1280]{2,1,0:T(8,128)(2,1)S(1)}, bf16[1,256,1280]{2,1,0:T(8,128)(2,1)}, u32[]{:S(2)}) copy-start(bf16[1,256,1280]{2,1,0:T(8,128)(2,1)} %param.6) | copy-start | bytes 1966084
  74.6 17.2 %copy-start.4 = (bf16[1280,8]{0,1:T(8,128)(2,1)S(1)}, bf16[1280,8]{0,1:T(8,128)(2,1)}, u32[]{:S(2)}) copy-start(bf16[1280,8]{0,1:T(8,128)(2,1)} %param.7) | copy-start | bytes 61444
  75.9 17.9 %collective-permute-start.5 = (bf16[80,1280]{1,0:T(8,128)(2,1)}, bf16[80,1280]{1,0:T(8,128)(2,1)S(1)}, u32[]{:S(2)}, u32[]{:S(2)}) collective-permute-start(bf16[80,1280]{1,0:T(8,128)(2,1)} %get-tuple-element.34), channel_id=1, source_target_pairs={{0,512},{256,768},{512,0},{768,256},{1,513},{257,769},{513,1},{769... | collective-permute-start | bytes 614408 | tf_op jit(solution)/shard_map/ppermute | solution.py:216
  83.4 14.6 %collective-permute-start.6 = (bf16[80,1280]{1,0:T(8,128)(2,1)}, bf16[80,1280]{1,0:T(8,128)(2,1)S(1)}, u32[]{:S(2)}, u32[]{:S(2)}) collective-permute-start(bf16[80,1280]{1,0:T(8,128)(2,1)} %get-tuple-element.35), channel_id=1, source_target_pairs={{0,256},{256,512},{512,768},{768,0},{1,257},{257,513},{513,769},{7... | collective-permute-start | bytes 614408 | tf_op jit(solution)/shard_map/ppermute | solution.py:216
  85.8 17.2 %collective-permute-start.7 = (bf16[80,1280]{1,0:T(8,128)(2,1)S(1)}, bf16[80,1280]{1,0:T(8,128)(2,1)S(1)}, u32[]{:S(2)}, u32[]{:S(2)}) collective-permute-start(bf16[80,1280]{1,0:T(8,128)(2,1)S(1)} %get-tuple-element.36), channel_id=1, source_target_pairs={{0,768},{256,0},{512,256},{768,512},{1,769},{257,1},{513,257},{769... | collective-permute-start | bytes 614408 | tf_op jit(solution)/shard_map/ppermute | solution.py:216

commit v5 on v4

--- a/solution.py
+++ b/solution.py
@@ -60,14 +60,19 @@
     )
 
 
-def route_kernel(tok_hbm, cot_hbm, sp, send, disp, comb, tok, cot, sems):
-    step = tok.shape[0] // PIECES
+def start_pieces(pairs, sems):
     copies = []
-    for i, (src, dst) in enumerate(((tok_hbm, tok), (cot_hbm, cot))):
+    for i, (src, dst) in enumerate(pairs):
+        step = dst.shape[0] // PIECES
         for p in range(PIECES):
             rows = pl.ds(p * step, step)
             copies.append(pltpu.make_async_copy(src.at[rows], dst.at[rows], sems.at[i, p]))
             copies[-1].start()
+    return copies
+
+
+def route_kernel(tok_hbm, cot_hbm, sp, send, disp, comb, tok, cot, sems):
+    copies = start_pieces(((tok_hbm, tok), (cot_hbm, cot)), sems)
     for copy in copies[:PIECES]:
         copy.wait()
     logits = nt(sp[...], tok[...])
@@ -88,36 +93,19 @@
 
 
 def expert_kernel(place, own, other, w_in, w_out_hbm, part_own, part_other, c0, c1, c2, c3, turned, w_out, sems):
-    step = w_out.shape[0] // PIECES
-    copies = []
-    for p in range(PIECES):
-        rows = pl.ds(p * step, step)
-        copies.append(pltpu.make_async_copy(w_out_hbm.at[rows], w_out.at[rows], sems.at[p]))
-        copies[-1].start()
+    copies = start_pieces(((w_out_hbm, w_out),), sems)
     n = own.shape[0] // 2
     even = pick(n, 2 * n, lambda r: 2 * r)
     odd = pick(n, 2 * n, lambda r: 2 * r + 1)
     rows_in = jnp.concatenate([nn(even, own[...]), nn(even, other[...])], axis=0).astype(bf16)
     rows_grad = jnp.concatenate([nn(odd, own[...]), nn(odd, other[...])], axis=0).astype(bf16)
     preact = nn(rows_in, w_in[...])
-    for copy in copies:
-        copy.wait()
-    hidden_grad = nn(rows_grad, w_out[...])
-    cumulative = 0.5 * (1.0 + lax.erf(preact * root_half))
-    slope = cumulative + preact * jnp.exp(-0.5 * preact * preact) * density
-    act = (preact * cumulative).astype(bf16)
-    gp = (hidden_grad * slope).astype(bf16)
-    out_part = nt(act, w_out[...]).astype(bf16)
-    grad_part = nt(gp, w_in[...]).astype(bf16)
-    part_own[...] = (tn(even, out_part[:n]) + tn(odd, grad_part[:n])).astype(bf16)
-    part_other[...] = (tn(even, out_part[n:]) + tn(odd, grad_part[n:])).astype(bf16)
     both = jnp.concatenate([rows_in, rows_grad], axis=0)
     turned[...] = jnp.transpose(both.astype(f32)).astype(bf16)
     yh, j0 = place[0], place[1]
     depth = turned.shape[0] // 16
-    for m, chunk in enumerate((c0, c1, c2, c3)):
-        chunk[0 : 2 * n, :] = gp
-        chunk[2 * n : 4 * n, :] = act
+    chunks = (c0, c1, c2, c3)
+    for m, chunk in enumerate(chunks):
         j = jnp.bitwise_xor(j0, m)
         pieces = []
         for k in range(4):
@@ -126,6 +114,21 @@
         piece = jnp.concatenate(pieces, axis=0)
         for b in range(5):
             chunk[4 * n : 6 * n, 128 * b : 128 * (b + 1)] = piece[64 * b : 64 * (b + 1)]
+    cumulative = 0.5 * (1.0 + lax.erf(preact * root_half))
+    slope = cumulative + preact * jnp.exp(-0.5 * preact * preact) * density
+    act = (preact * cumulative).astype(bf16)
+    for chunk in chunks:
+        chunk[2 * n : 4 * n, :] = act
+    for copy in copies:
+        copy.wait()
+    hidden_grad = nn(rows_grad, w_out[...])
+    gp = (hidden_grad * slope).astype(bf16)
+    for chunk in chunks:
+        chunk[0 : 2 * n, :] = gp
+    out_part = nt(act, w_out[...]).astype(bf16)
+    grad_part = nt(gp, w_in[...]).astype(bf16)
+    part_own[...] = (tn(even, out_part[:n]) + tn(odd, grad_part[:n])).astype(bf16)
+    part_other[...] = (tn(even, out_part[n:]) + tn(odd, grad_part[n:])).astype(bf16)
 
 
 def term_kernel(c0, c1, c2, c3, _, keep, s1, s2, s3):
@@ -142,7 +145,10 @@
         s[...] = total[(k + 1) * depth : (k + 2) * depth].astype(bf16)
 
 
-def finish_kernel(tok, cot, sp, parts, disp, comb, mixed, grad_tokens, done):
+def finish_kernel(tok_hbm, cot_hbm, sp, parts, disp, comb, mixed, grad_tokens, done, tok, cot, sems):
+    copies = start_pieces(((tok_hbm, tok), (cot_hbm, cot)), sems)
+    for copy in copies:
+        copy.wait()
     done[...] = jnp.zeros_like(done)
     r = lax.broadcasted_iota(jnp.int32, (16, 2 * CHIP_COUNT), 0)
     c = lax.broadcasted_iota(jnp.int32, (16, 2 * CHIP_COUNT), 1)
@@ -194,7 +200,7 @@
         expert_kernel,
         [((n2, width), bf16), ((n2, width), bf16)] + [chunk_shape] * 4,
         5 * 10**8, 4500000, "svvvh",
-        [pltpu.VMEM((width, 128), bf16), pltpu.VMEM((width, hidden), bf16), pltpu.SemaphoreType.DMA((PIECES,))],
+        [pltpu.VMEM((width, 128), bf16), pltpu.VMEM((width, hidden), bf16), pltpu.SemaphoreType.DMA((1, PIECES))],
         53_000_000,
     )(place, own, other, in_weight, out_weight)
 
@@ -219,7 +225,8 @@
     mixed, grad_tokens, done = call(
         finish_kernel,
         [((patch, width), bf16), ((patch, width), bf16), ((8, 128), f32)],
-        3 * 10**7, 3000000, "vvvvvv",
+        3 * 10**7, 3000000, "hhvvvv",
+        [pltpu.VMEM((patch, width), bf16)] * 2 + [pltpu.SemaphoreType.DMA((2, PIECES))], 56_000_000,
     )(tok, cot, sp, parts, disp, comb)
     grad_in, grad_out = call(
         total_kernel, [((depth, hidden), f32)] * 2, 10**6, 1500000, "vvvva",

time: 104 us -> 102 us (0.981)
  local copies, waits for them, and re-layouts: 4.33 us -> 1.78 us
  Pallas kernels: 10.2 us -> 11.4 us
    unnamed x14 -> x6, local copies, waits for them, and re-layouts: 2.5 us -> 0.85 us
    pallas_call x1, Pallas kernels: 2.05 us -> 3.49 us  [per_device(): call(finish_kernel, [((patch, width), bf16), ((patch, width), bf16), ((8,...]
  transfers between devices with their start and end apart: 9 -> 9, of which waited for: 4 -> 4; matrix products, arithmetic and copies ran while one was open for 2% -> 1% of each run, Pallas kernels for 3% -> 4%
where the time goes in v5:
time: 102 us
  blocking collectives  39.5 us (39%)
  starting transfers between devices  34.5 us (34%)
  waiting for transfers between devices  13.7 us (13%)
  Pallas kernels  11.4 us (11%)
  local copies, waits for them, and re-layouts  1.78 us (2%)
    all_to_all x1, blocking collectives, exchange(): lax.all_to_all(rows.reshape(CHIP_COUNT, 2, width), CHIPS, 0, 0, tiled=True)  39.5 us
    ppermute x3, starting transfers between devices, per_device(): lax.ppermute(s, 'yh', [(i, (i + k) % 4) for i in range(4)])  14.9 us
    ppermute x3, starting transfers between devices, per_device(): got.append(lax.ppermute(chunk, QUAD, [(i, i ^ m) for i in range(QUADS)]))  8.37 us
    ppermute x3, waiting for transfers between devices, per_device(): lax.ppermute(s, 'yh', [(i, (i + k) % 4) for i in range(4)])  8.37 us
    ppermute x1, starting transfers between devices, per_device(): other = lax.ppermute(own, 'c', swap)  5.15 us
    ppermute x3, waiting for transfers between devices, per_device(): got.append(lax.ppermute(chunk, QUAD, [(i, i ^ m) for i in range(QUADS)]))  4.37 us
    pallas_call x1, Pallas kernels, per_device(): call(expert_kernel, [((n2, width), bf16), ((n2, width), bf16)] + [chunk_s...  3.96 us
    all_to_all x1, starting transfers between devices, exchange(): lax.all_to_all(rows.reshape(CHIP_COUNT, 2, width), CHIPS, 0, 0, tiled=True)  3.86 us
  transfers between devices with their start and end apart: 9, of which 4 were waited for; matrix products, arithmetic and copies ran while one was open for 1% of the time, Pallas kernels for 4%

profile of v5, /device:TPU:1, one launch (start us, length us, event | category | flops | bytes accessed | tf_op | source)
XLA Modules:
  0.0 101.8 jit_solution(12247271501902535439)
XLA Ops:
  0.6 0.0 copy-start
  0.6 0.0 copy-start.1
  0.7 0.8 copy-done.1
  1.5 2.5 %shard_map.84 = (bf16[64,1280]{1,0:T(8,128)(2,1)S(1)}, f32[8,256]{1,0:T(8,128)S(1)}, f32[8,256]{1,0:T(8,128)S(1)}) custom-call(bf16[256,1280]{1,0:T(8,128)(2,1)} %bitcast.9, bf16[256,1280]{1,0:T(8,128)(2,1)} %bitcast.11, bf16[8,1280]{1,0:T(8,128)(2,1)S(1)} %bitcast.7), custom_call_target="tpu_custom_call" | custom-call | flops 10000000 | bytes 1500000 | tf_op jit(solution)/shard_map/pallas_call | solution.py:183
  4.0 0.1 reshape.20
  4.1 39.5 %all_to_all.10 = bf16[32,2,1280]{2,1,0:T(2,128)(2,1)S(1)} all-to-all(bf16[32,2,1280]{2,1,0:T(2,128)(2,1)S(1)} %reshape.20), channel_id=1, replica_groups=mesh['yh'=4,'yl'=2,'xl'=2,'xh'=2,'zh'=4,'zl'=4,'c'=2] {'xh','zh','zl'}, dimensions={0} | all-to-all | bytes 327680 | tf_op jit(solution)/shard_map/all_to_all | solution.py:191
  43.6 0.1 reshape.21.own
  43.7 5.2 %collective-permute-start = (bf16[64,1280]{1,0:T(8,128)(2,1)S(1)}, bf16[64,1280]{1,0:T(8,128)(2,1)S(1)}, u32[]{:S(2)}, u32[]{:S(2)}) collective-permute-start(bf16[64,1280]{1,0:T(8,128)(2,1)S(1)} %reshape.21.own), channel_id=1, source_target_pairs={{0,1},{1,0},{2,3},{3,2},{4,5},{5,4},{6,7},{7,6},{8,9},{9,8},{10,11... | collective-permute-start | bytes 491528 | tf_op jit(solution)/shard_map/ppermute | solution.py:196
  48.9 0.1 pad_add_fusion.place
  48.9 0.9 collective-permute-done.other
  49.9 0.0 copy-done
  49.9 4.0 %shard_map.85 = (bf16[64,1280]{1,0:T(8,128)(2,1)S(1)}, bf16[64,1280]{1,0:T(8,128)(2,1)S(1)}, bf16[192,640]{1,0:T(8,128)(2,1)S(1)}, bf16[192,640]{1,0:T(8,128)(2,...) custom-call(s32[2]{0:T(128)S(1)} %pad_add_fusion.place, bf16[64,1280]{1,0:T(8,128)(2,1)S(1)} %reshape.21.own, ...), custom_call_target="tpu_custom_call" | custom-call | flops 500000000 | bytes 4500000 | tf_op jit(solution)/shard_map/pallas_call | solution.py:199
  53.8 2.3 %collective-permute-start.1 = (bf16[64,1280]{1,0:T(8,128)(2,1)S(1)}, bf16[64,1280]{1,0:T(8,128)(2,1)S(1)}, u32[]{:S(2)}, u32[]{:S(2)}) collective-permute-start(bf16[64,1280]{1,0:T(8,128)(2,1)S(1)} %get-tuple-element.24), channel_id=1, source_target_pairs={{0,1},{1,0},{2,3},{3,2},{4,5},{5,4},{6,7},{7,6},{8,9},{9,8},{10,11... | collective-permute-start | bytes 491528 | tf_op jit(solution)/shard_map/ppermute | solution.py:207
  56.1 2.2 %collective-permute-start.2 = (bf16[192,640]{1,0:T(8,128)(2,1)S(1)}, bf16[192,640]{1,0:T(8,128)(2,1)S(1)}, u32[]{:S(2)}, u32[]{:S(2)}) collective-permute-start(bf16[192,640]{1,0:T(8,128)(2,1)S(1)} %get-tuple-element.30), channel_id=1, source_target_pairs={{0,64},{64,0},{128,192},{192,128},{1,65},{65,1},{129,193},{193,129... | collective-permute-start | bytes 737288 | tf_op jit(solution)/shard_map/ppermute | solution.py:210
  58.3 3.2 %collective-permute-start.3 = (bf16[192,640]{1,0:T(8,128)(2,1)S(1)}, bf16[192,640]{1,0:T(8,128)(2,1)S(1)}, u32[]{:S(2)}, u32[]{:S(2)}) collective-permute-start(bf16[192,640]{1,0:T(8,128)(2,1)S(1)} %get-tuple-element.31), channel_id=1, source_target_pairs={{0,128},{64,192},{128,0},{192,64},{1,129},{65,193},{129,1},{193,65... | collective-permute-start | bytes 737288 | tf_op jit(solution)/shard_map/ppermute | solution.py:210
  61.6 2.9 %collective-permute-start.4 = (bf16[192,640]{1,0:T(8,128)(2,1)S(1)}, bf16[192,640]{1,0:T(8,128)(2,1)S(1)}, u32[]{:S(2)}, u32[]{:S(2)}) collective-permute-start(bf16[192,640]{1,0:T(8,128)(2,1)S(1)} %get-tuple-element.32), channel_id=1, source_target_pairs={{0,192},{64,128},{128,64},{192,0},{1,193},{65,129},{129,65},{193,1... | collective-permute-start | bytes 737288 | tf_op jit(solution)/shard_map/ppermute | solution.py:210
  64.5 0.0 collective-permute-done.1
  64.6 0.7 reshape.22
  65.3 3.9 %all-to-all-start.1 = ((bf16[32,2,1280]{2,1,0:T(2,128)(2,1)}), bf16[32,2,1280]{2,1,0:T(2,128)(2,1)S(1)}, u32[]{:S(2)}, u32[]{:S(2)}) async-start(bf16[32,2,1280]{2,1,0:T(2,128)(2,1)} %reshape.22), calls=%async_computation.1 | async-start | bytes 327680 | tf_op jit(solution)/shard_map/all_to_all | solution.py:191
  69.2 0.0 collective-permute-done.2.c1
  69.2 0.0 collective-permute-done.3.c2
  69.2 4.4 %collective-permute-done.4.c3 = bf16[192,640]{1,0:T(8,128)(2,1)S(1)} collective-permute-done((bf16[192,640]{1,0:T(8,128)(2,1)S(1)}, bf16[192,640]{1,0:T(8,128)(2,1)S(1)}, u32[]{:S(2)}, u32[]{:S(2)}) %collective-permute-start.4) | collective-permute-done | bytes 245792 | tf_op jit(solution)/shard_map/ppermute | solution.py:210
  73.6 0.0 copy-start.2
  73.6 0.6 shard_map.87
  74.1 7.5 %collective-permute-start.5 = (bf16[80,1280]{1,0:T(8,128)(2,1)S(1)}, bf16[80,1280]{1,0:T(8,128)(2,1)S(1)}, u32[]{:S(2)}, u32[]{:S(2)}) collective-permute-start(bf16[80,1280]{1,0:T(8,128)(2,1)S(1)} %get-tuple-element.34), channel_id=1, source_target_pairs={{0,512},{256,768},{512,0},{768,256},{1,513},{257,769},{513,1},{769... | collective-permute-start | bytes 614408 | tf_op jit(solution)/shard_map/ppermute | solution.py:222
  81.6 2.4 %collective-permute-start.6 = (bf16[80,1280]{1,0:T(8,128)(2,1)S(1)}, bf16[80,1280]{1,0:T(8,128)(2,1)S(1)}, u32[]{:S(2)}, u32[]{:S(2)}) collective-permute-start(bf16[80,1280]{1,0:T(8,128)(2,1)S(1)} %get-tuple-element.35), channel_id=1, source_target_pairs={{0,256},{256,512},{512,768},{768,0},{1,257},{257,513},{513,769},{7... | collective-permute-start | bytes 614408 | tf_op jit(solution)/shard_map/ppermute | solution.py:222
  84.0 5.0 %collective-permute-start.7 = (bf16[80,1280]{1,0:T(8,128)(2,1)S(1)}, bf16[80,1280]{1,0:T(8,128)(2,1)S(1)}, u32[]{:S(2)}, u32[]{:S(2)}) collective-permute-start(bf16[80,1280]{1,0:T(8,128)(2,1)S(1)} %get-tuple-element.36), channel_id=1, source_target_pairs={{0,768},{256,0},{512,256},{768,512},{1,769},{257,1},{513,257},{769... | collective-permute-start | bytes 614408 | tf_op jit(solution)/shard_map/ppermute | solution.py:222
  89.0 0.0 all-to-all-done.1
  89.0 0.1 reshape.23.parts
  89.1 0.0 copy-done.2
  89.1 3.5 %shard_map.86 = (bf16[256,1280]{1,0:T(8,128)(2,1)}, bf16[256,1280]{1,0:T(8,128)(2,1)}, f32[8,128]{1,0:T(8,128)S(1)}) custom-call(bf16[256,1280]{1,0:T(8,128)(2,1)} %bitcast.10, bf16[256,1280]{1,0:T(8,128)(2,1)} %bitcast.12, bf16[8,1280]{1,0:T(8,128)(2,1)S(1)} %bitcast.8, bf16[64,1280]{1,0:T(8,128)(2,1)S(1)} %reshape.23.parts, ...), custom_call_target="tpu_custom_call" | custom-call | flops 30000000 | bytes 3000000 | tf_op jit(solution)/shard_map/pallas_call | solution.py:225
  92.6 0.0 collective-permute-done.5.a
  92.6 3.4 %collective-permute-done.6.b = bf16[80,1280]{1,0:T(8,128)(2,1)S(1)} collective-permute-done((bf16[80,1280]{1,0:T(8,128)(2,1)S(1)}, bf16[80,1280]{1,0:T(8,128)(2,1)S(1)}, u32[]{:S(2)}, u32[]{:S(2)}) %collective-permute-start.6) | collective-permute-done | bytes 204832 | tf_op jit(solution)/shard_map/ppermute | solution.py:222
  96.1 5.0 %collective-permute-done.7.c = bf16[80,1280]{1,0:T(8,128)(2,1)S(1)} collective-permute-done((bf16[80,1280]{1,0:T(8,128)(2,1)S(1)}, bf16[80,1280]{1,0:T(8,128)(2,1)S(1)}, u32[]{:S(2)}, u32[]{:S(2)}) %collective-permute-start.7) | collective-permute-done | bytes 204832 | tf_op jit(solution)/shard_map/ppermute | solution.py:222
  101.0 0.8 shard_map.88
  (1 shorter events, 0.0 us)
Async XLA Ops:
  0.6 49.2 %copy-start = (bf16[1280,640]{1,0:T(8,128)(2,1)S(1)}, bf16[1280,640]{1,0:T(8,128)(2,1)}, u32[]{:S(2)}) copy-start(bf16[1280,640]{1,0:T(8,128)(2,1)} %w_in.1) | copy-start | bytes 4915204
  0.6 0.9 copy-start.1
  43.7 6.2 %collective-permute-start = (bf16[64,1280]{1,0:T(8,128)(2,1)S(1)}, bf16[64,1280]{1,0:T(8,128)(2,1)S(1)}, u32[]{:S(2)}, u32[]{:S(2)}) collective-permute-start(bf16[64,1280]{1,0:T(8,128)(2,1)S(1)} %reshape.21.own), channel_id=1, source_target_pairs={{0,1},{1,0},{2,3},{3,2},{4,5},{5,4},{6,7},{7,6},{8,9},{9,8},{10,11... | collective-permute-start | bytes 491528 | tf_op jit(solution)/shard_map/ppermute | solution.py:196
  53.8 10.7 %collective-permute-start.1 = (bf16[64,1280]{1,0:T(8,128)(2,1)S(1)}, bf16[64,1280]{1,0:T(8,128)(2,1)S(1)}, u32[]{:S(2)}, u32[]{:S(2)}) collective-permute-start(bf16[64,1280]{1,0:T(8,128)(2,1)S(1)} %get-tuple-element.24), channel_id=1, source_target_pairs={{0,1},{1,0},{2,3},{3,2},{4,5},{5,4},{6,7},{7,6},{8,9},{9,8},{10,11... | collective-permute-start | bytes 491528 | tf_op jit(solution)/shard_map/ppermute | solution.py:207
  56.1 13.1 %collective-permute-start.2 = (bf16[192,640]{1,0:T(8,128)(2,1)S(1)}, bf16[192,640]{1,0:T(8,128)(2,1)S(1)}, u32[]{:S(2)}, u32[]{:S(2)}) collective-permute-start(bf16[192,640]{1,0:T(8,128)(2,1)S(1)} %get-tuple-element.30), channel_id=1, source_target_pairs={{0,64},{64,0},{128,192},{192,128},{1,65},{65,1},{129,193},{193,129... | collective-permute-start | bytes 737288 | tf_op jit(solution)/shard_map/ppermute | solution.py:210
  58.3 10.8 %collective-permute-start.3 = (bf16[192,640]{1,0:T(8,128)(2,1)S(1)}, bf16[192,640]{1,0:T(8,128)(2,1)S(1)}, u32[]{:S(2)}, u32[]{:S(2)}) collective-permute-start(bf16[192,640]{1,0:T(8,128)(2,1)S(1)} %get-tuple-element.31), channel_id=1, source_target_pairs={{0,128},{64,192},{128,0},{192,64},{1,129},{65,193},{129,1},{193,65... | collective-permute-start | bytes 737288 | tf_op jit(solution)/shard_map/ppermute | solution.py:210
  61.6 12.0 %collective-permute-start.4 = (bf16[192,640]{1,0:T(8,128)(2,1)S(1)}, bf16[192,640]{1,0:T(8,128)(2,1)S(1)}, u32[]{:S(2)}, u32[]{:S(2)}) collective-permute-start(bf16[192,640]{1,0:T(8,128)(2,1)S(1)} %get-tuple-element.32), channel_id=1, source_target_pairs={{0,192},{64,128},{128,64},{192,0},{1,193},{65,129},{129,65},{193,1... | collective-permute-start | bytes 737288 | tf_op jit(solution)/shard_map/ppermute | solution.py:210
  65.3 23.7 %all-to-all-start.1 = ((bf16[32,2,1280]{2,1,0:T(2,128)(2,1)}), bf16[32,2,1280]{2,1,0:T(2,128)(2,1)S(1)}, u32[]{:S(2)}, u32[]{:S(2)}) async-start(bf16[32,2,1280]{2,1,0:T(2,128)(2,1)} %reshape.22), calls=%async_computation.1 | async-start | bytes 327680 | tf_op jit(solution)/shard_map/all_to_all | solution.py:191
  73.6 15.6 %copy-start.2 = (bf16[1280,8]{0,1:T(8,128)(2,1)S(1)}, bf16[1280,8]{0,1:T(8,128)(2,1)}, u32[]{:S(2)}) copy-start(bf16[1280,8]{0,1:T(8,128)(2,1)} %param.7) | copy-start | bytes 61444
  74.1 18.5 %collective-permute-start.5 = (bf16[80,1280]{1,0:T(8,128)(2,1)S(1)}, bf16[80,1280]{1,0:T(8,128)(2,1)S(1)}, u32[]{:S(2)}, u32[]{:S(2)}) collective-permute-start(bf16[80,1280]{1,0:T(8,128)(2,1)S(1)} %get-tuple-element.34), channel_id=1, source_target_pairs={{0,512},{256,768},{512,0},{768,256},{1,513},{257,769},{513,1},{769... | collective-permute-start | bytes 614408 | tf_op jit(solution)/shard_map/ppermute | solution.py:222
  81.6 14.4 %collective-permute-start.6 = (bf16[80,1280]{1,0:T(8,128)(2,1)S(1)}, bf16[80,1280]{1,0:T(8,128)(2,1)S(1)}, u32[]{:S(2)}, u32[]{:S(2)}) collective-permute-start(bf16[80,1280]{1,0:T(8,128)(2,1)S(1)} %get-tuple-element.35), channel_id=1, source_target_pairs={{0,256},{256,512},{512,768},{768,0},{1,257},{257,513},{513,769},{7... | collective-permute-start | bytes 614408 | tf_op jit(solution)/shard_map/ppermute | solution.py:222
  84.0 17.0 %collective-permute-start.7 = (bf16[80,1280]{1,0:T(8,128)(2,1)S(1)}, bf16[80,1280]{1,0:T(8,128)(2,1)S(1)}, u32[]{:S(2)}, u32[]{:S(2)}) collective-permute-start(bf16[80,1280]{1,0:T(8,128)(2,1)S(1)} %get-tuple-element.36), channel_id=1, source_target_pairs={{0,768},{256,0},{512,256},{768,512},{1,769},{257,1},{513,257},{769... | collective-permute-start | bytes 614408 | tf_op jit(solution)/shard_map/ppermute | solution.py:222

commit v6 on v4

--- a/solution.py
+++ b/solution.py
@@ -60,14 +60,19 @@
     )
 
 
-def route_kernel(tok_hbm, cot_hbm, sp, send, disp, comb, tok, cot, sems):
-    step = tok.shape[0] // PIECES
+def start_pieces(pairs, sems):
     copies = []
-    for i, (src, dst) in enumerate(((tok_hbm, tok), (cot_hbm, cot))):
+    for i, (src, dst) in enumerate(pairs):
+        step = dst.shape[0] // PIECES
         for p in range(PIECES):
             rows = pl.ds(p * step, step)
             copies.append(pltpu.make_async_copy(src.at[rows], dst.at[rows], sems.at[i, p]))
             copies[-1].start()
+    return copies
+
+
+def route_kernel(tok_hbm, cot_hbm, sp, send, disp, comb, tok, cot, sems):
+    copies = start_pieces(((tok_hbm, tok), (cot_hbm, cot)), sems)
     for copy in copies[:PIECES]:
         copy.wait()
     logits = nt(sp[...], tok[...])
@@ -87,21 +92,13 @@
     send[...] = nn(sel, both).astype(bf16)
 
 
-def expert_kernel(place, own, other, w_in, w_out_hbm, part_own, part_other, c0, c1, c2, c3, turned, w_out, sems):
-    step = w_out.shape[0] // PIECES
-    copies = []
-    for p in range(PIECES):
-        rows = pl.ds(p * step, step)
-        copies.append(pltpu.make_async_copy(w_out_hbm.at[rows], w_out.at[rows], sems.at[p]))
-        copies[-1].start()
+def expert_kernel(place, own, other, w_in, w_out, part_own, part_other, c0, c1, c2, c3, turned):
     n = own.shape[0] // 2
     even = pick(n, 2 * n, lambda r: 2 * r)
     odd = pick(n, 2 * n, lambda r: 2 * r + 1)
     rows_in = jnp.concatenate([nn(even, own[...]), nn(even, other[...])], axis=0).astype(bf16)
     rows_grad = jnp.concatenate([nn(odd, own[...]), nn(odd, other[...])], axis=0).astype(bf16)
     preact = nn(rows_in, w_in[...])
-    for copy in copies:
-        copy.wait()
     hidden_grad = nn(rows_grad, w_out[...])
     cumulative = 0.5 * (1.0 + lax.erf(preact * root_half))
     slope = cumulative + preact * jnp.exp(-0.5 * preact * preact) * density
@@ -142,7 +139,10 @@
         s[...] = total[(k + 1) * depth : (k + 2) * depth].astype(bf16)
 
 
-def finish_kernel(tok, cot, sp, parts, disp, comb, mixed, grad_tokens, done):
+def finish_kernel(tok_hbm, cot_hbm, sp, parts, disp, comb, mixed, grad_tokens, done, tok, cot, sems):
+    copies = start_pieces(((tok_hbm, tok), (cot_hbm, cot)), sems)
+    for copy in copies:
+        copy.wait()
     done[...] = jnp.zeros_like(done)
     r = lax.broadcasted_iota(jnp.int32, (16, 2 * CHIP_COUNT), 0)
     c = lax.broadcasted_iota(jnp.int32, (16, 2 * CHIP_COUNT), 1)
@@ -178,7 +178,8 @@
         route_kernel,
         [((n2, width), bf16), ((EXPERTS, patch), f32), ((EXPERTS, patch), f32)],
         10**7, 1500000, "hhv",
-        [pltpu.VMEM((patch, width), bf16)] * 2 + [pltpu.SemaphoreType.DMA((2, PIECES))], 56_000_000,
+        [pltpu.VMEM((patch, width), bf16)] * 2 + [pltpu.SemaphoreType.DMA((2, PIECES))],
+        56_000_000,
     )(tok, cot, sp)
 
     def exchange(rows):
@@ -193,14 +194,12 @@
     part_own, part_other, c0, c1, c2, c3 = call(
         expert_kernel,
         [((n2, width), bf16), ((n2, width), bf16)] + [chunk_shape] * 4,
-        5 * 10**8, 4500000, "svvvh",
-        [pltpu.VMEM((width, 128), bf16), pltpu.VMEM((width, hidden), bf16), pltpu.SemaphoreType.DMA((PIECES,))],
-        53_000_000,
+        5 * 10**8, 4500000, "svvvv", [pltpu.VMEM((width, 128), bf16)],
     )(place, own, other, in_weight, out_weight)
 
     back = lax.ppermute(part_other, "c", swap)
     got = [c0]
-    for m, chunk in ((1, c1), (2, c2), (3, c3)):
+    for m, chunk in ((3, c3), (1, c1), (2, c2)):
         got.append(lax.ppermute(chunk, QUAD, [(i, i ^ m) for i in range(QUADS)]))
     returned = (part_own.astype(f32) + back.astype(f32)).astype(bf16)
     parts = exchange(returned)
@@ -219,7 +218,8 @@
     mixed, grad_tokens, done = call(
         finish_kernel,
         [((patch, width), bf16), ((patch, width), bf16), ((8, 128), f32)],
-        3 * 10**7, 3000000, "vvvvvv",
+        3 * 10**7, 3000000, "hhvvvv",
+        [pltpu.VMEM((patch, width), bf16)] * 2 + [pltpu.SemaphoreType.DMA((2, PIECES))], 56_000_000,
     )(tok, cot, sp, parts, disp, comb)
     grad_in, grad_out = call(
         total_kernel, [((depth, hidden), f32)] * 2, 10**6, 1500000, "vvvva",

time: 104 us -> 101 us (0.971)
  waiting for transfers between devices: 13.6 us -> 12.2 us
  local copies, waits for them, and re-layouts: 4.33 us -> 3.21 us
    pallas_call x1, Pallas kernels: 2.05 us -> 3.5 us  [per_device(): call(finish_kernel, [((patch, width), bf16), ((patch, width), bf16), ((8,...]
    unnamed x14 -> x8, local copies, waits for them, and re-layouts: 2.5 us -> 2.28 us
  transfers between devices with their start and end apart: 9 -> 9, of which waited for: 4 -> 4; matrix products, arithmetic and copies ran while one was open for 2% -> 1% of each run, Pallas kernels for 3% -> 4%
where the time goes in v6:
time: 101 us; the launch traced here: 100 us
  blocking collectives  39.5 us (39%)
  starting transfers between devices  34.5 us (34%)
  waiting for transfers between devices  12.2 us (12%)
  Pallas kernels  9.95 us (10%)
  local copies, waits for them, and re-layouts  3.21 us (3%)
    all_to_all x1, blocking collectives, exchange(): lax.all_to_all(rows.reshape(CHIP_COUNT, 2, width), CHIPS, 0, 0, tiled=True)  39.5 us
    ppermute x3, starting transfers between devices, per_device(): lax.ppermute(s, 'yh', [(i, (i + k) % 4) for i in range(4)])  14.8 us
    ppermute x3, waiting for transfers between devices, per_device(): lax.ppermute(s, 'yh', [(i, (i + k) % 4) for i in range(4)])  8.38 us
    ppermute x3, starting transfers between devices, per_device(): got.append(lax.ppermute(chunk, QUAD, [(i, i ^ m) for i in range(QUADS)]))  8.37 us
    ppermute x1, starting transfers between devices, per_device(): other = lax.ppermute(own, 'c', swap)  5.15 us
    all_to_all x1, starting transfers between devices, exchange(): lax.all_to_all(rows.reshape(CHIP_COUNT, 2, width), CHIPS, 0, 0, tiled=True)  3.87 us
    pallas_call x1, Pallas kernels, per_device(): call(finish_kernel, [((patch, width), bf16), ((patch, width), bf16), ((8,...  3.5 us
    ppermute x3, waiting for transfers between devices, per_device(): got.append(lax.ppermute(chunk, QUAD, [(i, i ^ m) for i in range(QUADS)]))  2.88 us
  transfers between devices with their start and end apart: 9, of which 4 were waited for; matrix products, arithmetic and copies ran while one was open for 1% of the time, Pallas kernels for 4%

profile of v6, /device:TPU:1, one launch (start us, length us, event | category | flops | bytes accessed | tf_op | source)
XLA Modules:
  0.0 100.3 jit_solution(3801542245382547626)
XLA Ops:
  0.6 0.0 copy-start
  0.6 0.0 copy-start.2
  0.7 0.8 copy-done.2
  1.5 2.5 %shard_map.84 = (bf16[64,1280]{1,0:T(8,128)(2,1)S(1)}, f32[8,256]{1,0:T(8,128)S(1)}, f32[8,256]{1,0:T(8,128)S(1)}) custom-call(bf16[256,1280]{1,0:T(8,128)(2,1)} %bitcast.9, bf16[256,1280]{1,0:T(8,128)(2,1)} %bitcast.11, bf16[8,1280]{1,0:T(8,128)(2,1)S(1)} %bitcast.7), custom_call_target="tpu_custom_call" | custom-call | flops 10000000 | bytes 1500000 | tf_op jit(solution)/shard_map/pallas_call | solution.py:177
  4.0 0.1 reshape.20
  4.1 39.5 %all_to_all.10 = bf16[32,2,1280]{2,1,0:T(2,128)(2,1)S(1)} all-to-all(bf16[32,2,1280]{2,1,0:T(2,128)(2,1)S(1)} %reshape.20), channel_id=1, replica_groups=mesh['yh'=4,'yl'=2,'xl'=2,'xh'=2,'zh'=4,'zl'=4,'c'=2] {'xh','zh','zl'}, dimensions={0} | all-to-all | bytes 327680 | tf_op jit(solution)/shard_map/all_to_all | solution.py:186
  43.6 0.1 reshape.21.own
  43.7 5.2 %collective-permute-start = (bf16[64,1280]{1,0:T(8,128)(2,1)S(1)}, bf16[64,1280]{1,0:T(8,128)(2,1)S(1)}, u32[]{:S(2)}, u32[]{:S(2)}) collective-permute-start(bf16[64,1280]{1,0:T(8,128)(2,1)S(1)} %reshape.21.own), channel_id=1, source_target_pairs={{0,1},{1,0},{2,3},{3,2},{4,5},{5,4},{6,7},{7,6},{8,9},{9,8},{10,11... | collective-permute-start | bytes 491528 | tf_op jit(solution)/shard_map/ppermute | solution.py:191
  48.9 0.1 pad_add_fusion.place
  48.9 0.9 collective-permute-done.other
  49.9 0.0 copy-done
  49.9 0.0 copy-start.1
  49.9 1.4 %copy-done.1 = bf16[1280,640]{1,0:T(8,128)(2,1)S(1)} copy-done((bf16[1280,640]{1,0:T(8,128)(2,1)S(1)}, bf16[1280,640]{1,0:T(8,128)(2,1)}, u32[]{:S(2)}) %copy-start.1) | copy-done | bytes 1638424
  51.3 2.6 %shard_map.85 = (bf16[64,1280]{1,0:T(8,128)(2,1)S(1)}, bf16[64,1280]{1,0:T(8,128)(2,1)S(1)}, bf16[192,640]{1,0:T(8,128)(2,1)S(1)}, bf16[192,640]{1,0:T(8,128)(2,...) custom-call(s32[2]{0:T(128)S(1)} %pad_add_fusion.place, bf16[64,1280]{1,0:T(8,128)(2,1)S(1)} %reshape.21.own, ...), custom_call_target="tpu_custom_call" | custom-call | flops 500000000 | bytes 4500000 | tf_op jit(solution)/shard_map/pallas_call | solution.py:194
  53.9 2.3 %collective-permute-start.1 = (bf16[64,1280]{1,0:T(8,128)(2,1)S(1)}, bf16[64,1280]{1,0:T(8,128)(2,1)S(1)}, u32[]{:S(2)}, u32[]{:S(2)}) collective-permute-start(bf16[64,1280]{1,0:T(8,128)(2,1)S(1)} %get-tuple-element.24), channel_id=1, source_target_pairs={{0,1},{1,0},{2,3},{3,2},{4,5},{5,4},{6,7},{7,6},{8,9},{9,8},{10,11... | collective-permute-start | bytes 491528 | tf_op jit(solution)/shard_map/ppermute | solution.py:200
  56.1 3.2 %collective-permute-start.2 = (bf16[192,640]{1,0:T(8,128)(2,1)S(1)}, bf16[192,640]{1,0:T(8,128)(2,1)S(1)}, u32[]{:S(2)}, u32[]{:S(2)}) collective-permute-start(bf16[192,640]{1,0:T(8,128)(2,1)S(1)} %get-tuple-element.30), channel_id=1, source_target_pairs={{0,192},{64,128},{128,64},{192,0},{1,193},{65,129},{129,65},{193,1... | collective-permute-start | bytes 737288 | tf_op jit(solution)/shard_map/ppermute | solution.py:203
  59.4 3.1 %collective-permute-start.3 = (bf16[192,640]{1,0:T(8,128)(2,1)S(1)}, bf16[192,640]{1,0:T(8,128)(2,1)S(1)}, u32[]{:S(2)}, u32[]{:S(2)}) collective-permute-start(bf16[192,640]{1,0:T(8,128)(2,1)S(1)} %get-tuple-element.31), channel_id=1, source_target_pairs={{0,64},{64,0},{128,192},{192,128},{1,65},{65,1},{129,193},{193,129... | collective-permute-start | bytes 737288 | tf_op jit(solution)/shard_map/ppermute | solution.py:203
  62.4 2.1 %collective-permute-start.4 = (bf16[192,640]{1,0:T(8,128)(2,1)S(1)}, bf16[192,640]{1,0:T(8,128)(2,1)S(1)}, u32[]{:S(2)}, u32[]{:S(2)}) collective-permute-start(bf16[192,640]{1,0:T(8,128)(2,1)S(1)} %get-tuple-element.32), channel_id=1, source_target_pairs={{0,128},{64,192},{128,0},{192,64},{1,129},{65,193},{129,1},{193,65... | collective-permute-start | bytes 737288 | tf_op jit(solution)/shard_map/ppermute | solution.py:203
  64.5 0.0 collective-permute-done.1
  64.6 0.7 reshape.22
  65.3 3.9 %all-to-all-start.1 = ((bf16[32,2,1280]{2,1,0:T(2,128)(2,1)}), bf16[32,2,1280]{2,1,0:T(2,128)(2,1)S(1)}, u32[]{:S(2)}, u32[]{:S(2)}) async-start(bf16[32,2,1280]{2,1,0:T(2,128)(2,1)} %reshape.22), calls=%async_computation.1 | async-start | bytes 327680 | tf_op jit(solution)/shard_map/all_to_all | solution.py:186
  69.2 0.0 collective-permute-done.2.c1
  69.2 2.9 %collective-permute-done.3.c2 = bf16[192,640]{1,0:T(8,128)(2,1)S(1)} collective-permute-done((bf16[192,640]{1,0:T(8,128)(2,1)S(1)}, bf16[192,640]{1,0:T(8,128)(2,1)S(1)}, u32[]{:S(2)}, u32[]{:S(2)}) %collective-permute-start.3) | collective-permute-done | bytes 245792 | tf_op jit(solution)/shard_map/ppermute | solution.py:203
  72.1 0.0 collective-permute-done.4.c3
  72.1 0.0 copy-start.3
  72.1 0.6 shard_map.87
  72.7 7.4 %collective-permute-start.5 = (bf16[80,1280]{1,0:T(8,128)(2,1)S(1)}, bf16[80,1280]{1,0:T(8,128)(2,1)S(1)}, u32[]{:S(2)}, u32[]{:S(2)}) collective-permute-start(bf16[80,1280]{1,0:T(8,128)(2,1)S(1)} %get-tuple-element.34), channel_id=1, source_target_pairs={{0,512},{256,768},{512,0},{768,256},{1,513},{257,769},{513,1},{769... | collective-permute-start | bytes 614408 | tf_op jit(solution)/shard_map/ppermute | solution.py:215
  80.1 2.4 %collective-permute-start.6 = (bf16[80,1280]{1,0:T(8,128)(2,1)S(1)}, bf16[80,1280]{1,0:T(8,128)(2,1)S(1)}, u32[]{:S(2)}, u32[]{:S(2)}) collective-permute-start(bf16[80,1280]{1,0:T(8,128)(2,1)S(1)} %get-tuple-element.35), channel_id=1, source_target_pairs={{0,256},{256,512},{512,768},{768,0},{1,257},{257,513},{513,769},{7... | collective-permute-start | bytes 614408 | tf_op jit(solution)/shard_map/ppermute | solution.py:215
  82.6 5.0 %collective-permute-start.7 = (bf16[80,1280]{1,0:T(8,128)(2,1)S(1)}, bf16[80,1280]{1,0:T(8,128)(2,1)S(1)}, u32[]{:S(2)}, u32[]{:S(2)}) collective-permute-start(bf16[80,1280]{1,0:T(8,128)(2,1)S(1)} %get-tuple-element.36), channel_id=1, source_target_pairs={{0,768},{256,0},{512,256},{768,512},{1,769},{257,1},{513,257},{769... | collective-permute-start | bytes 614408 | tf_op jit(solution)/shard_map/ppermute | solution.py:215
  87.5 0.0 all-to-all-done.1
  87.6 0.1 reshape.23.parts
  87.6 0.0 copy-done.3
  87.6 3.5 %shard_map.86 = (bf16[256,1280]{1,0:T(8,128)(2,1)}, bf16[256,1280]{1,0:T(8,128)(2,1)}, f32[8,128]{1,0:T(8,128)S(1)}) custom-call(bf16[256,1280]{1,0:T(8,128)(2,1)} %bitcast.10, bf16[256,1280]{1,0:T(8,128)(2,1)} %bitcast.12, bf16[8,1280]{1,0:T(8,128)(2,1)S(1)} %bitcast.8, bf16[64,1280]{1,0:T(8,128)(2,1)S(1)} %reshape.23.parts, ...), custom_call_target="tpu_custom_call" | custom-call | flops 30000000 | bytes 3000000 | tf_op jit(solution)/shard_map/pallas_call | solution.py:218
  91.1 0.0 collective-permute-done.5.a
  91.2 3.4 %collective-permute-done.6.b = bf16[80,1280]{1,0:T(8,128)(2,1)S(1)} collective-permute-done((bf16[80,1280]{1,0:T(8,128)(2,1)S(1)}, bf16[80,1280]{1,0:T(8,128)(2,1)S(1)}, u32[]{:S(2)}, u32[]{:S(2)}) %collective-permute-start.6) | collective-permute-done | bytes 204832 | tf_op jit(solution)/shard_map/ppermute | solution.py:215
  94.6 5.0 %collective-permute-done.7.c = bf16[80,1280]{1,0:T(8,128)(2,1)S(1)} collective-permute-done((bf16[80,1280]{1,0:T(8,128)(2,1)S(1)}, bf16[80,1280]{1,0:T(8,128)(2,1)S(1)}, u32[]{:S(2)}, u32[]{:S(2)}) %collective-permute-start.7) | collective-permute-done | bytes 204832 | tf_op jit(solution)/shard_map/ppermute | solution.py:215
  99.5 0.8 shard_map.88
  (1 shorter events, 0.0 us)
Async XLA Ops:
  0.6 49.2 %copy-start = (bf16[1280,640]{1,0:T(8,128)(2,1)S(1)}, bf16[1280,640]{1,0:T(8,128)(2,1)}, u32[]{:S(2)}) copy-start(bf16[1280,640]{1,0:T(8,128)(2,1)} %w_in.1) | copy-start | bytes 4915204
  0.6 0.9 copy-start.2
  43.7 6.2 %collective-permute-start = (bf16[64,1280]{1,0:T(8,128)(2,1)S(1)}, bf16[64,1280]{1,0:T(8,128)(2,1)S(1)}, u32[]{:S(2)}, u32[]{:S(2)}) collective-permute-start(bf16[64,1280]{1,0:T(8,128)(2,1)S(1)} %reshape.21.own), channel_id=1, source_target_pairs={{0,1},{1,0},{2,3},{3,2},{4,5},{5,4},{6,7},{7,6},{8,9},{9,8},{10,11... | collective-permute-start | bytes 491528 | tf_op jit(solution)/shard_map/ppermute | solution.py:191
  49.9 1.4 %copy-start.1 = (bf16[1280,640]{1,0:T(8,128)(2,1)S(1)}, bf16[1280,640]{1,0:T(8,128)(2,1)}, u32[]{:S(2)}) copy-start(bf16[1280,640]{1,0:T(8,128)(2,1)} %w_out.1) | copy-start | bytes 4915204
  53.9 10.7 %collective-permute-start.1 = (bf16[64,1280]{1,0:T(8,128)(2,1)S(1)}, bf16[64,1280]{1,0:T(8,128)(2,1)S(1)}, u32[]{:S(2)}, u32[]{:S(2)}) collective-permute-start(bf16[64,1280]{1,0:T(8,128)(2,1)S(1)} %get-tuple-element.24), channel_id=1, source_target_pairs={{0,1},{1,0},{2,3},{3,2},{4,5},{5,4},{6,7},{7,6},{8,9},{9,8},{10,11... | collective-permute-start | bytes 491528 | tf_op jit(solution)/shard_map/ppermute | solution.py:200
  56.1 13.1 %collective-permute-start.2 = (bf16[192,640]{1,0:T(8,128)(2,1)S(1)}, bf16[192,640]{1,0:T(8,128)(2,1)S(1)}, u32[]{:S(2)}, u32[]{:S(2)}) collective-permute-start(bf16[192,640]{1,0:T(8,128)(2,1)S(1)} %get-tuple-element.30), channel_id=1, source_target_pairs={{0,192},{64,128},{128,64},{192,0},{1,193},{65,129},{129,65},{193,1... | collective-permute-start | bytes 737288 | tf_op jit(solution)/shard_map/ppermute | solution.py:203
  59.4 12.7 %collective-permute-start.3 = (bf16[192,640]{1,0:T(8,128)(2,1)S(1)}, bf16[192,640]{1,0:T(8,128)(2,1)S(1)}, u32[]{:S(2)}, u32[]{:S(2)}) collective-permute-start(bf16[192,640]{1,0:T(8,128)(2,1)S(1)} %get-tuple-element.31), channel_id=1, source_target_pairs={{0,64},{64,0},{128,192},{192,128},{1,65},{65,1},{129,193},{193,129... | collective-permute-start | bytes 737288 | tf_op jit(solution)/shard_map/ppermute | solution.py:203
  62.4 9.6 %collective-permute-start.4 = (bf16[192,640]{1,0:T(8,128)(2,1)S(1)}, bf16[192,640]{1,0:T(8,128)(2,1)S(1)}, u32[]{:S(2)}, u32[]{:S(2)}) collective-permute-start(bf16[192,640]{1,0:T(8,128)(2,1)S(1)} %get-tuple-element.32), channel_id=1, source_target_pairs={{0,128},{64,192},{128,0},{192,64},{1,129},{65,193},{129,1},{193,65... | collective-permute-start | bytes 737288 | tf_op jit(solution)/shard_map/ppermute | solution.py:203
  65.3 22.2 %all-to-all-start.1 = ((bf16[32,2,1280]{2,1,0:T(2,128)(2,1)}), bf16[32,2,1280]{2,1,0:T(2,128)(2,1)S(1)}, u32[]{:S(2)}, u32[]{:S(2)}) async-start(bf16[32,2,1280]{2,1,0:T(2,128)(2,1)} %reshape.22), calls=%async_computation.1 | async-start | bytes 327680 | tf_op jit(solution)/shard_map/all_to_all | solution.py:186
  72.1 15.5 %copy-start.3 = (bf16[1280,8]{0,1:T(8,128)(2,1)S(1)}, bf16[1280,8]{0,1:T(8,128)(2,1)}, u32[]{:S(2)}) copy-start(bf16[1280,8]{0,1:T(8,128)(2,1)} %param.7) | copy-start | bytes 61444
  72.7 18.5 %collective-permute-start.5 = (bf16[80,1280]{1,0:T(8,128)(2,1)S(1)}, bf16[80,1280]{1,0:T(8,128)(2,1)S(1)}, u32[]{:S(2)}, u32[]{:S(2)}) collective-permute-start(bf16[80,1280]{1,0:T(8,128)(2,1)S(1)} %get-tuple-element.34), channel_id=1, source_target_pairs={{0,512},{256,768},{512,0},{768,256},{1,513},{257,769},{513,1},{769... | collective-permute-start | bytes 614408 | tf_op jit(solution)/shard_map/ppermute | solution.py:215
  80.1 14.4 %collective-permute-start.6 = (bf16[80,1280]{1,0:T(8,128)(2,1)S(1)}, bf16[80,1280]{1,0:T(8,128)(2,1)S(1)}, u32[]{:S(2)}, u32[]{:S(2)}) collective-permute-start(bf16[80,1280]{1,0:T(8,128)(2,1)S(1)} %get-tuple-element.35), channel_id=1, source_target_pairs={{0,256},{256,512},{512,768},{768,0},{1,257},{257,513},{513,769},{7... | collective-permute-start | bytes 614408 | tf_op jit(solution)/shard_map/ppermute | solution.py:215
  82.6 17.0 %collective-permute-start.7 = (bf16[80,1280]{1,0:T(8,128)(2,1)S(1)}, bf16[80,1280]{1,0:T(8,128)(2,1)S(1)}, u32[]{:S(2)}, u32[]{:S(2)}) collective-permute-start(bf16[80,1280]{1,0:T(8,128)(2,1)S(1)} %get-tuple-element.36), channel_id=1, source_target_pairs={{0,768},{256,0},{512,256},{768,512},{1,769},{257,1},{513,257},{769... | collective-permute-start | bytes 614408 | tf_op jit(solution)/shard_map/ppermute | solution.py:215

commit v7 on v6

--- a/solution.py
+++ b/solution.py
@@ -14,12 +14,14 @@
 f32 = jnp.float32
 bf16 = jnp.bfloat16
 
-AXES = ("yh", "yl", "xl", "xh", "zh", "zl", "c")
-SIZES = (4, 2, 2, 2, 4, 4, 2)
-DP = ("yh", "yl", "xl")
+AXES = ("ya", "yb", "xl", "xh", "zh", "zl", "c")
+SIZES = (2, 4, 2, 2, 4, 4, 2)
+DP = ("ya", "yb", "xl")
+Y, ROWS = ("ya", "yb"), 8
+STEPS = (0, 2, 1, 7)
 PEERS = ("xh", "zh", "zl", "c")
 CHIPS = ("xh", "zh", "zl")
-QUAD = ("yl", "xl")
+QUAD = ("ya", "xl")
 EXPERTS, SPREAD, CHIP_COUNT = 8, 4, 32
 QUADS = 4
 PIECES = 4
@@ -110,15 +112,15 @@
     part_other[...] = (tn(even, out_part[n:]) + tn(odd, grad_part[n:])).astype(bf16)
     both = jnp.concatenate([rows_in, rows_grad], axis=0)
     turned[...] = jnp.transpose(both.astype(f32)).astype(bf16)
-    yh, j0 = place[0], place[1]
+    y, xl = place[0], place[1]
     depth = turned.shape[0] // 16
     for m, chunk in enumerate((c0, c1, c2, c3)):
         chunk[0 : 2 * n, :] = gp
         chunk[2 * n : 4 * n, :] = act
-        j = jnp.bitwise_xor(j0, m)
+        there = jnp.bitwise_xor(y, 4 * (m // 2)), jnp.bitwise_xor(xl, m % 2)
         pieces = []
-        for k in range(4):
-            at = (lax.rem(yh + k, 4) * QUADS + j) * depth
+        for k in STEPS:
+            at = (jnp.bitwise_and(there[0] + k, ROWS - 1) * 2 + there[1]) * depth
             pieces.append(turned[pl.ds(pl.multiple_of(at, 16), depth), :])
         piece = jnp.concatenate(pieces, axis=0)
         for b in range(5):
@@ -189,7 +191,7 @@
     swap = [(0, 1), (1, 0)]
     own = exchange(send)
     other = lax.ppermute(own, "c", swap)
-    place = jnp.stack([lax.axis_index("yh"), lax.axis_index(QUAD)]).astype(jnp.int32)
+    place = jnp.stack([lax.axis_index(Y), lax.axis_index("xl")]).astype(jnp.int32)
     chunk_shape = ((192, hidden), bf16)
     part_own, part_other, c0, c1, c2, c3 = call(
         expert_kernel,
@@ -199,7 +201,7 @@
 
     back = lax.ppermute(part_other, "c", swap)
     got = [c0]
-    for m, chunk in ((3, c3), (1, c1), (2, c2)):
+    for m, chunk in ((3, c3), (2, c2), (1, c1)):
         got.append(lax.ppermute(chunk, QUAD, [(i, i ^ m) for i in range(QUADS)]))
     returned = (part_own.astype(f32) + back.astype(f32)).astype(bf16)
     parts = exchange(returned)
@@ -212,7 +214,7 @@
         12 * 10**9, 2500000, "vvvva",
     )(*got, returned)
     shares = [
-        lax.ppermute(s, "yh", [(i, (i + k) % 4) for i in range(4)]) for k, s in ((2, s2), (1, s1), (3, s3))
+        lax.ppermute(s, Y, [(i, (i + k) % ROWS) for i in range(ROWS)]) for k, s in zip(STEPS[1:], (s1, s2, s3))
     ]
 
     mixed, grad_tokens, done = call(

time: 101 us -> 106 us (1.050)
  starting transfers between devices: 34.5 us -> 39.7 us
    ppermute x3, waiting for transfers between devices: 2.88 us -> 7.12 us  [per_device(): got.append(lax.ppermute(chunk, QUAD, [(i, i ^ m) for i in range(QUADS)]))]
    ppermute x3, starting transfers between devices: 8.37 us -> 12.5 us  [per_device(): got.append(lax.ppermute(chunk, QUAD, [(i, i ^ m) for i in range(QUADS)]))]
    ppermute x3, waiting for transfers between devices: 8.38 us -> 4.39 us  [per_device(): lax.ppermute(s, Y, [(i, (i + k) % ROWS) for i in range(ROWS)])]
    ppermute x3, starting transfers between devices: 14.8 us -> 15.9 us  [per_device(): lax.ppermute(s, Y, [(i, (i + k) % ROWS) for i in range(ROWS)])]
  transfers between devices with their start and end apart: 9 -> 9, of which waited for: 4 -> 3; matrix products, arithmetic and copies ran while one was open for 1% -> 1% of each run, Pallas kernels for 4% -> 4%
where the time goes in v7:
time: 106 us
  starting transfers between devices  39.7 us (37%)
  blocking collectives  39.5 us (37%)
  waiting for transfers between devices  12.4 us (12%)
  Pallas kernels  9.95 us (9%)
  local copies, waits for them, and re-layouts  3.21 us (3%)
    all_to_all x1, blocking collectives, exchange(): lax.all_to_all(rows.reshape(CHIP_COUNT, 2, width), CHIPS, 0, 0, tiled=True)  39.5 us
    ppermute x3, starting transfers between devices, per_device(): lax.ppermute(s, Y, [(i, (i + k) % ROWS) for i in range(ROWS)])  15.9 us
    ppermute x3, starting transfers between devices, per_device(): got.append(lax.ppermute(chunk, QUAD, [(i, i ^ m) for i in range(QUADS)]))  12.5 us
    ppermute x3, waiting for transfers between devices, per_device(): got.append(lax.ppermute(chunk, QUAD, [(i, i ^ m) for i in range(QUADS)]))  7.12 us
    ppermute x1, starting transfers between devices, per_device(): other = lax.ppermute(own, 'c', swap)  5.15 us
    ppermute x3, waiting for transfers between devices, per_device(): lax.ppermute(s, Y, [(i, (i + k) % ROWS) for i in range(ROWS)])  4.39 us
    all_to_all x1, starting transfers between devices, exchange(): lax.all_to_all(rows.reshape(CHIP_COUNT, 2, width), CHIPS, 0, 0, tiled=True)  3.87 us
    pallas_call x1, Pallas kernels, per_device(): call(finish_kernel, [((patch, width), bf16), ((patch, width), bf16), ((8,...  3.49 us
  transfers between devices with their start and end apart: 9, of which 3 were waited for; matrix products, arithmetic and copies ran while one was open for 1% of the time, Pallas kernels for 4%

profile of v7, /device:TPU:1, one launch (start us, length us, event | category | flops | bytes accessed | tf_op | source)
XLA Modules:
  0.0 105.7 jit_solution(7613031931778010951)
XLA Ops:
  0.6 0.0 copy-start
  0.6 0.0 copy-start.2
  0.7 0.8 copy-done.2
  1.5 2.5 %shard_map.84 = (bf16[64,1280]{1,0:T(8,128)(2,1)S(1)}, f32[8,256]{1,0:T(8,128)S(1)}, f32[8,256]{1,0:T(8,128)S(1)}) custom-call(bf16[256,1280]{1,0:T(8,128)(2,1)} %bitcast.9, bf16[256,1280]{1,0:T(8,128)(2,1)} %bitcast.11, bf16[8,1280]{1,0:T(8,128)(2,1)S(1)} %bitcast.7), custom_call_target="tpu_custom_call" | custom-call | flops 10000000 | bytes 1500000 | tf_op jit(solution)/shard_map/pallas_call | solution.py:179
  4.0 0.1 reshape.20
  4.1 39.5 %all_to_all.10 = bf16[32,2,1280]{2,1,0:T(2,128)(2,1)S(1)} all-to-all(bf16[32,2,1280]{2,1,0:T(2,128)(2,1)S(1)} %reshape.20), channel_id=1, replica_groups=mesh['ya'=2,'yb'=4,'xl'=2,'xh'=2,'zh'=4,'zl'=4,'c'=2] {'xh','zh','zl'}, dimensions={0} | all-to-all | bytes 327680 | tf_op jit(solution)/shard_map/all_to_all | solution.py:188
  43.6 0.1 reshape.21.own
  43.7 5.2 %collective-permute-start = (bf16[64,1280]{1,0:T(8,128)(2,1)S(1)}, bf16[64,1280]{1,0:T(8,128)(2,1)S(1)}, u32[]{:S(2)}, u32[]{:S(2)}) collective-permute-start(bf16[64,1280]{1,0:T(8,128)(2,1)S(1)} %reshape.21.own), channel_id=1, source_target_pairs={{0,1},{1,0},{2,3},{3,2},{4,5},{5,4},{6,7},{7,6},{8,9},{9,8},{10,11... | collective-permute-start | bytes 491528 | tf_op jit(solution)/shard_map/ppermute | solution.py:193
  48.9 0.1 pad_add_fusion.place
  48.9 0.9 collective-permute-done.other
  49.9 0.0 copy-done
  49.9 0.0 copy-start.1
  49.9 1.4 %copy-done.1 = bf16[1280,640]{1,0:T(8,128)(2,1)S(1)} copy-done((bf16[1280,640]{1,0:T(8,128)(2,1)S(1)}, bf16[1280,640]{1,0:T(8,128)(2,1)}, u32[]{:S(2)}) %copy-start.1) | copy-done | bytes 1638424
  51.3 2.6 %shard_map.85 = (bf16[64,1280]{1,0:T(8,128)(2,1)S(1)}, bf16[64,1280]{1,0:T(8,128)(2,1)S(1)}, bf16[192,640]{1,0:T(8,128)(2,1)S(1)}, bf16[192,640]{1,0:T(8,128)(2,...) custom-call(s32[2]{0:T(128)S(1)} %pad_add_fusion.place, bf16[64,1280]{1,0:T(8,128)(2,1)S(1)} %reshape.21.own, ...), custom_call_target="tpu_custom_call" | custom-call | flops 500000000 | bytes 4500000 | tf_op jit(solution)/shard_map/pallas_call | solution.py:196
  53.9 2.3 %collective-permute-start.1 = (bf16[64,1280]{1,0:T(8,128)(2,1)S(1)}, bf16[64,1280]{1,0:T(8,128)(2,1)S(1)}, u32[]{:S(2)}, u32[]{:S(2)}) collective-permute-start(bf16[64,1280]{1,0:T(8,128)(2,1)S(1)} %get-tuple-element.24), channel_id=1, source_target_pairs={{0,1},{1,0},{2,3},{3,2},{4,5},{5,4},{6,7},{7,6},{8,9},{9,8},{10,11... | collective-permute-start | bytes 491528 | tf_op jit(solution)/shard_map/ppermute | solution.py:202
  56.1 7.5 %collective-permute-start.2 = (bf16[192,640]{1,0:T(8,128)(2,1)S(1)}, bf16[192,640]{1,0:T(8,128)(2,1)S(1)}, u32[]{:S(2)}, u32[]{:S(2)}) collective-permute-start(bf16[192,640]{1,0:T(8,128)(2,1)S(1)} %get-tuple-element.30), channel_id=1, source_target_pairs={{0,576},{64,512},{512,64},{576,0},{1,577},{65,513},{513,65},{577,1... | collective-permute-start | bytes 737288 | tf_op jit(solution)/shard_map/ppermute | solution.py:205
  63.6 1.9 %collective-permute-start.3 = (bf16[192,640]{1,0:T(8,128)(2,1)S(1)}, bf16[192,640]{1,0:T(8,128)(2,1)S(1)}, u32[]{:S(2)}, u32[]{:S(2)}) collective-permute-start(bf16[192,640]{1,0:T(8,128)(2,1)S(1)} %get-tuple-element.31), channel_id=1, source_target_pairs={{0,512},{64,576},{512,0},{576,64},{1,513},{65,577},{513,1},{577,65... | collective-permute-start | bytes 737288 | tf_op jit(solution)/shard_map/ppermute | solution.py:205
  65.5 3.1 %collective-permute-start.4 = (bf16[192,640]{1,0:T(8,128)(2,1)S(1)}, bf16[192,640]{1,0:T(8,128)(2,1)S(1)}, u32[]{:S(2)}, u32[]{:S(2)}) collective-permute-start(bf16[192,640]{1,0:T(8,128)(2,1)S(1)} %get-tuple-element.32), channel_id=1, source_target_pairs={{0,64},{64,0},{512,576},{576,512},{1,65},{65,1},{513,577},{577,513... | collective-permute-start | bytes 737288 | tf_op jit(solution)/shard_map/ppermute | solution.py:205
  68.6 0.0 collective-permute-done.1
  68.7 0.7 reshape.22
  69.4 3.9 %all-to-all-start.1 = ((bf16[32,2,1280]{2,1,0:T(2,128)(2,1)}), bf16[32,2,1280]{2,1,0:T(2,128)(2,1)S(1)}, u32[]{:S(2)}, u32[]{:S(2)}) async-start(bf16[32,2,1280]{2,1,0:T(2,128)(2,1)} %reshape.22), calls=%async_computation.1 | async-start | bytes 327680 | tf_op jit(solution)/shard_map/all_to_all | solution.py:188
  73.3 0.0 collective-permute-done.2.c1
  73.3 7.1 %collective-permute-done.3.c2 = bf16[192,640]{1,0:T(8,128)(2,1)S(1)} collective-permute-done((bf16[192,640]{1,0:T(8,128)(2,1)S(1)}, bf16[192,640]{1,0:T(8,128)(2,1)S(1)}, u32[]{:S(2)}, u32[]{:S(2)}) %collective-permute-start.3) | collective-permute-done | bytes 245792 | tf_op jit(solution)/shard_map/ppermute | solution.py:205
  80.4 0.0 collective-permute-done.4.c3
  80.4 0.0 copy-start.3
  80.4 0.6 shard_map.87
  81.0 9.4 %collective-permute-start.5 = (bf16[80,1280]{1,0:T(8,128)(2,1)S(1)}, bf16[80,1280]{1,0:T(8,128)(2,1)S(1)}, u32[]{:S(2)}, u32[]{:S(2)}) collective-permute-start(bf16[80,1280]{1,0:T(8,128)(2,1)S(1)} %get-tuple-element.34), channel_id=1, source_target_pairs={{0,256},{128,384},{256,512},{384,640},{512,768},{640,896},{768,0},... | collective-permute-start | bytes 614408 | tf_op jit(solution)/shard_map/ppermute | solution.py:217
  90.4 1.9 %collective-permute-start.6 = (bf16[80,1280]{1,0:T(8,128)(2,1)S(1)}, bf16[80,1280]{1,0:T(8,128)(2,1)S(1)}, u32[]{:S(2)}, u32[]{:S(2)}) collective-permute-start(bf16[80,1280]{1,0:T(8,128)(2,1)S(1)} %get-tuple-element.35), channel_id=1, source_target_pairs={{0,128},{128,256},{256,384},{384,512},{512,640},{640,768},{768,896... | collective-permute-start | bytes 614408 | tf_op jit(solution)/shard_map/ppermute | solution.py:217
  92.4 4.6 %collective-permute-start.7 = (bf16[80,1280]{1,0:T(8,128)(2,1)S(1)}, bf16[80,1280]{1,0:T(8,128)(2,1)S(1)}, u32[]{:S(2)}, u32[]{:S(2)}) collective-permute-start(bf16[80,1280]{1,0:T(8,128)(2,1)S(1)} %get-tuple-element.36), channel_id=1, source_target_pairs={{0,896},{128,0},{256,128},{384,256},{512,384},{640,512},{768,640},... | collective-permute-start | bytes 614408 | tf_op jit(solution)/shard_map/ppermute | solution.py:217
  96.9 0.0 all-to-all-done.1
  97.0 0.1 reshape.23.parts
  97.0 0.0 copy-done.3
  97.0 3.5 %shard_map.86 = (bf16[256,1280]{1,0:T(8,128)(2,1)}, bf16[256,1280]{1,0:T(8,128)(2,1)}, f32[8,128]{1,0:T(8,128)S(1)}) custom-call(bf16[256,1280]{1,0:T(8,128)(2,1)} %bitcast.10, bf16[256,1280]{1,0:T(8,128)(2,1)} %bitcast.12, bf16[8,1280]{1,0:T(8,128)(2,1)S(1)} %bitcast.8, bf16[64,1280]{1,0:T(8,128)(2,1)S(1)} %reshape.23.parts, ...), custom_call_target="tpu_custom_call" | custom-call | flops 30000000 | bytes 3000000 | tf_op jit(solution)/shard_map/pallas_call | solution.py:220
  100.5 0.0 collective-permute-done.5.a
  100.5 4.4 %collective-permute-done.6.b = bf16[80,1280]{1,0:T(8,128)(2,1)S(1)} collective-permute-done((bf16[80,1280]{1,0:T(8,128)(2,1)S(1)}, bf16[80,1280]{1,0:T(8,128)(2,1)S(1)}, u32[]{:S(2)}, u32[]{:S(2)}) %collective-permute-start.6) | collective-permute-done | bytes 204832 | tf_op jit(solution)/shard_map/ppermute | solution.py:217
  104.9 0.0 collective-permute-done.7.c
  104.9 0.8 shard_map.88
  (1 shorter events, 0.0 us)
Async XLA Ops:
  0.6 49.2 %copy-start = (bf16[1280,640]{1,0:T(8,128)(2,1)S(1)}, bf16[1280,640]{1,0:T(8,128)(2,1)}, u32[]{:S(2)}) copy-start(bf16[1280,640]{1,0:T(8,128)(2,1)} %w_in.1) | copy-start | bytes 4915204
  0.6 0.9 copy-start.2
  43.7 6.2 %collective-permute-start = (bf16[64,1280]{1,0:T(8,128)(2,1)S(1)}, bf16[64,1280]{1,0:T(8,128)(2,1)S(1)}, u32[]{:S(2)}, u32[]{:S(2)}) collective-permute-start(bf16[64,1280]{1,0:T(8,128)(2,1)S(1)} %reshape.21.own), channel_id=1, source_target_pairs={{0,1},{1,0},{2,3},{3,2},{4,5},{5,4},{6,7},{7,6},{8,9},{9,8},{10,11... | collective-permute-start | bytes 491528 | tf_op jit(solution)/shard_map/ppermute | solution.py:193
  49.9 1.4 %copy-start.1 = (bf16[1280,640]{1,0:T(8,128)(2,1)S(1)}, bf16[1280,640]{1,0:T(8,128)(2,1)}, u32[]{:S(2)}) copy-start(bf16[1280,640]{1,0:T(8,128)(2,1)} %w_out.1) | copy-start | bytes 4915204
  53.9 14.8 %collective-permute-start.1 = (bf16[64,1280]{1,0:T(8,128)(2,1)S(1)}, bf16[64,1280]{1,0:T(8,128)(2,1)S(1)}, u32[]{:S(2)}, u32[]{:S(2)}) collective-permute-start(bf16[64,1280]{1,0:T(8,128)(2,1)S(1)} %get-tuple-element.24), channel_id=1, source_target_pairs={{0,1},{1,0},{2,3},{3,2},{4,5},{5,4},{6,7},{7,6},{8,9},{9,8},{10,11... | collective-permute-start | bytes 491528 | tf_op jit(solution)/shard_map/ppermute | solution.py:202
  56.1 17.1 %collective-permute-start.2 = (bf16[192,640]{1,0:T(8,128)(2,1)S(1)}, bf16[192,640]{1,0:T(8,128)(2,1)S(1)}, u32[]{:S(2)}, u32[]{:S(2)}) collective-permute-start(bf16[192,640]{1,0:T(8,128)(2,1)S(1)} %get-tuple-element.30), channel_id=1, source_target_pairs={{0,576},{64,512},{512,64},{576,0},{1,577},{65,513},{513,65},{577,1... | collective-permute-start | bytes 737288 | tf_op jit(solution)/shard_map/ppermute | solution.py:205
  63.6 16.8 %collective-permute-start.3 = (bf16[192,640]{1,0:T(8,128)(2,1)S(1)}, bf16[192,640]{1,0:T(8,128)(2,1)S(1)}, u32[]{:S(2)}, u32[]{:S(2)}) collective-permute-start(bf16[192,640]{1,0:T(8,128)(2,1)S(1)} %get-tuple-element.31), channel_id=1, source_target_pairs={{0,512},{64,576},{512,0},{576,64},{1,513},{65,577},{513,1},{577,65... | collective-permute-start | bytes 737288 | tf_op jit(solution)/shard_map/ppermute | solution.py:205
  65.5 14.9 %collective-permute-start.4 = (bf16[192,640]{1,0:T(8,128)(2,1)S(1)}, bf16[192,640]{1,0:T(8,128)(2,1)S(1)}, u32[]{:S(2)}, u32[]{:S(2)}) collective-permute-start(bf16[192,640]{1,0:T(8,128)(2,1)S(1)} %get-tuple-element.32), channel_id=1, source_target_pairs={{0,64},{64,0},{512,576},{576,512},{1,65},{65,1},{513,577},{577,513... | collective-permute-start | bytes 737288 | tf_op jit(solution)/shard_map/ppermute | solution.py:205
  69.4 27.5 %all-to-all-start.1 = ((bf16[32,2,1280]{2,1,0:T(2,128)(2,1)}), bf16[32,2,1280]{2,1,0:T(2,128)(2,1)S(1)}, u32[]{:S(2)}, u32[]{:S(2)}) async-start(bf16[32,2,1280]{2,1,0:T(2,128)(2,1)} %reshape.22), calls=%async_computation.1 | async-start | bytes 327680 | tf_op jit(solution)/shard_map/all_to_all | solution.py:188
  80.4 16.6 %copy-start.3 = (bf16[1280,8]{0,1:T(8,128)(2,1)S(1)}, bf16[1280,8]{0,1:T(8,128)(2,1)}, u32[]{:S(2)}) copy-start(bf16[1280,8]{0,1:T(8,128)(2,1)} %param.7) | copy-start | bytes 61444
  81.0 19.5 %collective-permute-start.5 = (bf16[80,1280]{1,0:T(8,128)(2,1)S(1)}, bf16[80,1280]{1,0:T(8,128)(2,1)S(1)}, u32[]{:S(2)}, u32[]{:S(2)}) collective-permute-start(bf16[80,1280]{1,0:T(8,128)(2,1)S(1)} %get-tuple-element.34), channel_id=1, source_target_pairs={{0,256},{128,384},{256,512},{384,640},{512,768},{640,896},{768,0},... | collective-permute-start | bytes 614408 | tf_op jit(solution)/shard_map/ppermute | solution.py:217
  90.4 14.5 %collective-permute-start.6 = (bf16[80,1280]{1,0:T(8,128)(2,1)S(1)}, bf16[80,1280]{1,0:T(8,128)(2,1)S(1)}, u32[]{:S(2)}, u32[]{:S(2)}) collective-permute-start(bf16[80,1280]{1,0:T(8,128)(2,1)S(1)} %get-tuple-element.35), channel_id=1, source_target_pairs={{0,128},{128,256},{256,384},{384,512},{512,640},{640,768},{768,896... | collective-permute-start | bytes 614408 | tf_op jit(solution)/shard_map/ppermute | solution.py:217
  92.4 12.6 %collective-permute-start.7 = (bf16[80,1280]{1,0:T(8,128)(2,1)S(1)}, bf16[80,1280]{1,0:T(8,128)(2,1)S(1)}, u32[]{:S(2)}, u32[]{:S(2)}) collective-permute-start(bf16[80,1280]{1,0:T(8,128)(2,1)S(1)} %get-tuple-element.36), channel_id=1, source_target_pairs={{0,896},{128,0},{256,128},{384,256},{512,384},{640,512},{768,640},... | collective-permute-start | bytes 614408 | tf_op jit(solution)/shard_map/ppermute | solution.py:217

commit v8 on v6

--- a/solution.py
+++ b/solution.py
@@ -14,11 +14,13 @@
 f32 = jnp.float32
 bf16 = jnp.bfloat16
 
-AXES = ("yh", "yl", "xl", "xh", "zh", "zl", "c")
-SIZES = (4, 2, 2, 2, 4, 4, 2)
+AXES = ("yh", "yl", "xl", "xh", "zh", "zu", "zv", "c")
+SIZES = (4, 2, 2, 2, 4, 2, 2, 2)
 DP = ("yh", "yl", "xl")
-PEERS = ("xh", "zh", "zl", "c")
-CHIPS = ("xh", "zh", "zl")
+PEERS = ("xh", "zh", "zu", "zv", "c")
+CHIPS = ("xh", "zh", "zu", "zv")
+PAIRS, NEAR = ("xh", "zh", "zu"), ("zv", "c")
+PAIR_COUNT = 16
 QUAD = ("yl", "xl")
 EXPERTS, SPREAD, CHIP_COUNT = 8, 4, 32
 QUADS = 4
@@ -87,17 +89,25 @@
         copy.wait()
     slot_grad = nn(c.astype(bf16), cot[...]).astype(bf16)
     both = jnp.concatenate([slot_in.astype(f32), slot_grad.astype(f32)], axis=0).astype(bf16)
-    rows = 2 * CHIP_COUNT
-    sel = pick(rows, 16, lambda r: (r % 2) * EXPERTS + r // (2 * SPREAD))
+    rows = 2 * PAIR_COUNT
+    sel = pick(rows, 16, lambda r: (r % 2) * EXPERTS + r // 4)
     send[...] = nn(sel, both).astype(bf16)
 
 
-def expert_kernel(place, own, other, w_in, w_out, part_own, part_other, c0, c1, c2, c3, turned):
-    n = own.shape[0] // 2
+def expert_kernel(place, rows, w_in, w_out, part_own, part_other, c0, c1, c2, c3, turned):
+    n = rows.shape[0] // 4
     even = pick(n, 2 * n, lambda r: 2 * r)
     odd = pick(n, 2 * n, lambda r: 2 * r + 1)
-    rows_in = jnp.concatenate([nn(even, own[...]), nn(even, other[...])], axis=0).astype(bf16)
-    rows_grad = jnp.concatenate([nn(odd, own[...]), nn(odd, other[...])], axis=0).astype(bf16)
+    take_in = pick(n, 2 * n, lambda r: (r % 2) * n + (r // 2) * 2)
+    take_grad = pick(n, 2 * n, lambda r: (r % 2) * n + (r // 2) * 2 + 1)
+
+    def of_core(core):
+        at = pl.multiple_of(core * n, n)
+        return jnp.concatenate([rows[pl.ds(at, n), :], rows[pl.ds(2 * n + at, n), :]], axis=0)
+
+    own, other = of_core(place[2]), of_core(1 - place[2])
+    rows_in = jnp.concatenate([nn(take_in, own), nn(take_in, other)], axis=0).astype(bf16)
+    rows_grad = jnp.concatenate([nn(take_grad, own), nn(take_grad, other)], axis=0).astype(bf16)
     preact = nn(rows_in, w_in[...])
     hidden_grad = nn(rows_grad, w_out[...])
     cumulative = 0.5 * (1.0 + lax.erf(preact * root_half))
@@ -176,7 +186,7 @@
     n2 = 2 * CHIP_COUNT
     send, disp, comb = call(
         route_kernel,
-        [((n2, width), bf16), ((EXPERTS, patch), f32), ((EXPERTS, patch), f32)],
+        [((2 * PAIR_COUNT, width), bf16), ((EXPERTS, patch), f32), ((EXPERTS, patch), f32)],
         10**7, 1500000, "hhv",
         [pltpu.VMEM((patch, width), bf16)] * 2 + [pltpu.SemaphoreType.DMA((2, PIECES))],
         56_000_000,
@@ -187,15 +197,15 @@
         return got.reshape(n2, width)
 
     swap = [(0, 1), (1, 0)]
-    own = exchange(send)
-    other = lax.ppermute(own, "c", swap)
-    place = jnp.stack([lax.axis_index("yh"), lax.axis_index(QUAD)]).astype(jnp.int32)
+    part = lax.all_to_all(send.reshape(PAIR_COUNT, 2, width), PAIRS, 0, 0, tiled=True)
+    rows = lax.all_gather(part.reshape(2 * PAIR_COUNT, width), NEAR, tiled=True)
+    place = jnp.stack([lax.axis_index("yh"), lax.axis_index(QUAD), lax.axis_index("c")]).astype(jnp.int32)
     chunk_shape = ((192, hidden), bf16)
     part_own, part_other, c0, c1, c2, c3 = call(
         expert_kernel,
         [((n2, width), bf16), ((n2, width), bf16)] + [chunk_shape] * 4,
-        5 * 10**8, 4500000, "svvvv", [pltpu.VMEM((width, 128), bf16)],
-    )(place, own, other, in_weight, out_weight)
+        5 * 10**8, 4500000, "svvv", [pltpu.VMEM((width, 128), bf16)],
+    )(place, rows, in_weight, out_weight)
 
     back = lax.ppermute(part_other, "c", swap)
     got = [c0]

time: 101 us -> 99.3 us (0.983)
  blocking collectives: 39.5 us -> 8.07 us
  starting transfers between devices: 34.5 us -> 51.2 us
  waiting for transfers between devices: 12.2 us -> 24.8 us
    all_to_all x1 -> x0, blocking collectives: 39.5 us -> none  [exchange(): lax.all_to_all(rows.reshape(CHIP_COUNT, 2, width), CHIPS, 0, 0, tiled=True)]
    all_to_all x0 -> x1, starting transfers between devices: none -> 21.9 us  [per_device(): lax.all_to_all(send.reshape(PAIR_COUNT, 2, width), PAIRS, 0, 0, tiled=True)]
    all_to_all x0 -> x1, waiting for transfers between devices: none -> 13.7 us  [per_device(): lax.all_to_all(send.reshape(PAIR_COUNT, 2, width), PAIRS, 0, 0, tiled=True)]
    all_gather x0 -> x1, blocking collectives: none -> 8.07 us  [per_device(): rows = lax.all_gather(part.reshape(2 * PAIR_COUNT, width), NEAR, tiled=True)]
    ppermute x1 -> x0, starting transfers between devices: 5.15 us -> none  [per_device(): other = lax.ppermute(own, 'c', swap)]
where the time goes in v8:
time: 99.3 us; the launch traced here: 98.7 us
  starting transfers between devices  51.2 us (52%)
  waiting for transfers between devices  24.8 us (25%)
  Pallas kernels  9.97 us (10%)
  blocking collectives  8.07 us (8%)
  local copies, waits for them, and re-layouts  3.78 us (4%)
    all_to_all x1, starting transfers between devices, per_device(): lax.all_to_all(send.reshape(PAIR_COUNT, 2, width), PAIRS, 0, 0, tiled=True)  21.9 us
    ppermute x3, starting transfers between devices, per_device(): lax.ppermute(s, 'yh', [(i, (i + k) % 4) for i in range(4)])  14.8 us
    all_to_all x1, waiting for transfers between devices, per_device(): lax.all_to_all(send.reshape(PAIR_COUNT, 2, width), PAIRS, 0, 0, tiled=True)  13.7 us
    ppermute x3, waiting for transfers between devices, per_device(): lax.ppermute(s, 'yh', [(i, (i + k) % 4) for i in range(4)])  8.4 us
    ppermute x3, starting transfers between devices, per_device(): got.append(lax.ppermute(chunk, QUAD, [(i, i ^ m) for i in range(QUADS)]))  8.37 us
    all_gather x1, blocking collectives, per_device(): rows = lax.all_gather(part.reshape(2 * PAIR_COUNT, width), NEAR, tiled=True)  8.07 us
    all_to_all x1, starting transfers between devices, exchange(): lax.all_to_all(rows.reshape(CHIP_COUNT, 2, width), CHIPS, 0, 0, tiled=True)  4.02 us
    pallas_call x1, Pallas kernels, per_device(): call(finish_kernel, [((patch, width), bf16), ((patch, width), bf16), ((8,...  3.49 us
  transfers between devices with their start and end apart: 9, of which 4 were waited for; matrix products, arithmetic and copies ran while one was open for 1% of the time, Pallas kernels for 4%

profile of v8, /device:TPU:1, one launch (start us, length us, event | category | flops | bytes accessed | tf_op | source)
XLA Modules:
  0.0 98.7 jit_solution(15312642095795902627)
XLA Ops:
  0.6 0.0 copy-start
  0.6 0.0 copy-start.2
  0.7 0.8 copy-done.2
  1.5 2.5 %shard_map.84 = (bf16[32,1280]{1,0:T(8,128)(2,1)S(1)}, f32[8,256]{1,0:T(8,128)S(1)}, f32[8,256]{1,0:T(8,128)S(1)}) custom-call(bf16[256,1280]{1,0:T(8,128)(2,1)} %bitcast.10, bf16[256,1280]{1,0:T(8,128)(2,1)} %bitcast.12, bf16[8,1280]{1,0:T(8,128)(2,1)S(1)} %bitcast.8), custom_call_target="tpu_custom_call" | custom-call | flops 10000000 | bytes 1500000 | tf_op jit(solution)/shard_map/pallas_call | solution.py:187
  4.0 0.7 reshape.20
  4.7 21.9 %all-to-all-start = ((bf16[16,2,1280]{2,1,0:T(2,128)(2,1)}), bf16[16,2,1280]{2,1,0:T(2,128)(2,1)S(1)}, u32[]{:S(2)}, u32[]{:S(2)}) async-start(bf16[16,2,1280]{2,1,0:T(2,128)(2,1)} %reshape.20), calls=%async_computation | async-start | bytes 163840 | tf_op jit(solution)/shard_map/all_to_all | solution.py:200
  26.6 0.1 pad_add_fusion.place
  26.6 13.7 %all-to-all-done = bf16[16,2,1280]{2,1,0:T(2,128)(2,1)S(1)} async-done(((bf16[16,2,1280]{2,1,0:T(2,128)(2,1)}), bf16[16,2,1280]{2,1,0:T(2,128)(2,1)S(1)}, u32[]{:S(2)}, u32[]{:S(2)}) %all-to-all-start) | async-done | bytes 81952 | tf_op jit(solution)/shard_map/all_to_all | solution.py:200
  40.3 8.1 %all_gather.3.rows = bf16[128,1280]{1,0:T(8,128)(2,1)S(1)} all-gather(bf16[32,1280]{1,0:T(8,128)(2,1)S(1)} %reshape.21), channel_id=1, replica_groups=mesh['yh'=4,'yl'=2,'xl'=2,'xh'=2,'zh'=4,'zu'=2,'zv'=2,'c'=2] {'zv','c'}, dimensions={0}, use_global_device_ids=true | all-gather | bytes 409600 | tf_op jit(solution)/shard_map/all_gather | solution.py:201
  48.4 0.0 copy-done
  48.4 0.0 copy-start.1
  48.4 1.4 %copy-done.1 = bf16[1280,640]{1,0:T(8,128)(2,1)S(1)} copy-done((bf16[1280,640]{1,0:T(8,128)(2,1)S(1)}, bf16[1280,640]{1,0:T(8,128)(2,1)}, u32[]{:S(2)}) %copy-start.1) | copy-done | bytes 1638424
  49.8 2.6 %shard_map.85 = (bf16[64,1280]{1,0:T(8,128)(2,1)S(1)}, bf16[64,1280]{1,0:T(8,128)(2,1)S(1)}, bf16[192,640]{1,0:T(8,128)(2,1)S(1)}, bf16[192,640]{1,0:T(8,128)(2,...) custom-call(s32[3]{0:T(128)S(1)} %pad_add_fusion.place, bf16[128,1280]{1,0:T(8,128)(2,1)S(1)} %all_gather.3.rows, ...), custom_call_target="tpu_custom_call" | custom-call | flops 500000000 | bytes 4500000 | tf_op jit(solution)/shard_map/pallas_call | solution.py:204
  52.4 2.1 %collective-permute-start = (bf16[64,1280]{1,0:T(8,128)(2,1)S(1)}, bf16[64,1280]{1,0:T(8,128)(2,1)S(1)}, u32[]{:S(2)}, u32[]{:S(2)}) collective-permute-start(bf16[64,1280]{1,0:T(8,128)(2,1)S(1)} %get-tuple-element.24), channel_id=1, source_target_pairs={{0,1},{1,0},{2,3},{3,2},{4,5},{5,4},{6,7},{7,6},{8,9},{9,8},{10,11... | collective-permute-start | bytes 491528 | tf_op jit(solution)/shard_map/ppermute | solution.py:210
  54.5 3.2 %collective-permute-start.1 = (bf16[192,640]{1,0:T(8,128)(2,1)S(1)}, bf16[192,640]{1,0:T(8,128)(2,1)S(1)}, u32[]{:S(2)}, u32[]{:S(2)}) collective-permute-start(bf16[192,640]{1,0:T(8,128)(2,1)S(1)} %get-tuple-element.30), channel_id=1, source_target_pairs={{0,192},{64,128},{128,64},{192,0},{1,193},{65,129},{129,65},{193,1... | collective-permute-start | bytes 737288 | tf_op jit(solution)/shard_map/ppermute | solution.py:213
  57.7 3.1 %collective-permute-start.2 = (bf16[192,640]{1,0:T(8,128)(2,1)S(1)}, bf16[192,640]{1,0:T(8,128)(2,1)S(1)}, u32[]{:S(2)}, u32[]{:S(2)}) collective-permute-start(bf16[192,640]{1,0:T(8,128)(2,1)S(1)} %get-tuple-element.31), channel_id=1, source_target_pairs={{0,64},{64,0},{128,192},{192,128},{1,65},{65,1},{129,193},{193,129... | collective-permute-start | bytes 737288 | tf_op jit(solution)/shard_map/ppermute | solution.py:213
  60.8 2.1 %collective-permute-start.3 = (bf16[192,640]{1,0:T(8,128)(2,1)S(1)}, bf16[192,640]{1,0:T(8,128)(2,1)S(1)}, u32[]{:S(2)}, u32[]{:S(2)}) collective-permute-start(bf16[192,640]{1,0:T(8,128)(2,1)S(1)} %get-tuple-element.32), channel_id=1, source_target_pairs={{0,128},{64,192},{128,0},{192,64},{1,129},{65,193},{129,1},{193,65... | collective-permute-start | bytes 737288 | tf_op jit(solution)/shard_map/ppermute | solution.py:213
  62.9 0.0 collective-permute-done
  63.0 0.7 reshape.22
  63.7 4.0 %all-to-all-start.1 = ((bf16[32,2,1280]{2,1,0:T(2,128)(2,1)}), bf16[32,2,1280]{2,1,0:T(2,128)(2,1)S(1)}, u32[]{:S(2)}, u32[]{:S(2)}) async-start(bf16[32,2,1280]{2,1,0:T(2,128)(2,1)} %reshape.22), calls=%async_computation.1 | async-start | bytes 327680 | tf_op jit(solution)/shard_map/all_to_all | solution.py:196
  67.7 0.0 collective-permute-done.1.c1
  67.7 2.7 %collective-permute-done.2.c2 = bf16[192,640]{1,0:T(8,128)(2,1)S(1)} collective-permute-done((bf16[192,640]{1,0:T(8,128)(2,1)S(1)}, bf16[192,640]{1,0:T(8,128)(2,1)S(1)}, u32[]{:S(2)}, u32[]{:S(2)}) %collective-permute-start.2) | collective-permute-done | bytes 245792 | tf_op jit(solution)/shard_map/ppermute | solution.py:213
  70.4 0.0 collective-permute-done.3.c3
  70.4 0.0 copy-start.3
  70.4 0.6 shard_map.87
  71.0 7.4 %collective-permute-start.4 = (bf16[80,1280]{1,0:T(8,128)(2,1)S(1)}, bf16[80,1280]{1,0:T(8,128)(2,1)S(1)}, u32[]{:S(2)}, u32[]{:S(2)}) collective-permute-start(bf16[80,1280]{1,0:T(8,128)(2,1)S(1)} %get-tuple-element.34), channel_id=1, source_target_pairs={{0,512},{256,768},{512,0},{768,256},{1,513},{257,769},{513,1},{769... | collective-permute-start | bytes 614408 | tf_op jit(solution)/shard_map/ppermute | solution.py:225
  78.5 2.4 %collective-permute-start.5 = (bf16[80,1280]{1,0:T(8,128)(2,1)S(1)}, bf16[80,1280]{1,0:T(8,128)(2,1)S(1)}, u32[]{:S(2)}, u32[]{:S(2)}) collective-permute-start(bf16[80,1280]{1,0:T(8,128)(2,1)S(1)} %get-tuple-element.35), channel_id=1, source_target_pairs={{0,256},{256,512},{512,768},{768,0},{1,257},{257,513},{513,769},{7... | collective-permute-start | bytes 614408 | tf_op jit(solution)/shard_map/ppermute | solution.py:225
  80.9 5.0 %collective-permute-start.6 = (bf16[80,1280]{1,0:T(8,128)(2,1)S(1)}, bf16[80,1280]{1,0:T(8,128)(2,1)S(1)}, u32[]{:S(2)}, u32[]{:S(2)}) collective-permute-start(bf16[80,1280]{1,0:T(8,128)(2,1)S(1)} %get-tuple-element.36), channel_id=1, source_target_pairs={{0,768},{256,0},{512,256},{768,512},{1,769},{257,1},{513,257},{769... | collective-permute-start | bytes 614408 | tf_op jit(solution)/shard_map/ppermute | solution.py:225
  85.9 0.0 all-to-all-done.1
  85.9 0.1 reshape.23.parts
  86.0 0.0 copy-done.3
  86.0 3.5 %shard_map.86 = (bf16[256,1280]{1,0:T(8,128)(2,1)}, bf16[256,1280]{1,0:T(8,128)(2,1)}, f32[8,128]{1,0:T(8,128)S(1)}) custom-call(bf16[256,1280]{1,0:T(8,128)(2,1)} %bitcast.11, bf16[256,1280]{1,0:T(8,128)(2,1)} %bitcast.13, bf16[8,1280]{1,0:T(8,128)(2,1)S(1)} %bitcast.9, bf16[64,1280]{1,0:T(8,128)(2,1)S(1)} %reshape.23.parts, ...), custom_call_target="tpu_custom_call" | custom-call | flops 30000000 | bytes 3000000 | tf_op jit(solution)/shard_map/pallas_call | solution.py:228
  89.5 0.0 collective-permute-done.4.a
  89.5 3.4 %collective-permute-done.5.b = bf16[80,1280]{1,0:T(8,128)(2,1)S(1)} collective-permute-done((bf16[80,1280]{1,0:T(8,128)(2,1)S(1)}, bf16[80,1280]{1,0:T(8,128)(2,1)S(1)}, u32[]{:S(2)}, u32[]{:S(2)}) %collective-permute-start.5) | collective-permute-done | bytes 204832 | tf_op jit(solution)/shard_map/ppermute | solution.py:225
  92.9 5.0 %collective-permute-done.6.c = bf16[80,1280]{1,0:T(8,128)(2,1)S(1)} collective-permute-done((bf16[80,1280]{1,0:T(8,128)(2,1)S(1)}, bf16[80,1280]{1,0:T(8,128)(2,1)S(1)}, u32[]{:S(2)}, u32[]{:S(2)}) %collective-permute-start.6) | collective-permute-done | bytes 204832 | tf_op jit(solution)/shard_map/ppermute | solution.py:225
  97.9 0.8 shard_map.88
  (2 shorter events, 0.1 us)
Async XLA Ops:
  0.6 47.8 %copy-start = (bf16[1280,640]{1,0:T(8,128)(2,1)S(1)}, bf16[1280,640]{1,0:T(8,128)(2,1)}, u32[]{:S(2)}) copy-start(bf16[1280,640]{1,0:T(8,128)(2,1)} %w_in.1) | copy-start | bytes 4915204
  0.6 0.9 copy-start.2
  4.7 35.6 %all-to-all-start = ((bf16[16,2,1280]{2,1,0:T(2,128)(2,1)}), bf16[16,2,1280]{2,1,0:T(2,128)(2,1)S(1)}, u32[]{:S(2)}, u32[]{:S(2)}) async-start(bf16[16,2,1280]{2,1,0:T(2,128)(2,1)} %reshape.20), calls=%async_computation | async-start | bytes 163840 | tf_op jit(solution)/shard_map/all_to_all | solution.py:200
  48.4 1.4 %copy-start.1 = (bf16[1280,640]{1,0:T(8,128)(2,1)S(1)}, bf16[1280,640]{1,0:T(8,128)(2,1)}, u32[]{:S(2)}) copy-start(bf16[1280,640]{1,0:T(8,128)(2,1)} %w_out.1) | copy-start | bytes 4915204
  52.4 10.5 %collective-permute-start = (bf16[64,1280]{1,0:T(8,128)(2,1)S(1)}, bf16[64,1280]{1,0:T(8,128)(2,1)S(1)}, u32[]{:S(2)}, u32[]{:S(2)}) collective-permute-start(bf16[64,1280]{1,0:T(8,128)(2,1)S(1)} %get-tuple-element.24), channel_id=1, source_target_pairs={{0,1},{1,0},{2,3},{3,2},{4,5},{5,4},{6,7},{7,6},{8,9},{9,8},{10,11... | collective-permute-start | bytes 491528 | tf_op jit(solution)/shard_map/ppermute | solution.py:210
  54.5 13.2 %collective-permute-start.1 = (bf16[192,640]{1,0:T(8,128)(2,1)S(1)}, bf16[192,640]{1,0:T(8,128)(2,1)S(1)}, u32[]{:S(2)}, u32[]{:S(2)}) collective-permute-start(bf16[192,640]{1,0:T(8,128)(2,1)S(1)} %get-tuple-element.30), channel_id=1, source_target_pairs={{0,192},{64,128},{128,64},{192,0},{1,193},{65,129},{129,65},{193,1... | collective-permute-start | bytes 737288 | tf_op jit(solution)/shard_map/ppermute | solution.py:213
  57.7 12.7 %collective-permute-start.2 = (bf16[192,640]{1,0:T(8,128)(2,1)S(1)}, bf16[192,640]{1,0:T(8,128)(2,1)S(1)}, u32[]{:S(2)}, u32[]{:S(2)}) collective-permute-start(bf16[192,640]{1,0:T(8,128)(2,1)S(1)} %get-tuple-element.31), channel_id=1, source_target_pairs={{0,64},{64,0},{128,192},{192,128},{1,65},{65,1},{129,193},{193,129... | collective-permute-start | bytes 737288 | tf_op jit(solution)/shard_map/ppermute | solution.py:213
  60.8 9.6 %collective-permute-start.3 = (bf16[192,640]{1,0:T(8,128)(2,1)S(1)}, bf16[192,640]{1,0:T(8,128)(2,1)S(1)}, u32[]{:S(2)}, u32[]{:S(2)}) collective-permute-start(bf16[192,640]{1,0:T(8,128)(2,1)S(1)} %get-tuple-element.32), channel_id=1, source_target_pairs={{0,128},{64,192},{128,0},{192,64},{1,129},{65,193},{129,1},{193,65... | collective-permute-start | bytes 737288 | tf_op jit(solution)/shard_map/ppermute | solution.py:213
  63.7 22.2 %all-to-all-start.1 = ((bf16[32,2,1280]{2,1,0:T(2,128)(2,1)}), bf16[32,2,1280]{2,1,0:T(2,128)(2,1)S(1)}, u32[]{:S(2)}, u32[]{:S(2)}) async-start(bf16[32,2,1280]{2,1,0:T(2,128)(2,1)} %reshape.22), calls=%async_computation.1 | async-start | bytes 327680 | tf_op jit(solution)/shard_map/all_to_all | solution.py:196
  70.4 15.6 %copy-start.3 = (bf16[1280,8]{0,1:T(8,128)(2,1)S(1)}, bf16[1280,8]{0,1:T(8,128)(2,1)}, u32[]{:S(2)}) copy-start(bf16[1280,8]{0,1:T(8,128)(2,1)} %param.7) | copy-start | bytes 61444
  71.0 18.5 %collective-permute-start.4 = (bf16[80,1280]{1,0:T(8,128)(2,1)S(1)}, bf16[80,1280]{1,0:T(8,128)(2,1)S(1)}, u32[]{:S(2)}, u32[]{:S(2)}) collective-permute-start(bf16[80,1280]{1,0:T(8,128)(2,1)S(1)} %get-tuple-element.34), channel_id=1, source_target_pairs={{0,512},{256,768},{512,0},{768,256},{1,513},{257,769},{513,1},{769... | collective-permute-start | bytes 614408 | tf_op jit(solution)/shard_map/ppermute | solution.py:225
  78.5 14.4 %collective-permute-start.5 = (bf16[80,1280]{1,0:T(8,128)(2,1)S(1)}, bf16[80,1280]{1,0:T(8,128)(2,1)S(1)}, u32[]{:S(2)}, u32[]{:S(2)}) collective-permute-start(bf16[80,1280]{1,0:T(8,128)(2,1)S(1)} %get-tuple-element.35), channel_id=1, source_target_pairs={{0,256},{256,512},{512,768},{768,0},{1,257},{257,513},{513,769},{7... | collective-permute-start | bytes 614408 | tf_op jit(solution)/shard_map/ppermute | solution.py:225
  80.9 17.0 %collective-permute-start.6 = (bf16[80,1280]{1,0:T(8,128)(2,1)S(1)}, bf16[80,1280]{1,0:T(8,128)(2,1)S(1)}, u32[]{:S(2)}, u32[]{:S(2)}) collective-permute-start(bf16[80,1280]{1,0:T(8,128)(2,1)S(1)} %get-tuple-element.36), channel_id=1, source_target_pairs={{0,768},{256,0},{512,256},{768,512},{1,769},{257,1},{513,257},{769... | collective-permute-start | bytes 614408 | tf_op jit(solution)/shard_map/ppermute | solution.py:225
